TPU v7x, 32 devices: a whole 2x2x4 slice. The times are simulated.
32 devices in a mesh: gx: 4 (over y, x), gy: 8 (over z, core).
Axes of the slice: x: 2, y: 2, z: 4, core: 2. Of those that a mesh axis runs over, the one named last changes fastest.
Arguments:
- plan: int32 [16], replicated, may hold values from 0 to 15, each once
- amplitude: float32 [4, 8, 16, 2, 128], P('gx', 'gy'), may hold values from -12 to 12
- positions: int32 [4, 8, 16, 128], P('gx', 'gy'), may hold values from 0 to 1023
- west_in: bfloat16 [4, 8, 2, 128, 1024], P('gx', 'gy'), may hold values from -6 to 6
- north_in: bfloat16 [4, 8, 2, 128, 1024], P('gx', 'gy'), may hold values from -6 to 6
- corner_now: bfloat16 [4, 8, 2, 128, 128], P('gx', 'gy'), may hold values from -6 to 6
- corner_next: bfloat16 [4, 8, 2, 128, 128], P('gx', 'gy'), may hold values from -6 to 6
- east_map: bfloat16 [4, 8, 2, 1024, 1024], P('gx', 'gy'), may hold values from -0.09375 to 0.09375
- south_map: bfloat16 [4, 8, 2, 1024, 1024], P('gx', 'gy'), may hold values from -0.09375 to 0.09375
Outputs:
- west_out: bfloat16 [4, 8, 2, 128, 1024], P('gx', 'gy')
- north_out: bfloat16 [4, 8, 2, 128, 1024], P('gx', 'gy')
- corner_first: bfloat16 [4, 8, 2, 128, 128], P('gx', 'gy')
- corner_second: bfloat16 [4, 8, 2, 128, 128], P('gx', 'gy')
- interface_residual: float32 [4, 8, 2, 128, 1024], P('gx', 'gy')
Inputs may be any that keep to these rules, and one draw needn't show every extreme that they name: `plan`: a permutation of the 16 batches.
All inputs are finite; a program needn't handle non-finite values.
Results may differ from a plain program's by a relative error of at most 0.015.
Values may be sent and summed in bfloat16 or wider, within the bound.
No kernel may reach another device: no remote copies, remote signals or barrier semaphores. Data moves between devices by JAX's collectives and lax.ppermute only.
A program may use at most 64 MiB of HBM per device.

v0:
```python
import jax
import jax.numpy as jnp
from jax import lax
from jax.sharding import PartitionSpec as P

TICKS = 6


def shifted(block, axis, distance):
    devices = range(lax.axis_size(axis))
    route = [(i - distance, i) for i in devices if i - distance in devices]
    return lax.ppermute(block, axis, route)


def padded_2(x, sides, width):
    for axis, dim in sides:
        size, length = (lax.axis_size(axis), x.shape[dim])
        up = [(i, (i + 1) % size) for i in range(size - 1)]
        down = [(j, i) for i, j in up]
        last = lax.slice_in_dim(x, length - width, length, axis=dim)
        leading = lax.slice_in_dim(x, 0, width, axis=dim)
        before = lax.ppermute(last, axis, up)
        after = lax.ppermute(leading, axis, down)
        x = jnp.concatenate([before, x, after], axis=dim)
    return x


def complex_apply(boundary, maps):
    real = jnp.dot(boundary[0], maps[0], preferred_element_type=jnp.float32) - jnp.dot(
        boundary[1], maps[1], preferred_element_type=jnp.float32
    )
    imag = jnp.dot(boundary[0], maps[1], preferred_element_type=jnp.float32) + jnp.dot(
        boundary[1], maps[0], preferred_element_type=jnp.float32
    )
    return jnp.stack([real, imag], 0).astype(jnp.bfloat16)


def on_device(
    plan, amplitude, positions, west_in, north_in, corner_now, corner_next, east_map, south_map
):
    column = lax.axis_index("gx")
    row = lax.axis_index("gy")
    span = lax.axis_size("gx") + lax.axis_size("gy") - 2
    west = west_in[0, 0]
    north = north_in[0, 0]
    corner_a = corner_now[0, 0]
    corner_b = corner_next[0, 0]
    east_local = east_map[0, 0]
    south_local = south_map[0, 0]
    cell_amps = amplitude[0, 0]
    cell_places = positions[0, 0]
    width = west.shape[-1]
    corner_width = corner_a.shape[-1]
    sources = west.shape[1]
    boundary = west
    for tick in range(TICKS):
        slot = tick - column - row + span
        batch = lax.dynamic_index_in_dim(plan, slot, 0, keepdims=False)
        amps = lax.dynamic_index_in_dim(cell_amps, batch, 0, keepdims=False)
        places = lax.dynamic_index_in_dim(cell_places, batch, 0, keepdims=False)
        points = lax.broadcasted_iota(jnp.int32, (sources, width), 1)
        onehot = (points == places[:, None]).astype(jnp.float32)
        total = (
            west.astype(jnp.float32) + north.astype(jnp.float32) + amps[:, :, None] * onehot[None]
        )
        total = total + jnp.pad(
            corner_a.astype(jnp.float32), ((0, 0), (0, 0), (0, width - corner_width))
        )
        boundary = total.astype(jnp.bfloat16)
        east_out = complex_apply(boundary, east_local)
        south_out = complex_apply(boundary, south_local)
        corner_out = east_out[..., :corner_width]
        west, passing = shifted((east_out, corner_out), "gx", 1)
        north, arrived = shifted((south_out, passing), "gy", 1)
        corner_a = corner_b
        corner_b = arrived
    padded = padded_2(boundary[None, None], (("gx", 0), ("gy", 1)), 1).astype(jnp.float32)
    residual = 4.0 * padded[1, 1] - padded[0, 1] - padded[2, 1] - padded[1, 0] - padded[1, 2]
    return (
        west[None, None],
        north[None, None],
        corner_a[None, None],
        corner_b[None, None],
        residual[None, None],
    )


def solution(mesh):
    return jax.shard_map(
        on_device,
        mesh=mesh,
        in_specs=(
            P(),
            P("gx", "gy", None, None, None),
            P("gx", "gy", None, None),
            P("gx", "gy", None, None, None),
            P("gx", "gy", None, None, None),
            P("gx", "gy", None, None, None),
            P("gx", "gy", None, None, None),
            P("gx", "gy", None, None, None),
            P("gx", "gy", None, None, None),
        ),
        out_specs=(
            P("gx", "gy", None, None, None),
            P("gx", "gy", None, None, None),
            P("gx", "gy", None, None, None),
            P("gx", "gy", None, None, None),
            P("gx", "gy", None, None, None),
        ),
        check_vma=False,
    )
```

profile of v0, /device:TPU:12, one launch (start us, length us, event | category | flops | bytes accessed | tf_op | source)
XLA Modules:
  0.0 212.1 jit_solution(12488450048254218171)
XLA Ops:
  17.1 2.1 fusion.70
  20.7 3.5 %collective-permute-start = (bf16[2,128,1024]{2,1,0:T(8,128)(2,1)S(1)}, bf16[2,128,1024]{2,1,0:T(8,128)(2,1)S(1)}, u32[]{:S(2)}, u32[]{:S(2)}) collective-permute-start(bf16[2,128,1024]{2,1,0:T(8,128)(2,1)S(1)} %pad_maximum_fusion.1), channel_id=1, source_target_pairs={{0,8},{8,16},{16,24},{1,9},{9,17},{17,25},{2,10},{10,18},{18,26},{... | collective-permute-start | bytes 1572872 | tf_op jit(solution)/shard_map/ppermute | solution.py:12
  26.2 1.9 collective-permute-start.1
  28.2 9.0 %collective-permute-done = bf16[2,128,1024]{2,1,0:T(8,128)(2,1)S(1)} collective-permute-done((bf16[2,128,1024]{2,1,0:T(8,128)(2,1)S(1)}, bf16[2,128,1024]{2,1,0:T(8,128)(2,1)S(1)}, u32[]{:S(2)}, u32[]{:S(2)}) %collective-permute-start) | collective-permute-done | bytes 524320 | tf_op jit(solution)/shard_map/ppermute | solution.py:12
  40.4 2.5 %collective-permute-start.2 = (bf16[2,128,1024]{2,1,0:T(8,128)(2,1)S(1)}, bf16[2,128,1024]{2,1,0:T(8,128)(2,1)S(1)}, u32[]{:S(2)}, u32[]{:S(2)}) collective-permute-start(bf16[2,128,1024]{2,1,0:T(8,128)(2,1)S(1)} %pad_maximum_fusion.2), channel_id=1, source_target_pairs={{0,8},{8,16},{16,24},{1,9},{9,17},{17,25},{2,10},{10,18},{18,26},{... | collective-permute-start | bytes 1572872 | tf_op jit(solution)/shard_map/ppermute | solution.py:12
  43.9 1.9 collective-permute-start.3
  45.8 1.9 collective-permute-start.4
  47.7 9.6 %collective-permute-done.4 = bf16[2,128,128]{2,1,0:T(8,128)(2,1)S(1)} collective-permute-done((bf16[2,128,128]{2,1,0:T(8,128)(2,1)S(1)}, bf16[2,128,128]{2,1,0:T(8,128)(2,1)S(1)}, u32[]{:S(2)}, u32[]{:S(2)}) %collective-permute-start.4) | collective-permute-done | bytes 65568 | tf_op jit(solution)/shard_map/ppermute | solution.py:12
  59.4 3.5 %collective-permute-done.5 = bf16[2,128,128]{2,1,0:T(8,128)(2,1)S(1)} collective-permute-done((bf16[2,128,128]{2,1,0:T(8,128)(2,1)S(1)}, bf16[2,128,128]{2,1,0:T(8,128)(2,1)S(1)}, u32[]{:S(2)}, u32[]{:S(2)}) %collective-permute-start.5) | collective-permute-done | bytes 65568 | tf_op jit(solution)/shard_map/ppermute | solution.py:12
  66.0 1.9 collective-permute-start.6
  69.0 1.9 collective-permute-start.7
  70.9 1.9 collective-permute-start.8
  72.9 10.5 %collective-permute-done.8 = bf16[2,128,128]{2,1,0:T(8,128)(2,1)S(1)} collective-permute-done((bf16[2,128,128]{2,1,0:T(8,128)(2,1)S(1)}, bf16[2,128,128]{2,1,0:T(8,128)(2,1)S(1)}, u32[]{:S(2)}, u32[]{:S(2)}) %collective-permute-start.8) | collective-permute-done | bytes 65568 | tf_op jit(solution)/shard_map/ppermute | solution.py:12
  83.4 2.1 collective-permute-start.9
  85.6 3.4 %collective-permute-done.9 = bf16[2,128,128]{2,1,0:T(8,128)(2,1)S(1)} collective-permute-done((bf16[2,128,128]{2,1,0:T(8,128)(2,1)S(1)}, bf16[2,128,128]{2,1,0:T(8,128)(2,1)S(1)}, u32[]{:S(2)}, u32[]{:S(2)}) %collective-permute-start.9) | collective-permute-done | bytes 65568 | tf_op jit(solution)/shard_map/ppermute | solution.py:12
  92.0 1.9 collective-permute-start.10
  96.9 1.9 collective-permute-start.12
  98.8 10.5 %collective-permute-done.12 = bf16[2,128,128]{2,1,0:T(8,128)(2,1)S(1)} collective-permute-done((bf16[2,128,128]{2,1,0:T(8,128)(2,1)S(1)}, bf16[2,128,128]{2,1,0:T(8,128)(2,1)S(1)}, u32[]{:S(2)}, u32[]{:S(2)}) %collective-permute-start.12) | collective-permute-done | bytes 65568 | tf_op jit(solution)/shard_map/ppermute | solution.py:12
  111.3 3.5 %collective-permute-done.13 = bf16[2,128,128]{2,1,0:T(8,128)(2,1)S(1)} collective-permute-done((bf16[2,128,128]{2,1,0:T(8,128)(2,1)S(1)}, bf16[2,128,128]{2,1,0:T(8,128)(2,1)S(1)}, u32[]{:S(2)}, u32[]{:S(2)}) %collective-permute-start.13) | collective-permute-done | bytes 65568 | tf_op jit(solution)/shard_map/ppermute | solution.py:12
  120.9 1.9 collective-permute-start.15
  124.8 8.8 %collective-permute-done.16 = bf16[2,128,128]{2,1,0:T(8,128)(2,1)S(1)} collective-permute-done((bf16[2,128,128]{2,1,0:T(8,128)(2,1)S(1)}, bf16[2,128,128]{2,1,0:T(8,128)(2,1)S(1)}, u32[]{:S(2)}, u32[]{:S(2)}) %collective-permute-start.16) | collective-permute-done | bytes 65568 | tf_op jit(solution)/shard_map/ppermute | solution.py:12
  135.6 3.5 %collective-permute-done.17 = bf16[2,128,128]{2,1,0:T(8,128)(2,1)S(1)} collective-permute-done((bf16[2,128,128]{2,1,0:T(8,128)(2,1)S(1)}, bf16[2,128,128]{2,1,0:T(8,128)(2,1)S(1)}, u32[]{:S(2)}, u32[]{:S(2)}) %collective-permute-start.17) | collective-permute-done | bytes 65568 | tf_op jit(solution)/shard_map/ppermute | solution.py:12
  139.4 1.9 collective-permute-start.24
  141.3 4.8 %collective-permute-start.25 = (bf16[1,1,2,128,1024]{4,3,2,1,0:T(8,128)(2,1)S(1)}, bf16[1,1,2,128,1024]{4,3,2,1,0:T(8,128)(2,1)S(1)}, u32[]{:S(2)}, u32[]{:S(2)}) collective-permute-start(bf16[1,1,2,128,1024]{4,3,2,1,0:T(8,128)(2,1)S(1)} %bitcast.408), channel_id=1, source_target_pairs={{8,0},{16,8},{24,16},{9,1},{17,9},{25,17},{10,2},{18,10},{26,18},{... | collective-permute-start | bytes 1572872 | tf_op jit(solution)/shard_map/ppermute | solution.py:23
  148.4 8.6 %collective-permute-done.24 = bf16[1,1,2,128,1024]{4,3,2,1,0:T(8,128)(2,1)S(1)} collective-permute-done((bf16[1,1,2,128,1024]{4,3,2,1,0:T(8,128)(2,1)S(1)}, bf16[1,1,2,128,1024]{4,3,2,1,0:T(8,128)(2,1)S(1)}, u32[]{:S(2)}, u32[]{:S(2)}) %collective-permute-start.24) | collective-permute-done | bytes 524320 | tf_op jit(solution)/shard_map/ppermute | solution.py:22
  157.0 4.7 %collective-permute-done.25 = bf16[1,1,2,128,1024]{4,3,2,1,0:T(8,128)(2,1)S(1)} collective-permute-done((bf16[1,1,2,128,1024]{4,3,2,1,0:T(8,128)(2,1)S(1)}, bf16[1,1,2,128,1024]{4,3,2,1,0:T(8,128)(2,1)S(1)}, u32[]{:S(2)}, u32[]{:S(2)}) %collective-permute-start.25) | collective-permute-done | bytes 524320 | tf_op jit(solution)/shard_map/ppermute | solution.py:23
  163.8 3.6 %collective-permute-start.27 = (bf16[3,1,2,128,1024]{4,3,2,1,0:T(8,128)(2,1)S(1)}, bf16[3,1,2,128,1024]{4,3,2,1,0:T(8,128)(2,1)S(1)}, u32[]{:S(2)}, u32[]{:S(2)}) collective-permute-start(bf16[3,1,2,128,1024]{4,3,2,1,0:T(8,128)(2,1)S(1)} %pad_maximum_fusion), channel_id=1, source_target_pairs={{1,0},{2,1},{3,2},{4,3},{5,4},{6,5},{7,6},{9,8},{10,9},{11,10},{12... | collective-permute-start | bytes 4718600 | tf_op jit(solution)/shard_map/ppermute | solution.py:23
  170.9 1.9 collective-permute-start.18
  174.8 14.8 %collective-permute-done.20 = bf16[2,128,128]{2,1,0:T(8,128)(2,1)S(1)} collective-permute-done((bf16[2,128,128]{2,1,0:T(8,128)(2,1)S(1)}, bf16[2,128,128]{2,1,0:T(8,128)(2,1)S(1)}, u32[]{:S(2)}, u32[]{:S(2)}) %collective-permute-start.20) | collective-permute-done | bytes 65568 | tf_op jit(solution)/shard_map/ppermute | solution.py:12
  191.5 3.6 %collective-permute-done.21 = bf16[2,128,128]{2,1,0:T(8,128)(2,1)S(1)} collective-permute-done((bf16[2,128,128]{2,1,0:T(8,128)(2,1)S(1)}, bf16[2,128,128]{2,1,0:T(8,128)(2,1)S(1)}, u32[]{:S(2)}, u32[]{:S(2)}) %collective-permute-start.21) | collective-permute-done | bytes 65568 | tf_op jit(solution)/shard_map/ppermute | solution.py:12
  197.1 5.1 %collective-permute-done.22 = bf16[2,128,128]{2,1,0:T(8,128)(2,1)S(1)} collective-permute-done((bf16[2,128,128]{2,1,0:T(8,128)(2,1)S(1)}, bf16[2,128,128]{2,1,0:T(8,128)(2,1)S(1)}, u32[]{:S(2)}, u32[]{:S(2)}) %collective-permute-start.22) | collective-permute-done | bytes 65568 | tf_op jit(solution)/shard_map/ppermute | solution.py:12
  204.1 3.7 %collective-permute-done.23 = bf16[2,128,128]{2,1,0:T(8,128)(2,1)S(1)} collective-permute-done((bf16[2,128,128]{2,1,0:T(8,128)(2,1)S(1)}, bf16[2,128,128]{2,1,0:T(8,128)(2,1)S(1)}, u32[]{:S(2)}, u32[]{:S(2)}) %collective-permute-start.23) | collective-permute-done | bytes 65568 | tf_op jit(solution)/shard_map/ppermute | solution.py:12
  (117 shorter events, 56.2 us)
Async XLA Ops:
  15.6 3.6 %copy-start.2 = (bf16[1,1,2,1024,1024]{4,3,2,1,0:T(8,128)(2,1)S(1)}, bf16[1,1,2,1024,1024]{4,3,2,1,0:T(8,128)(2,1)}, u32[]{:S(2)}) copy-start(bf16[1,1,2,1024,1024]{4,3,2,1,0:T(8,128)(2,1)} %param.16) | copy-start | bytes 12582916
  20.1 4.1 %copy-start.1 = (bf16[1,1,2,1024,1024]{4,3,2,1,0:T(8,128)(2,1)S(1)}, bf16[1,1,2,1024,1024]{4,3,2,1,0:T(8,128)(2,1)}, u32[]{:S(2)}) copy-start(bf16[1,1,2,1024,1024]{4,3,2,1,0:T(8,128)(2,1)} %param.17) | copy-start | bytes 12582916
  20.7 16.6 %collective-permute-start = (bf16[2,128,1024]{2,1,0:T(8,128)(2,1)S(1)}, bf16[2,128,1024]{2,1,0:T(8,128)(2,1)S(1)}, u32[]{:S(2)}, u32[]{:S(2)}) collective-permute-start(bf16[2,128,1024]{2,1,0:T(8,128)(2,1)S(1)} %pad_maximum_fusion.1), channel_id=1, source_target_pairs={{0,8},{8,16},{16,24},{1,9},{9,17},{17,25},{2,10},{10,18},{18,26},{... | collective-permute-start | bytes 1572872 | tf_op jit(solution)/shard_map/ppermute | solution.py:12
  25.7 11.6 %copy-start = (bf16[1,1,2,128,128]{4,3,2,1,0:T(8,128)(2,1)S(1)}, bf16[1,1,2,128,128]{4,3,2,1,0:T(8,128)(2,1)}, u32[]{:S(2)}) copy-start(bf16[1,1,2,128,128]{4,3,2,1,0:T(8,128)(2,1)} %param.15) | copy-start | bytes 196612
  26.2 11.1 %collective-permute-start.1 = (bf16[2,128,1024]{2,1,0:T(8,128)(2,1)S(1)}, bf16[2,128,1024]{2,1,0:T(8,128)(2,1)S(1)}, u32[]{:S(2)}, u32[]{:S(2)}) collective-permute-start(bf16[2,128,1024]{2,1,0:T(8,128)(2,1)S(1)} %pad_maximum_fusion.11), channel_id=1, source_target_pairs={{0,1},{1,2},{2,3},{3,4},{4,5},{5,6},{6,7},{8,9},{9,10},{10,11},{11... | collective-permute-start | bytes 1572872 | tf_op jit(solution)/shard_map/ppermute | solution.py:12
  40.4 22.6 %collective-permute-start.2 = (bf16[2,128,1024]{2,1,0:T(8,128)(2,1)S(1)}, bf16[2,128,1024]{2,1,0:T(8,128)(2,1)S(1)}, u32[]{:S(2)}, u32[]{:S(2)}) collective-permute-start(bf16[2,128,1024]{2,1,0:T(8,128)(2,1)S(1)} %pad_maximum_fusion.2), channel_id=1, source_target_pairs={{0,8},{8,16},{16,24},{1,9},{9,17},{17,25},{2,10},{10,18},{18,26},{... | collective-permute-start | bytes 1572872 | tf_op jit(solution)/shard_map/ppermute | solution.py:12
  43.9 19.1 %collective-permute-start.3 = (bf16[2,128,1024]{2,1,0:T(8,128)(2,1)S(1)}, bf16[2,128,1024]{2,1,0:T(8,128)(2,1)S(1)}, u32[]{:S(2)}, u32[]{:S(2)}) collective-permute-start(bf16[2,128,1024]{2,1,0:T(8,128)(2,1)S(1)} %pad_maximum_fusion.12), channel_id=1, source_target_pairs={{0,1},{1,2},{2,3},{3,4},{4,5},{5,6},{6,7},{8,9},{9,10},{10,11},{11... | collective-permute-start | bytes 1572872 | tf_op jit(solution)/shard_map/ppermute | solution.py:12
  45.8 11.5 %collective-permute-start.4 = (bf16[2,128,128]{2,1,0:T(8,128)(2,1)S(1)}, bf16[2,128,128]{2,1,0:T(8,128)(2,1)S(1)}, u32[]{:S(2)}, u32[]{:S(2)}) collective-permute-start(bf16[2,128,128]{2,1,0:T(8,128)(2,1)S(1)} %fusion.326), channel_id=1, source_target_pairs={{0,8},{8,16},{16,24},{1,9},{9,17},{17,25},{2,10},{10,18},{18,26},{... | collective-permute-start | bytes 196616 | tf_op jit(solution)/shard_map/ppermute | solution.py:12
  57.4 5.6 %collective-permute-start.5 = (bf16[2,128,128]{2,1,0:T(8,128)(2,1)S(1)}, bf16[2,128,128]{2,1,0:T(8,128)(2,1)S(1)}, u32[]{:S(2)}, u32[]{:S(2)}) collective-permute-start(bf16[2,128,128]{2,1,0:T(8,128)(2,1)S(1)} %collective-permute-done.4), channel_id=1, source_target_pairs={{0,1},{1,2},{2,3},{3,4},{4,5},{5,6},{6,7},{8,9},{9,10},{10,11},{11... | collective-permute-start | bytes 196616 | tf_op jit(solution)/shard_map/ppermute | solution.py:12
  66.0 22.9 %collective-permute-start.6 = (bf16[2,128,1024]{2,1,0:T(8,128)(2,1)S(1)}, bf16[2,128,1024]{2,1,0:T(8,128)(2,1)S(1)}, u32[]{:S(2)}, u32[]{:S(2)}) collective-permute-start(bf16[2,128,1024]{2,1,0:T(8,128)(2,1)S(1)} %pad_maximum_fusion.3), channel_id=1, source_target_pairs={{0,8},{8,16},{16,24},{1,9},{9,17},{17,25},{2,10},{10,18},{18,26},{... | collective-permute-start | bytes 1572872 | tf_op jit(solution)/shard_map/ppermute | solution.py:12
  69.0 20.0 %collective-permute-start.7 = (bf16[2,128,1024]{2,1,0:T(8,128)(2,1)S(1)}, bf16[2,128,1024]{2,1,0:T(8,128)(2,1)S(1)}, u32[]{:S(2)}, u32[]{:S(2)}) collective-permute-start(bf16[2,128,1024]{2,1,0:T(8,128)(2,1)S(1)} %pad_maximum_fusion.13), channel_id=1, source_target_pairs={{0,1},{1,2},{2,3},{3,4},{4,5},{5,6},{6,7},{8,9},{9,10},{10,11},{11... | collective-permute-start | bytes 1572872 | tf_op jit(solution)/shard_map/ppermute | solution.py:12
  70.9 12.4 %collective-permute-start.8 = (bf16[2,128,128]{2,1,0:T(8,128)(2,1)S(1)}, bf16[2,128,128]{2,1,0:T(8,128)(2,1)S(1)}, u32[]{:S(2)}, u32[]{:S(2)}) collective-permute-start(bf16[2,128,128]{2,1,0:T(8,128)(2,1)S(1)} %fusion.325), channel_id=1, source_target_pairs={{0,8},{8,16},{16,24},{1,9},{9,17},{17,25},{2,10},{10,18},{18,26},{... | collective-permute-start | bytes 196616 | tf_op jit(solution)/shard_map/ppermute | solution.py:12
  83.4 5.6 %collective-permute-start.9 = (bf16[2,128,128]{2,1,0:T(8,128)(2,1)S(1)}, bf16[2,128,128]{2,1,0:T(8,128)(2,1)S(1)}, u32[]{:S(2)}, u32[]{:S(2)}) collective-permute-start(bf16[2,128,128]{2,1,0:T(8,128)(2,1)S(1)} %collective-permute-done.8), channel_id=1, source_target_pairs={{0,1},{1,2},{2,3},{3,4},{4,5},{5,6},{6,7},{8,9},{9,10},{10,11},{11... | collective-permute-start | bytes 196616 | tf_op jit(solution)/shard_map/ppermute | solution.py:12
  92.0 22.9 %collective-permute-start.10 = (bf16[2,128,1024]{2,1,0:T(8,128)(2,1)S(1)}, bf16[2,128,1024]{2,1,0:T(8,128)(2,1)S(1)}, u32[]{:S(2)}, u32[]{:S(2)}) collective-permute-start(bf16[2,128,1024]{2,1,0:T(8,128)(2,1)S(1)} %pad_maximum_fusion.4), channel_id=1, source_target_pairs={{0,8},{8,16},{16,24},{1,9},{9,17},{17,25},{2,10},{10,18},{18,26},{... | collective-permute-start | bytes 1572872 | tf_op jit(solution)/shard_map/ppermute | solution.py:12
  95.0 20.0 %collective-permute-start.11 = (bf16[2,128,1024]{2,1,0:T(8,128)(2,1)S(1)}, bf16[2,128,1024]{2,1,0:T(8,128)(2,1)S(1)}, u32[]{:S(2)}, u32[]{:S(2)}) collective-permute-start(bf16[2,128,1024]{2,1,0:T(8,128)(2,1)S(1)} %pad_maximum_fusion.14), channel_id=1, source_target_pairs={{0,1},{1,2},{2,3},{3,4},{4,5},{5,6},{6,7},{8,9},{9,10},{10,11},{11... | collective-permute-start | bytes 1572872 | tf_op jit(solution)/shard_map/ppermute | solution.py:12
  96.9 12.4 %collective-permute-start.12 = (bf16[2,128,128]{2,1,0:T(8,128)(2,1)S(1)}, bf16[2,128,128]{2,1,0:T(8,128)(2,1)S(1)}, u32[]{:S(2)}, u32[]{:S(2)}) collective-permute-start(bf16[2,128,128]{2,1,0:T(8,128)(2,1)S(1)} %fusion.324), channel_id=1, source_target_pairs={{0,8},{8,16},{16,24},{1,9},{9,17},{17,25},{2,10},{10,18},{18,26},{... | collective-permute-start | bytes 196616 | tf_op jit(solution)/shard_map/ppermute | solution.py:12
  109.3 5.6 %collective-permute-start.13 = (bf16[2,128,128]{2,1,0:T(8,128)(2,1)S(1)}, bf16[2,128,128]{2,1,0:T(8,128)(2,1)S(1)}, u32[]{:S(2)}, u32[]{:S(2)}) collective-permute-start(bf16[2,128,128]{2,1,0:T(8,128)(2,1)S(1)} %collective-permute-done.12), channel_id=1, source_target_pairs={{0,1},{1,2},{2,3},{3,4},{4,5},{5,6},{6,7},{8,9},{9,10},{10,11},{11... | collective-permute-start | bytes 196616 | tf_op jit(solution)/shard_map/ppermute | solution.py:12
  118.0 21.2 %collective-permute-start.14 = (bf16[2,128,1024]{2,1,0:T(8,128)(2,1)S(1)}, bf16[2,128,1024]{2,1,0:T(8,128)(2,1)S(1)}, u32[]{:S(2)}, u32[]{:S(2)}) collective-permute-start(bf16[2,128,1024]{2,1,0:T(8,128)(2,1)S(1)} %pad_maximum_fusion.5), channel_id=1, source_target_pairs={{0,8},{8,16},{16,24},{1,9},{9,17},{17,25},{2,10},{10,18},{18,26},{... | collective-permute-start | bytes 1572872 | tf_op jit(solution)/shard_map/ppermute | solution.py:12
  120.9 18.2 %collective-permute-start.15 = (bf16[2,128,1024]{2,1,0:T(8,128)(2,1)S(1)}, bf16[2,128,1024]{2,1,0:T(8,128)(2,1)S(1)}, u32[]{:S(2)}, u32[]{:S(2)}) collective-permute-start(bf16[2,128,1024]{2,1,0:T(8,128)(2,1)S(1)} %pad_maximum_fusion.15), channel_id=1, source_target_pairs={{0,1},{1,2},{2,3},{3,4},{4,5},{5,6},{6,7},{8,9},{9,10},{10,11},{11... | collective-permute-start | bytes 1572872 | tf_op jit(solution)/shard_map/ppermute | solution.py:12
  122.9 10.7 %collective-permute-start.16 = (bf16[2,128,128]{2,1,0:T(8,128)(2,1)S(1)}, bf16[2,128,128]{2,1,0:T(8,128)(2,1)S(1)}, u32[]{:S(2)}, u32[]{:S(2)}) collective-permute-start(bf16[2,128,128]{2,1,0:T(8,128)(2,1)S(1)} %fusion.323), channel_id=1, source_target_pairs={{0,8},{8,16},{16,24},{1,9},{9,17},{17,25},{2,10},{10,18},{18,26},{... | collective-permute-start | bytes 196616 | tf_op jit(solution)/shard_map/ppermute | solution.py:12
  133.6 5.6 %collective-permute-start.17 = (bf16[2,128,128]{2,1,0:T(8,128)(2,1)S(1)}, bf16[2,128,128]{2,1,0:T(8,128)(2,1)S(1)}, u32[]{:S(2)}, u32[]{:S(2)}) collective-permute-start(bf16[2,128,128]{2,1,0:T(8,128)(2,1)S(1)} %collective-permute-done.16), channel_id=1, source_target_pairs={{0,1},{1,2},{2,3},{3,4},{4,5},{5,6},{6,7},{8,9},{9,10},{10,11},{11... | collective-permute-start | bytes 196616 | tf_op jit(solution)/shard_map/ppermute | solution.py:12
  139.4 17.7 %collective-permute-start.24 = (bf16[1,1,2,128,1024]{4,3,2,1,0:T(8,128)(2,1)S(1)}, bf16[1,1,2,128,1024]{4,3,2,1,0:T(8,128)(2,1)S(1)}, u32[]{:S(2)}, u32[]{:S(2)}) collective-permute-start(bf16[1,1,2,128,1024]{4,3,2,1,0:T(8,128)(2,1)S(1)} %bitcast.407), channel_id=1, source_target_pairs={{0,8},{8,16},{16,24},{1,9},{9,17},{17,25},{2,10},{10,18},{18,26},{... | collective-permute-start | bytes 1572872 | tf_op jit(solution)/shard_map/ppermute | solution.py:22
  141.3 20.4 %collective-permute-start.25 = (bf16[1,1,2,128,1024]{4,3,2,1,0:T(8,128)(2,1)S(1)}, bf16[1,1,2,128,1024]{4,3,2,1,0:T(8,128)(2,1)S(1)}, u32[]{:S(2)}, u32[]{:S(2)}) collective-permute-start(bf16[1,1,2,128,1024]{4,3,2,1,0:T(8,128)(2,1)S(1)} %bitcast.408), channel_id=1, source_target_pairs={{8,0},{16,8},{24,16},{9,1},{17,9},{25,17},{10,2},{18,10},{26,18},{... | collective-permute-start | bytes 1572872 | tf_op jit(solution)/shard_map/ppermute | solution.py:23
  161.9 45.9 %collective-permute-start.26 = (bf16[3,1,2,128,1024]{4,3,2,1,0:T(8,128)(2,1)S(1)}, bf16[3,1,2,128,1024]{4,3,2,1,0:T(8,128)(2,1)S(1)}, u32[]{:S(2)}, u32[]{:S(2)}) collective-permute-start(bf16[3,1,2,128,1024]{4,3,2,1,0:T(8,128)(2,1)S(1)} %pad_maximum_fusion), channel_id=1, source_target_pairs={{0,1},{1,2},{2,3},{3,4},{4,5},{5,6},{6,7},{8,9},{9,10},{10,11},{11... | collective-permute-start | bytes 4718600 | tf_op jit(solution)/shard_map/ppermute | solution.py:22
  163.8 44.0 %collective-permute-start.27 = (bf16[3,1,2,128,1024]{4,3,2,1,0:T(8,128)(2,1)S(1)}, bf16[3,1,2,128,1024]{4,3,2,1,0:T(8,128)(2,1)S(1)}, u32[]{:S(2)}, u32[]{:S(2)}) collective-permute-start(bf16[3,1,2,128,1024]{4,3,2,1,0:T(8,128)(2,1)S(1)} %pad_maximum_fusion), channel_id=1, source_target_pairs={{1,0},{2,1},{3,2},{4,3},{5,4},{6,5},{7,6},{9,8},{10,9},{11,10},{12... | collective-permute-start | bytes 4718600 | tf_op jit(solution)/shard_map/ppermute | solution.py:23
  167.6 40.2 %collective-permute-start.19 = (bf16[2,128,1024]{2,1,0:T(8,128)(2,1)S(1)}, bf16[2,128,1024]{2,1,0:T(8,128)(2,1)S(1)}, u32[]{:S(2)}, u32[]{:S(2)}) collective-permute-start(bf16[2,128,1024]{2,1,0:T(8,128)(2,1)S(1)} %pad_maximum_fusion.16), channel_id=1, source_target_pairs={{0,1},{1,2},{2,3},{3,4},{4,5},{5,6},{6,7},{8,9},{9,10},{10,11},{11... | collective-permute-start | bytes 1572872 | tf_op jit(solution)/shard_map/ppermute | solution.py:12
  170.9 36.9 %collective-permute-start.18 = (bf16[2,128,1024]{2,1,0:T(8,128)(2,1)S(1)}, bf16[2,128,1024]{2,1,0:T(8,128)(2,1)S(1)}, u32[]{:S(2)}, u32[]{:S(2)}) collective-permute-start(bf16[2,128,1024]{2,1,0:T(8,128)(2,1)S(1)} %pad_maximum_fusion.6), channel_id=1, source_target_pairs={{0,8},{8,16},{16,24},{1,9},{9,17},{17,25},{2,10},{10,18},{18,26},{... | collective-permute-start | bytes 1572872 | tf_op jit(solution)/shard_map/ppermute | solution.py:12
  172.9 16.7 %collective-permute-start.20 = (bf16[2,128,128]{2,1,0:T(8,128)(2,1)S(1)}, bf16[2,128,128]{2,1,0:T(8,128)(2,1)S(1)}, u32[]{:S(2)}, u32[]{:S(2)}) collective-permute-start(bf16[2,128,128]{2,1,0:T(8,128)(2,1)S(1)} %fusion.322), channel_id=1, source_target_pairs={{0,8},{8,16},{16,24},{1,9},{9,17},{17,25},{2,10},{10,18},{18,26},{... | collective-permute-start | bytes 196616 | tf_op jit(solution)/shard_map/ppermute | solution.py:12
  189.6 5.6 %collective-permute-start.21 = (bf16[2,128,128]{2,1,0:T(8,128)(2,1)S(1)}, bf16[2,128,128]{2,1,0:T(8,128)(2,1)S(1)}, u32[]{:S(2)}, u32[]{:S(2)}) collective-permute-start(bf16[2,128,128]{2,1,0:T(8,128)(2,1)S(1)} %collective-permute-done.20), channel_id=1, source_target_pairs={{0,1},{1,2},{2,3},{3,4},{4,5},{5,6},{6,7},{8,9},{9,10},{10,11},{11... | collective-permute-start | bytes 196616 | tf_op jit(solution)/shard_map/ppermute | solution.py:12
  195.2 7.0 %collective-permute-start.22 = (bf16[2,128,128]{2,1,0:T(8,128)(2,1)S(1)}, bf16[2,128,128]{2,1,0:T(8,128)(2,1)S(1)}, u32[]{:S(2)}, u32[]{:S(2)}) collective-permute-start(bf16[2,128,128]{2,1,0:T(8,128)(2,1)S(1)} %fusion.321), channel_id=1, source_target_pairs={{0,8},{8,16},{16,24},{1,9},{9,17},{17,25},{2,10},{10,18},{18,26},{... | collective-permute-start | bytes 196616 | tf_op jit(solution)/shard_map/ppermute | solution.py:12
  202.2 5.6 %collective-permute-start.23 = (bf16[2,128,128]{2,1,0:T(8,128)(2,1)S(1)}, bf16[2,128,128]{2,1,0:T(8,128)(2,1)S(1)}, u32[]{:S(2)}, u32[]{:S(2)}) collective-permute-start(bf16[2,128,128]{2,1,0:T(8,128)(2,1)S(1)} %collective-permute-done.22), channel_id=1, source_target_pairs={{0,1},{1,2},{2,3},{3,4},{4,5},{5,6},{6,7},{8,9},{9,10},{10,11},{11... | collective-permute-start | bytes 196616 | tf_op jit(solution)/shard_map/ppermute | solution.py:12
where the time goes:
time: 213 us; the launch traced here: 212 us
  waiting for transfers between devices  103 us (48%)
  starting transfers between devices  60.7 us (28%)
  matrix products  23.7 us (11%)
  between operations  13.1 us (6%)
  local copies, waits for them, and re-layouts  6.06 us (3%)
  other arithmetic  5.58 us (3%)
    ppermute x24, waiting for transfers between devices, shifted(): return lax.ppermute(block, axis, route)  89.7 us
    ppermute x24, starting transfers between devices, shifted(): return lax.ppermute(block, axis, route)  48.4 us
    ppermute x2, waiting for transfers between devices, padded_2(): before = lax.ppermute(last, axis, up)  8.61 us
    ppermute x2, starting transfers between devices, padded_2(): after = lax.ppermute(leading, axis, down)  8.46 us
    dot_general x12, matrix products, complex_apply(): jnp.dot(boundary[1], maps[1], preferred_element_type=jnp.float32)  7.05 us
    dot_general x12, matrix products, complex_apply(): jnp.dot(boundary[0], maps[0], preferred_element_type=jnp.float32)  5.58 us
    dot_general x12, matrix products, complex_apply(): jnp.dot(boundary[1], maps[0], preferred_element_type=jnp.float32)  5.58 us
    dot_general x12, matrix products, complex_apply(): jnp.dot(boundary[0], maps[1], preferred_element_type=jnp.float32)  5.44 us
  transfers between devices with their start and end apart: 28, of which 15 were waited for; matrix products, arithmetic and copies ran while one was open for 5% of the time, Pallas kernels for 0%

commit v1 on v0

v1 whole, which is shorter than its diff:
```python
import functools

import jax
import jax.numpy as jnp
from jax import lax
from jax.experimental import pallas as pl
from jax.experimental.pallas import tpu as pltpu
from jax.sharding import PartitionSpec as P

TICKS = 6
PARTS = 2
FIELDS = 3
PIECES = 8
VMEM = pl.BlockSpec(memory_space=pltpu.VMEM)
ANY = pl.BlockSpec(memory_space=pl.ANY)
HBM = pl.BlockSpec(memory_space=pltpu.HBM)


COSTS = dict.fromkeys(
    ("east", "south", "last_east0", "last_east1", "middle0", "middle1"), 10**10
)


def kernel_call(name, body, outs, in_specs, out_specs, scratch=()):
    return pl.pallas_call(
        body,
        name=name,
        out_shape=outs,
        in_specs=in_specs,
        out_specs=out_specs,
        scratch_shapes=list(scratch),
        compiler_params=pltpu.CompilerParams(vmem_limit_bytes=24 << 20),
        cost_estimate=pl.CostEstimate(flops=COSTS.get(name, 1000), bytes_accessed=1000, transcendentals=0),
    )


def ring(x, axis, distance):
    size = lax.axis_size(axis)
    return lax.ppermute(x, axis, [(i, (i + distance) % size) for i in range(size)])


def line(x, axis, distance):
    size = lax.axis_size(axis)
    return lax.ppermute(
        x, axis, [(i, i + distance) for i in range(size) if 0 <= i + distance < size]
    )


def inside(axis, towards_end=False):
    here = lax.axis_index(axis)
    there = here < lax.axis_size(axis) - 1 if towards_end else here > 0
    return there.astype(jnp.float32)


def f32(x):
    return x.astype(jnp.float32)


def sources_of(info, tick, rows):
    base = tick * FIELDS
    point = info[rows, base + 2 : base + 3].astype(jnp.int32)

    def spread(part, width):
        points = lax.broadcasted_iota(jnp.int32, (point.shape[0], width), 1)
        return jnp.where(points == point, info[rows, base + part : base + part + 1], 0.0)

    return spread


def stacked(q):
    return jnp.concatenate([q[0], q[1]], 0), jnp.concatenate([-q[1], q[0]], 0)


def product(q, maps):
    ahead, turned = stacked(q)
    out = jnp.dot(ahead, maps[0], preferred_element_type=jnp.float32)
    return out + jnp.dot(turned, maps[1], preferred_element_type=jnp.float32)


def map_copies(source, held, sems):
    depth = held.shape[1] * 2 // PIECES
    copies = []
    for k in range(PIECES):
        half, place = k * 2 // PIECES, pl.ds(k % (PIECES // 2) * depth, depth)
        copies.append(
            pltpu.make_async_copy(source.at[0, 0, half, place], held.at[half, place], sems.at[k])
        )
    return copies


def arriving_product(q, held, copies):
    depth = held.shape[1] * 2 // PIECES
    sides = stacked(q)
    out = None
    for k, copy in enumerate(copies):
        copy.wait()
        half, place = k * 2 // PIECES, k % (PIECES // 2) * depth
        term = jnp.dot(
            sides[half][:, place : place + depth],
            held[half, place : place + depth, :],
            preferred_element_type=jnp.float32,
        )
        out = term if out is None else out + term
    return out


def first_body(
    plan, amplitude, positions, west, north, corner, east_map,
    q0, q1, east, held, info, order, amps, places, w, n, c, table, list_sems, in_sems, map_sems,
):
    step, width = q0.shape[1:]
    corner_width = c.shape[-1]
    lists = [
        pltpu.make_async_copy(plan, order, list_sems.at[0]),
        pltpu.make_async_copy(amplitude.at[0, 0], amps, list_sems.at[1]),
        pltpu.make_async_copy(positions.at[0, 0], places, list_sems.at[2]),
    ]
    traces = []
    for p in range(PARTS):
        cut = pl.ds(p * step, step)
        traces.append(
            [
                pltpu.make_async_copy(west.at[0, 0, :, cut], w.at[:, cut], in_sems.at[p, 0]),
                pltpu.make_async_copy(north.at[0, 0, :, cut], n.at[:, cut], in_sems.at[p, 1]),
                pltpu.make_async_copy(corner.at[0, 0, :, cut], c.at[:, cut], in_sems.at[p, 2]),
            ]
        )
    pieces = map_copies(east_map, held, map_sems)
    for copy in lists + traces[0] + pieces + traces[1]:
        copy.start()
    span = lax.axis_size("gx") + lax.axis_size("gy") - 2
    start = span - lax.axis_index("gx") - lax.axis_index("gy")
    table[...] = jnp.zeros_like(table)
    for copy in lists:
        copy.wait()
    for tick in range(TICKS):
        batch = order[start + tick]
        base = tick * FIELDS
        table[base : base + 2, :] = amps[batch]
        table[base + 2 : base + 3, :] = places[pl.ds(batch, 1), :].astype(jnp.float32)
    info[...] = table[...].T
    for p, q in enumerate((q0, q1)):
        cut = slice(p * step, (p + 1) * step)
        for copy in traces[p]:
            copy.wait()
        spread = sources_of(info, 0, cut)
        for part in range(2):
            total = f32(w[part, cut]) + f32(n[part, cut]) + spread(part, width)
            q[part] = total.astype(q.dtype)
            head = total[:, :corner_width] + f32(c[part, cut])
            q[part, :, :corner_width] = head.astype(q.dtype)
    out = arriving_product(q0[...], held, pieces)
    east[0] = out[:step].astype(east.dtype)
    east[1] = out[step:].astype(east.dtype)


def first_south_body(q, south_map, out, held, map_sems):
    step = q.shape[1]
    pieces = map_copies(south_map, held, map_sems)
    for copy in pieces:
        copy.start()
    total = arriving_product(q[...], held, pieces)
    out[0] = total[:step].astype(out.dtype)
    out[1] = total[step:].astype(out.dtype)


def product_body(q, maps, turn, out):
    step = q.shape[1]
    total = product(q[...], maps)
    out[0] = total[:step].astype(out.dtype)
    out[1] = total[step:].astype(out.dtype)


def east_body(tick, part, w, n, info, maps, corner, turn, q, out):
    step, width = q.shape[1:]
    rows = slice(part * step, (part + 1) * step)
    from_west, from_north = inside("gx"), inside("gy")
    spread = sources_of(info, tick, rows)
    for half in range(2):
        total = f32(w[half]) * from_west + f32(n[half]) * from_north + spread(half, width)
        q[half] = total.astype(q.dtype)
        if corner is not None:
            corner_width = corner.shape[-1]
            head = total[:, :corner_width] + f32(corner[0, 0, half, rows])
            q[half, :, :corner_width] = head.astype(q.dtype)
    total = product(q[...], maps)
    out[0] = total[:step].astype(out.dtype)
    out[1] = total[step:].astype(out.dtype)


def east_plain_body(tick, part, w, n, info, maps, turn, q, out):
    east_body(tick, part, w, n, info, maps, None, turn, q, out)


def south_body(corner_width, q, maps, w, turn, out):
    step = q.shape[1]
    from_west = inside("gx")
    total = product(q[...], maps)
    for half in range(2):
        trace = total[half * step : (half + 1) * step]
        out[half] = trace.astype(out.dtype)
        head = trace[:, :corner_width] + f32(w[half, :, :corner_width]) * from_west
        out[half, :, :corner_width] = head.astype(out.dtype)


def last_south_body(q0, q1, maps, w0, w1, turn, tray):
    step, width = q0.shape[1:]
    from_west = inside("gx")
    for p, (q, w) in enumerate(((q0, w0), (q1, w1))):
        rows = slice(p * step, (p + 1) * step)
        tray[:, rows, width : 2 * width] = q[...]
        corner = f32(w[:, :, : tray.shape[2] - 2 * width]) * from_west
        tray[:, rows, 2 * width :] = corner.astype(tray.dtype)
    total = product(tray[:, :, width : 2 * width], maps)
    for half in range(2):
        trace = total[half * 2 * step : (half + 1) * 2 * step]
        tray[half, :, :width] = trace.astype(tray.dtype)


def first_middle_body(q0, q1, far, west, turn, total, both):
    total[...] = (f32(q0[...]) + f32(far[...])).astype(total.dtype)
    both[:, : q0.shape[1]] = q0[...]
    both[:, q0.shape[1] :] = q1[...]


def middle_body(a, b, w0, w1, turn, total, out, head, whole, sem):
    from_west = inside("gx")
    step = w0.shape[1]
    for p, w in enumerate((w0, w1)):
        whole[:, p * step : (p + 1) * step] = (f32(w[...]) * from_west).astype(whole.dtype)
    copy = pltpu.make_async_copy(whole, out.at[0, 0], sem)
    copy.start()
    head[...] = whole[:, :, : head.shape[-1]]
    total[...] = (f32(a[...]) + f32(b[...])).astype(total.dtype)
    copy.wait()


def base_body(q, tray, down, side, turn, base, first, out, trace, corner, sems):
    width = base.shape[-1]
    from_north, from_south = inside("gy"), inside("gy", True)
    trace[...] = (f32(tray[:, :, :width]) * from_north).astype(trace.dtype)
    corner[...] = (f32(tray[:, :, 2 * width :]) * from_north).astype(corner.dtype)
    copies = [
        pltpu.make_async_copy(trace, out.at[0, 0], sems.at[0]),
        pltpu.make_async_copy(corner, first.at[0, 0], sems.at[1]),
    ]
    for copy in copies:
        copy.start()
    rows = slice(0, side.shape[1])
    for half in range(2):
        base[half] = (
            4.0 * f32(q[half])
            - f32(tray[half, :, width : 2 * width]) * from_north
            - f32(down[half]) * from_south
        )
        base[half, rows] = base[half, rows] - f32(side[half])
    for copy in copies:
        copy.wait()


def final_body(base, side, second, out, corner, rest, held, sems, part_sems):
    held[...] = (f32(second[...]) * inside("gy")).astype(held.dtype)
    step = side.shape[1]
    done, left = pl.ds(0, step), pl.ds(step, step)
    copies = [
        pltpu.make_async_copy(held, corner.at[0, 0], sems.at[0]),
        pltpu.make_async_copy(base.at[:, done], out.at[0, 0, :, done], sems.at[1]),
    ]
    for copy in copies:
        copy.start()
    for half in range(2):
        rest[half] = base[half, step:] - f32(side[half])
        copy = pltpu.make_async_copy(
            rest.at[half], out.at[0, 0, half, left], part_sems.at[half]
        )
        copy.start()
        copies.append(copy)
    for copy in copies:
        copy.wait()


def on_device(
    plan, amplitude, positions, west_in, north_in, corner_now, corner_next, east_map, south_map
):
    columns = lax.axis_size("gx")
    kind = west_in.dtype
    sources, width = west_in.shape[-2:]
    corner_width = corner_now.shape[-1]
    step = sources // PARTS
    part = jax.ShapeDtypeStruct((2, step, width), kind)
    whole = jax.ShapeDtypeStruct((2, sources, width), kind)
    head = jax.ShapeDtypeStruct((2, sources, corner_width), kind)
    maps = jax.ShapeDtypeStruct((2, width, width), kind)
    info = jax.ShapeDtypeStruct((sources, sources), jnp.float32)
    dma = pltpu.SemaphoreType.DMA

    fixed = [
        pltpu.with_memory_space_constraint(x, pltpu.HBM)
        for x in (plan, amplitude, positions, west_in, north_in, corner_now, east_map, south_map)
    ]
    q0, q1, east, east_held, info = kernel_call(
        "first",
        first_body,
        (part, part, part, maps, info),
        [HBM] * 7,
        [VMEM] * 5,
        [
            pltpu.SMEM(plan.shape, plan.dtype),
            pltpu.VMEM(amplitude.shape[2:], amplitude.dtype),
            pltpu.VMEM(positions.shape[2:], positions.dtype),
            pltpu.VMEM((2, sources, width), kind),
            pltpu.VMEM((2, sources, width), kind),
            pltpu.VMEM((2, sources, corner_width), kind),
            pltpu.VMEM((sources, sources), jnp.float32),
            dma((3,)),
            dma((PARTS, 3)),
            dma((PIECES,)),
        ],
    )(*fixed[:-1])
    w0 = ring(east, "gx", 1)
    south, south_held = kernel_call(
        "first_south", first_south_body, (part, maps), [VMEM, HBM], [VMEM] * 2, [dma((PIECES,))]
    )(q0, fixed[-1])
    n0 = ring(south, "gy", 1)
    east = kernel_call("east", product_body, part, [VMEM, VMEM, ANY], VMEM)(q1, east_held, south)
    w1 = ring(east, "gx", 1)
    south = kernel_call("south", product_body, part, [VMEM, VMEM, ANY], VMEM)(q1, south_held, east)
    n1 = ring(south, "gy", 1)
    west, north = [w0, w1], [n0, n1]
    for tick in range(1, TICKS - 1):
        for p in range(PARTS):
            w, n = west[p], north[p]
            if tick == 1:
                q, east = kernel_call(
                    "east", functools.partial(east_body, tick, p), (part, part), [VMEM] * 5 + [ANY], [VMEM] * 2
                )(w, n, info, east_held, corner_next, south)
            else:
                q, east = kernel_call(
                    "east", functools.partial(east_plain_body, tick, p), (part, part), [VMEM] * 4 + [ANY], [VMEM] * 2
                )(w, n, info, east_held, south)
            west[p] = ring(east, "gx", 1)
            south = kernel_call(
                "south", functools.partial(south_body, corner_width), part, [VMEM] * 3 + [ANY], VMEM
            )(q, south_held, w, east)
            north[p] = ring(south, "gy", 1)
    qs, far, last_west, turn = [None] * PARTS, [None] * PARTS, list(west), south
    sends = [(i, i - 2) for i in range(2, columns, 2)] + [(i, i + 2) for i in range(1, columns - 2, 2)]
    for p in range(PARTS):
        qs[p], turn = kernel_call(
            "last_east%d" % p,
            functools.partial(east_plain_body, TICKS - 1, p),
            (part, part),
            [VMEM] * 4 + [ANY],
            [VMEM] * 2,
        )(west[p], north[p], info, east_held, turn)
        west[p] = line(turn, "gx", 1)
        far[p] = lax.ppermute(qs[p], "gx", sends)
    cell = lambda shape, dtype: jax.ShapeDtypeStruct((1, 1) + shape, dtype)
    pairs = [(i, i ^ 1) for i in range(columns)]
    tray = jax.ShapeDtypeStruct((2, sources, 2 * width + corner_width), kind)
    tray = kernel_call("last_south", last_south_body, tray, [VMEM] * 5 + [ANY], VMEM)(
        qs[0], qs[1], south_held, last_west[0], last_west[1], turn
    )
    total, both = kernel_call(
        "middle0", first_middle_body, (part, whole), [VMEM] * 3 + [ANY] * 2, [VMEM] * 2
    )(qs[0], qs[1], far[0], west[0], tray)
    arrived = line(tray, "gy", 1)
    side0 = lax.ppermute(total, "gx", pairs)
    down = line(both, "gy", -1)
    total, west_out, heads = kernel_call(
        "middle1",
        middle_body,
        (part, cell(whole.shape, kind), head),
        [VMEM] * 4 + [ANY],
        [VMEM, HBM, VMEM],
        [pltpu.VMEM(whole.shape, kind), dma(())],
    )(qs[1], far[1], west[0], west[1], total)
    side1 = lax.ppermute(total, "gx", pairs)
    second = ring(heads, "gy", 1)
    base, corner_first, north_out = kernel_call(
        "base",
        base_body,
        (
            jax.ShapeDtypeStruct(whole.shape, jnp.float32),
            cell(head.shape, kind),
            cell(whole.shape, kind),
        ),
        [VMEM] * 4 + [ANY],
        [VMEM, HBM, HBM],
        [pltpu.VMEM(whole.shape, kind), pltpu.VMEM(head.shape, kind), dma((2,))],
    )(both, arrived, down, side0, total)
    residual, corner_second = kernel_call(
        "final",
        final_body,
        (cell(whole.shape, jnp.float32), cell(head.shape, kind)),
        [VMEM] * 3,
        [HBM, HBM],
        [
            pltpu.VMEM(part.shape, jnp.float32),
            pltpu.VMEM(head.shape, kind),
            dma((2,)),
            dma((2,)),
        ],
    )(base, side1, second)
    return west_out, north_out, corner_first, corner_second, residual


def solution(mesh):
    cell = P("gx", "gy")
    return jax.shard_map(
        on_device,
        mesh=mesh,
        in_specs=(P(),) + (cell,) * 8,
        out_specs=(cell,) * 5,
        check_vma=False,
    )
```

time: 213 us -> 92 us (0.43)
  the two profiles are of different devices: /device:TPU:12 before, /device:TPU:0 now
where the time goes in v1:
time: 92 us; the launch traced here: 91.5 us
  waiting for transfers between devices  34.4 us (37%)
  starting transfers between devices  29.6 us (32%)
  Pallas kernels  26.3 us (29%)
  between operations  1.2 us (1%)
    ppermute x21, waiting for transfers between devices, ring(): lax.ppermute(x, axis, [(i, (i + distance) % size) for i in range(size)])  26.9 us
    ppermute x21, starting transfers between devices, ring(): lax.ppermute(x, axis, [(i, (i + distance) % size) for i in range(size)])  15.6 us
    ppermute x4, starting transfers between devices, line(): lax.ppermute(x, axis, [(i, i + distance) for i in range(size) if 0 <= i +...  9.08 us
    pallas_call x8, Pallas kernels, on_device(): kernel_call('south', functools.partial(south_body, corner_width), part, [...  5.72 us
    pallas_call x6, Pallas kernels, on_device(): kernel_call('east', functools.partial(east_plain_body, tick, p), (part, p...  5.13 us
    pallas_call x1, Pallas kernels, on_device(): kernel_call('first', first_body, (part, part, part, maps, info), [HBM] *...  3.81 us
    ppermute x1, waiting for transfers between devices, on_device(): side0 = lax.ppermute(total, 'gx', pairs)  3.42 us
    ppermute x1, waiting for transfers between devices, on_device(): side1 = lax.ppermute(total, 'gx', pairs)  3.37 us
  transfers between devices with their start and end apart: 29, of which 18 were waited for; matrix products, arithmetic and copies ran while one was open for 0% of the time, Pallas kernels for 23%

profile of v1, /device:TPU:0, one launch (start us, length us, event | category | flops | bytes accessed | tf_op | source)
XLA Modules:
  0.0 91.5 jit_solution(7283183941200041732)
XLA Ops:
  0.6 3.8 %first.1 = (bf16[2,64,1024]{2,1,0:T(8,128)(2,1)S(1)}, bf16[2,64,1024]{2,1,0:T(8,128)(2,1)S(1)}, bf16[2,64,1024]{2,1,0:T(8,128)(2,1)S(1)}, bf16[2,1024,1024]{2,1,0:T(8,128)(2,1)S(1)}, f32[128,128]{1,0:T(8,128)S(1)}) custom-call(s32[16]{0:T(128)} %plan.1, f32[1,1,16,2,128]{4,3,2,1,0:T(2,128)} %amplitude.1, s32[1,1,16,128]{3,2,1,0:T(8,128)} %positions.1, ...), custom_call_target="tpu_custom_call" | custom-call | flops 1000 | bytes 1000 | tf_op jit(solution)/shard_map/first/pallas_call | solution.py:301
  4.4 3.0 %collective-permute-start.2 = (bf16[2,64,1024]{2,1,0:T(8,128)(2,1)S(1)}, bf16[2,64,1024]{2,1,0:T(8,128)(2,1)S(1)}, u32[]{:S(2)}, u32[]{:S(2)}) collective-permute-start(bf16[2,64,1024]{2,1,0:T(8,128)(2,1)S(1)} %get-tuple-element.48), channel_id=1, source_target_pairs={{0,8},{8,16},{16,24},{24,0},{1,9},{9,17},{17,25},{25,1},{2,10},{10... | collective-permute-start | bytes 786440 | tf_op jit(solution)/shard_map/ppermute | solution.py:39
  7.4 2.5 %first_south.1 = (bf16[2,64,1024]{2,1,0:T(8,128)(2,1)S(1)}, bf16[2,1024,1024]{2,1,0:T(8,128)(2,1)S(1)}) custom-call(bf16[2,64,1024]{2,1,0:T(8,128)(2,1)S(1)} %get-tuple-element.44.q, bf16[1,1,2,1024,1024]{4,3,2,1,0:T(8,128)(2,1)} %south_map.1), custom_call_target="tpu_custom_call" | custom-call | flops 1000 | bytes 1000 | tf_op jit(solution)/shard_map/first_south/pallas_call | solution.py:321
  10.7 1.5 %collective-permute-start = (bf16[2,64,1024]{2,1,0:T(8,128)(2,1)S(1)}, bf16[2,64,1024]{2,1,0:T(8,128)(2,1)S(1)}, u32[]{:S(2)}, u32[]{:S(2)}) collective-permute-start(bf16[2,64,1024]{2,1,0:T(8,128)(2,1)S(1)} %east.9.turn), channel_id=1, source_target_pairs={{0,8},{8,16},{16,24},{24,0},{1,9},{9,17},{17,25},{25,1},{2,10},{10... | collective-permute-start | bytes 786440 | tf_op jit(solution)/shard_map/ppermute | solution.py:39
  13.0 1.5 %collective-permute-start.1 = (bf16[2,64,1024]{2,1,0:T(8,128)(2,1)S(1)}, bf16[2,64,1024]{2,1,0:T(8,128)(2,1)S(1)}, u32[]{:S(2)}, u32[]{:S(2)}) collective-permute-start(bf16[2,64,1024]{2,1,0:T(8,128)(2,1)S(1)} %south.9.turn), channel_id=1, source_target_pairs={{0,1},{1,2},{2,3},{3,4},{4,5},{5,6},{6,7},{7,0},{8,9},{9,10},{10,1... | collective-permute-start | bytes 786440 | tf_op jit(solution)/shard_map/ppermute | solution.py:39
  14.7 2.8 %collective-permute-done.3.n = bf16[2,64,1024]{2,1,0:T(8,128)(2,1)S(1)} collective-permute-done((bf16[2,64,1024]{2,1,0:T(8,128)(2,1)S(1)}, bf16[2,64,1024]{2,1,0:T(8,128)(2,1)S(1)}, u32[]{:S(2)}, u32[]{:S(2)}) %collective-permute-start.3) | collective-permute-done | bytes 262176 | tf_op jit(solution)/shard_map/ppermute | solution.py:39
  18.4 1.5 %collective-permute-start.6 = (bf16[2,64,1024]{2,1,0:T(8,128)(2,1)S(1)}, bf16[2,64,1024]{2,1,0:T(8,128)(2,1)S(1)}, u32[]{:S(2)}, u32[]{:S(2)}) collective-permute-start(bf16[2,64,1024]{2,1,0:T(8,128)(2,1)S(1)} %get-tuple-element.50.turn), channel_id=1, source_target_pairs={{0,8},{8,16},{16,24},{24,0},{1,9},{9,17},{17,25},{25,1},{2,10},{10... | collective-permute-start | bytes 786440 | tf_op jit(solution)/shard_map/ppermute | solution.py:39
  21.6 1.5 %collective-permute-start.4 = (bf16[2,64,1024]{2,1,0:T(8,128)(2,1)S(1)}, bf16[2,64,1024]{2,1,0:T(8,128)(2,1)S(1)}, u32[]{:S(2)}, u32[]{:S(2)}) collective-permute-start(bf16[2,64,1024]{2,1,0:T(8,128)(2,1)S(1)} %get-tuple-element.51.turn), channel_id=1, source_target_pairs={{0,8},{8,16},{16,24},{24,0},{1,9},{9,17},{17,25},{25,1},{2,10},{10... | collective-permute-start | bytes 786440 | tf_op jit(solution)/shard_map/ppermute | solution.py:39
  24.0 4.4 %collective-permute-done.7.n = bf16[2,64,1024]{2,1,0:T(8,128)(2,1)S(1)} collective-permute-done((bf16[2,64,1024]{2,1,0:T(8,128)(2,1)S(1)}, bf16[2,64,1024]{2,1,0:T(8,128)(2,1)S(1)}, u32[]{:S(2)}, u32[]{:S(2)}) %collective-permute-start.7) | collective-permute-done | bytes 262176 | tf_op jit(solution)/shard_map/ppermute | solution.py:39
  29.2 1.5 %collective-permute-start.10 = (bf16[2,64,1024]{2,1,0:T(8,128)(2,1)S(1)}, bf16[2,64,1024]{2,1,0:T(8,128)(2,1)S(1)}, u32[]{:S(2)}, u32[]{:S(2)}) collective-permute-start(bf16[2,64,1024]{2,1,0:T(8,128)(2,1)S(1)} %get-tuple-element.54.turn), channel_id=1, source_target_pairs={{0,8},{8,16},{16,24},{24,0},{1,9},{9,17},{17,25},{25,1},{2,10},{10... | collective-permute-start | bytes 786440 | tf_op jit(solution)/shard_map/ppermute | solution.py:39
  31.6 1.8 %collective-permute-done.4.w = bf16[2,64,1024]{2,1,0:T(8,128)(2,1)S(1)} collective-permute-done((bf16[2,64,1024]{2,1,0:T(8,128)(2,1)S(1)}, bf16[2,64,1024]{2,1,0:T(8,128)(2,1)S(1)}, u32[]{:S(2)}, u32[]{:S(2)}) %collective-permute-start.4) | collective-permute-done | bytes 262176 | tf_op jit(solution)/shard_map/ppermute | solution.py:39
  35.7 3.4 %collective-permute-done.11.n = bf16[2,64,1024]{2,1,0:T(8,128)(2,1)S(1)} collective-permute-done((bf16[2,64,1024]{2,1,0:T(8,128)(2,1)S(1)}, bf16[2,64,1024]{2,1,0:T(8,128)(2,1)S(1)}, u32[]{:S(2)}, u32[]{:S(2)}) %collective-permute-start.11) | collective-permute-done | bytes 262176 | tf_op jit(solution)/shard_map/ppermute | solution.py:39
  41.9 1.4 %collective-permute-done.9.n = bf16[2,64,1024]{2,1,0:T(8,128)(2,1)S(1)} collective-permute-done((bf16[2,64,1024]{2,1,0:T(8,128)(2,1)S(1)}, bf16[2,64,1024]{2,1,0:T(8,128)(2,1)S(1)}, u32[]{:S(2)}, u32[]{:S(2)}) %collective-permute-start.9) | collective-permute-done | bytes 262176 | tf_op jit(solution)/shard_map/ppermute | solution.py:39
  43.3 1.7 %collective-permute-done.8.w = bf16[2,64,1024]{2,1,0:T(8,128)(2,1)S(1)} collective-permute-done((bf16[2,64,1024]{2,1,0:T(8,128)(2,1)S(1)}, bf16[2,64,1024]{2,1,0:T(8,128)(2,1)S(1)}, u32[]{:S(2)}, u32[]{:S(2)}) %collective-permute-start.8) | collective-permute-done | bytes 262176 | tf_op jit(solution)/shard_map/ppermute | solution.py:39
  47.4 2.1 %collective-permute-done.15.n = bf16[2,64,1024]{2,1,0:T(8,128)(2,1)S(1)} collective-permute-done((bf16[2,64,1024]{2,1,0:T(8,128)(2,1)S(1)}, bf16[2,64,1024]{2,1,0:T(8,128)(2,1)S(1)}, u32[]{:S(2)}, u32[]{:S(2)}) %collective-permute-start.15) | collective-permute-done | bytes 262176 | tf_op jit(solution)/shard_map/ppermute | solution.py:39
  49.5 1.1 %collective-permute-done.14.w = bf16[2,64,1024]{2,1,0:T(8,128)(2,1)S(1)} collective-permute-done((bf16[2,64,1024]{2,1,0:T(8,128)(2,1)S(1)}, bf16[2,64,1024]{2,1,0:T(8,128)(2,1)S(1)}, u32[]{:S(2)}, u32[]{:S(2)}) %collective-permute-start.14) | collective-permute-done | bytes 262176 | tf_op jit(solution)/shard_map/ppermute | solution.py:39
  53.2 1.8 %collective-permute-done.13.n = bf16[2,64,1024]{2,1,0:T(8,128)(2,1)S(1)} collective-permute-done((bf16[2,64,1024]{2,1,0:T(8,128)(2,1)S(1)}, bf16[2,64,1024]{2,1,0:T(8,128)(2,1)S(1)}, u32[]{:S(2)}, u32[]{:S(2)}) %collective-permute-start.13) | collective-permute-done | bytes 262176 | tf_op jit(solution)/shard_map/ppermute | solution.py:39
  55.0 1.3 %collective-permute-done.12.w = bf16[2,64,1024]{2,1,0:T(8,128)(2,1)S(1)} collective-permute-done((bf16[2,64,1024]{2,1,0:T(8,128)(2,1)S(1)}, bf16[2,64,1024]{2,1,0:T(8,128)(2,1)S(1)}, u32[]{:S(2)}, u32[]{:S(2)}) %collective-permute-start.12) | collective-permute-done | bytes 262176 | tf_op jit(solution)/shard_map/ppermute | solution.py:39
  58.6 2.1 %collective-permute-done.19.n = bf16[2,64,1024]{2,1,0:T(8,128)(2,1)S(1)} collective-permute-done((bf16[2,64,1024]{2,1,0:T(8,128)(2,1)S(1)}, bf16[2,64,1024]{2,1,0:T(8,128)(2,1)S(1)}, u32[]{:S(2)}, u32[]{:S(2)}) %collective-permute-start.19) | collective-permute-done | bytes 262176 | tf_op jit(solution)/shard_map/ppermute | solution.py:39
  60.8 1.1 %collective-permute-done.18.w.w0 = bf16[2,64,1024]{2,1,0:T(8,128)(2,1)S(1)} collective-permute-done((bf16[2,64,1024]{2,1,0:T(8,128)(2,1)S(1)}, bf16[2,64,1024]{2,1,0:T(8,128)(2,1)S(1)}, u32[]{:S(2)}, u32[]{:S(2)}) %collective-permute-start.18) | collective-permute-done | bytes 262176 | tf_op jit(solution)/shard_map/ppermute | solution.py:39
  62.7 2.6 %collective-permute-start.21 = (bf16[2,64,1024]{2,1,0:T(8,128)(2,1)S(1)}, bf16[2,64,1024]{2,1,0:T(8,128)(2,1)S(1)}, u32[]{:S(2)}, u32[]{:S(2)}) collective-permute-start(bf16[2,64,1024]{2,1,0:T(8,128)(2,1)S(1)} %get-tuple-element.65.turn), channel_id=1, source_target_pairs={{0,8},{8,16},{16,24},{1,9},{9,17},{17,25},{2,10},{10,18},{18,26},{... | collective-permute-start | bytes 786440 | tf_op jit(solution)/shard_map/ppermute | solution.py:44
  65.3 1.3 %collective-permute-start.23 = (bf16[2,64,1024]{2,1,0:T(8,128)(2,1)S(1)}, bf16[2,64,1024]{2,1,0:T(8,128)(2,1)S(1)}, u32[]{:S(2)}, u32[]{:S(2)}) collective-permute-start(bf16[2,64,1024]{2,1,0:T(8,128)(2,1)S(1)} %get-tuple-element.68.q0), channel_id=1, source_target_pairs={{16,0},{8,24},{17,1},{9,25},{18,2},{10,26},{19,3},{11,27},{20,4},{... | collective-permute-start | bytes 786440 | tf_op jit(solution)/shard_map/ppermute | solution.py:357
  67.5 3.9 %collective-permute-start.22 = (bf16[2,64,1024]{2,1,0:T(8,128)(2,1)S(1)}, bf16[2,64,1024]{2,1,0:T(8,128)(2,1)S(1)}, u32[]{:S(2)}, u32[]{:S(2)}) collective-permute-start(bf16[2,64,1024]{2,1,0:T(8,128)(2,1)S(1)} %get-tuple-element.67.turn), channel_id=1, source_target_pairs={{0,8},{8,16},{16,24},{1,9},{9,17},{17,25},{2,10},{10,18},{18,26},{... | collective-permute-start | bytes 786440 | tf_op jit(solution)/shard_map/ppermute | solution.py:44
  71.4 1.3 %collective-permute-start.20 = (bf16[2,64,1024]{2,1,0:T(8,128)(2,1)S(1)}, bf16[2,64,1024]{2,1,0:T(8,128)(2,1)S(1)}, u32[]{:S(2)}, u32[]{:S(2)}) collective-permute-start(bf16[2,64,1024]{2,1,0:T(8,128)(2,1)S(1)} %get-tuple-element.66.q1.a), channel_id=1, source_target_pairs={{16,0},{8,24},{17,1},{9,25},{18,2},{10,26},{19,3},{11,27},{20,4},{... | collective-permute-start | bytes 786440 | tf_op jit(solution)/shard_map/ppermute | solution.py:357
  72.7 1.3 %last_south.1.turn = bf16[2,128,2176]{2,1,0:T(8,128)(2,1)S(1)} custom-call(bf16[2,64,1024]{2,1,0:T(8,128)(2,1)S(1)} %get-tuple-element.68.q0, bf16[2,64,1024]{2,1,0:T(8,128)(2,1)S(1)} %get-tuple-element.66.q1.a, bf16[2,1024,1024]{2,1,0:T(8,128)(2,1)S(1)} %get-tuple-element.46.maps, bf16[2,64,1024]{2,1,0:T(8,128)(2,1)S(1)} %collective-permute-done.18.w.w0, ...), custom_call_target="tpu_custom_call" | custom-call | flops 1000 | bytes 1000 | tf_op jit(solution)/shard_map/last_south/pallas_call | solution.py:361
  74.0 1.4 %collective-permute-start.24 = (bf16[2,128,2176]{2,1,0:T(8,128)(2,1)S(1)}, bf16[2,128,2176]{2,1,0:T(8,128)(2,1)S(1)}, u32[]{:S(2)}, u32[]{:S(2)}) collective-permute-start(bf16[2,128,2176]{2,1,0:T(8,128)(2,1)S(1)} %last_south.1.turn), channel_id=1, source_target_pairs={{0,1},{1,2},{2,3},{3,4},{4,5},{5,6},{6,7},{8,9},{9,10},{10,11},{11... | collective-permute-start | bytes 3342344 | tf_op jit(solution)/shard_map/ppermute | solution.py:44
  75.4 2.2 %collective-permute-start.26 = (bf16[2,64,1024]{2,1,0:T(8,128)(2,1)S(1)}, bf16[2,64,1024]{2,1,0:T(8,128)(2,1)S(1)}, u32[]{:S(2)}, u32[]{:S(2)}) collective-permute-start(bf16[2,64,1024]{2,1,0:T(8,128)(2,1)S(1)} %get-tuple-element.69.turn), channel_id=1, source_target_pairs={{0,8},{8,0},{16,24},{24,16},{1,9},{9,1},{17,25},{25,17},{2,10},{10... | collective-permute-start | bytes 786440 | tf_op jit(solution)/shard_map/ppermute | solution.py:368
  77.7 1.3 %collective-permute-start.25 = (bf16[2,128,1024]{2,1,0:T(8,128)(2,1)S(1)}, bf16[2,128,1024]{2,1,0:T(8,128)(2,1)S(1)}, u32[]{:S(2)}, u32[]{:S(2)}) collective-permute-start(bf16[2,128,1024]{2,1,0:T(8,128)(2,1)S(1)} %get-tuple-element.71.q), channel_id=1, source_target_pairs={{1,0},{2,1},{3,2},{4,3},{5,4},{6,5},{7,6},{9,8},{10,9},{11,10},{12... | collective-permute-start | bytes 1572872 | tf_op jit(solution)/shard_map/ppermute | solution.py:44
  81.2 3.4 %collective-permute-done.26.side = bf16[2,64,1024]{2,1,0:T(8,128)(2,1)S(1)} collective-permute-done((bf16[2,64,1024]{2,1,0:T(8,128)(2,1)S(1)}, bf16[2,64,1024]{2,1,0:T(8,128)(2,1)S(1)}, u32[]{:S(2)}, u32[]{:S(2)}) %collective-permute-start.26) | collective-permute-done | bytes 262176 | tf_op jit(solution)/shard_map/ppermute | solution.py:368
  85.7 1.2 %collective-permute-done.28.second = bf16[2,128,128]{2,1,0:T(8,128)(2,1)S(1)} collective-permute-done((bf16[2,128,128]{2,1,0:T(8,128)(2,1)S(1)}, bf16[2,128,128]{2,1,0:T(8,128)(2,1)S(1)}, u32[]{:S(2)}, u32[]{:S(2)}) %collective-permute-start.28) | collective-permute-done | bytes 65568 | tf_op jit(solution)/shard_map/ppermute | solution.py:39
  86.9 3.4 %collective-permute-done.27.side = bf16[2,64,1024]{2,1,0:T(8,128)(2,1)S(1)} collective-permute-done((bf16[2,64,1024]{2,1,0:T(8,128)(2,1)S(1)}, bf16[2,64,1024]{2,1,0:T(8,128)(2,1)S(1)}, u32[]{:S(2)}, u32[]{:S(2)}) %collective-permute-start.27) | collective-permute-done | bytes 262176 | tf_op jit(solution)/shard_map/ppermute | solution.py:378
  90.3 1.0 %final.1 = (f32[1,1,2,128,1024]{4,3,2,1,0:T(8,128)}, bf16[1,1,2,128,128]{4,3,2,1,0:T(8,128)(2,1)}) custom-call(f32[2,128,1024]{2,1,0:T(8,128)S(1)} %get-tuple-element.75.base, bf16[2,64,1024]{2,1,0:T(8,128)(2,1)S(1)} %collective-permute-done.27.side, bf16[2,128,128]{2,1,0:T(8,128)(2,1)S(1)} %collective-permute-done.28.second), custom_call_target="tpu_custom_call" | custom-call | flops 1000 | bytes 1000 | tf_op jit(solution)/shard_map/final/pallas_call | solution.py:392
  (55 shorter events, 24.1 us)
Async XLA Ops:
  4.4 10.3 %collective-permute-start.2 = (bf16[2,64,1024]{2,1,0:T(8,128)(2,1)S(1)}, bf16[2,64,1024]{2,1,0:T(8,128)(2,1)S(1)}, u32[]{:S(2)}, u32[]{:S(2)}) collective-permute-start(bf16[2,64,1024]{2,1,0:T(8,128)(2,1)S(1)} %get-tuple-element.48), channel_id=1, source_target_pairs={{0,8},{8,16},{16,24},{24,0},{1,9},{9,17},{17,25},{25,1},{2,10},{10... | collective-permute-start | bytes 786440 | tf_op jit(solution)/shard_map/ppermute | solution.py:39
  9.9 7.6 %collective-permute-start.3 = (bf16[2,64,1024]{2,1,0:T(8,128)(2,1)S(1)}, bf16[2,64,1024]{2,1,0:T(8,128)(2,1)S(1)}, u32[]{:S(2)}, u32[]{:S(2)}) collective-permute-start(bf16[2,64,1024]{2,1,0:T(8,128)(2,1)S(1)} %get-tuple-element.45.turn), channel_id=1, source_target_pairs={{0,1},{1,2},{2,3},{3,4},{4,5},{5,6},{6,7},{7,0},{8,9},{9,10},{10,1... | collective-permute-start | bytes 786440 | tf_op jit(solution)/shard_map/ppermute | solution.py:39
  10.7 10.1 %collective-permute-start = (bf16[2,64,1024]{2,1,0:T(8,128)(2,1)S(1)}, bf16[2,64,1024]{2,1,0:T(8,128)(2,1)S(1)}, u32[]{:S(2)}, u32[]{:S(2)}) collective-permute-start(bf16[2,64,1024]{2,1,0:T(8,128)(2,1)S(1)} %east.9.turn), channel_id=1, source_target_pairs={{0,8},{8,16},{16,24},{24,0},{1,9},{9,17},{17,25},{25,1},{2,10},{10... | collective-permute-start | bytes 786440 | tf_op jit(solution)/shard_map/ppermute | solution.py:39
  12.2 5.3 %copy-start = (bf16[1,1,2,128,128]{4,3,2,1,0:T(8,128)(2,1)S(1)}, bf16[1,1,2,128,128]{4,3,2,1,0:T(8,128)(2,1)}, u32[]{:S(2)}) copy-start(bf16[1,1,2,128,128]{4,3,2,1,0:T(8,128)(2,1)} %corner.5) | copy-start | bytes 196612
  13.0 7.8 %collective-permute-start.1 = (bf16[2,64,1024]{2,1,0:T(8,128)(2,1)S(1)}, bf16[2,64,1024]{2,1,0:T(8,128)(2,1)S(1)}, u32[]{:S(2)}, u32[]{:S(2)}) collective-permute-start(bf16[2,64,1024]{2,1,0:T(8,128)(2,1)S(1)} %south.9.turn), channel_id=1, source_target_pairs={{0,1},{1,2},{2,3},{3,4},{4,5},{5,6},{6,7},{7,0},{8,9},{9,10},{10,1... | collective-permute-start | bytes 786440 | tf_op jit(solution)/shard_map/ppermute | solution.py:39
  18.4 9.9 %collective-permute-start.6 = (bf16[2,64,1024]{2,1,0:T(8,128)(2,1)S(1)}, bf16[2,64,1024]{2,1,0:T(8,128)(2,1)S(1)}, u32[]{:S(2)}, u32[]{:S(2)}) collective-permute-start(bf16[2,64,1024]{2,1,0:T(8,128)(2,1)S(1)} %get-tuple-element.50.turn), channel_id=1, source_target_pairs={{0,8},{8,16},{16,24},{24,0},{1,9},{9,17},{17,25},{25,1},{2,10},{10... | collective-permute-start | bytes 786440 | tf_op jit(solution)/shard_map/ppermute | solution.py:39
  20.7 7.6 %collective-permute-start.7 = (bf16[2,64,1024]{2,1,0:T(8,128)(2,1)S(1)}, bf16[2,64,1024]{2,1,0:T(8,128)(2,1)S(1)}, u32[]{:S(2)}, u32[]{:S(2)}) collective-permute-start(bf16[2,64,1024]{2,1,0:T(8,128)(2,1)S(1)} %south.10.turn), channel_id=1, source_target_pairs={{0,1},{1,2},{2,3},{3,4},{4,5},{5,6},{6,7},{7,0},{8,9},{9,10},{10,1... | collective-permute-start | bytes 786440 | tf_op jit(solution)/shard_map/ppermute | solution.py:39
  21.6 11.7 %collective-permute-start.4 = (bf16[2,64,1024]{2,1,0:T(8,128)(2,1)S(1)}, bf16[2,64,1024]{2,1,0:T(8,128)(2,1)S(1)}, u32[]{:S(2)}, u32[]{:S(2)}) collective-permute-start(bf16[2,64,1024]{2,1,0:T(8,128)(2,1)S(1)} %get-tuple-element.51.turn), channel_id=1, source_target_pairs={{0,8},{8,16},{16,24},{24,0},{1,9},{9,17},{17,25},{25,1},{2,10},{10... | collective-permute-start | bytes 786440 | tf_op jit(solution)/shard_map/ppermute | solution.py:39
  23.9 7.6 %collective-permute-start.5 = (bf16[2,64,1024]{2,1,0:T(8,128)(2,1)S(1)}, bf16[2,64,1024]{2,1,0:T(8,128)(2,1)S(1)}, u32[]{:S(2)}, u32[]{:S(2)}) collective-permute-start(bf16[2,64,1024]{2,1,0:T(8,128)(2,1)S(1)} %south.11.turn), channel_id=1, source_target_pairs={{0,1},{1,2},{2,3},{3,4},{4,5},{5,6},{6,7},{7,0},{8,9},{9,10},{10,1... | collective-permute-start | bytes 786440 | tf_op jit(solution)/shard_map/ppermute | solution.py:39
  29.2 10.2 %collective-permute-start.10 = (bf16[2,64,1024]{2,1,0:T(8,128)(2,1)S(1)}, bf16[2,64,1024]{2,1,0:T(8,128)(2,1)S(1)}, u32[]{:S(2)}, u32[]{:S(2)}) collective-permute-start(bf16[2,64,1024]{2,1,0:T(8,128)(2,1)S(1)} %get-tuple-element.54.turn), channel_id=1, source_target_pairs={{0,8},{8,16},{16,24},{24,0},{1,9},{9,17},{17,25},{25,1},{2,10},{10... | collective-permute-start | bytes 786440 | tf_op jit(solution)/shard_map/ppermute | solution.py:39
  31.5 7.6 %collective-permute-start.11 = (bf16[2,64,1024]{2,1,0:T(8,128)(2,1)S(1)}, bf16[2,64,1024]{2,1,0:T(8,128)(2,1)S(1)}, u32[]{:S(2)}, u32[]{:S(2)}) collective-permute-start(bf16[2,64,1024]{2,1,0:T(8,128)(2,1)S(1)} %south.12.turn), channel_id=1, source_target_pairs={{0,1},{1,2},{2,3},{3,4},{4,5},{5,6},{6,7},{7,0},{8,9},{9,10},{10,1... | collective-permute-start | bytes 786440 | tf_op jit(solution)/shard_map/ppermute | solution.py:39
  34.2 10.8 %collective-permute-start.8 = (bf16[2,64,1024]{2,1,0:T(8,128)(2,1)S(1)}, bf16[2,64,1024]{2,1,0:T(8,128)(2,1)S(1)}, u32[]{:S(2)}, u32[]{:S(2)}) collective-permute-start(bf16[2,64,1024]{2,1,0:T(8,128)(2,1)S(1)} %get-tuple-element.55.turn), channel_id=1, source_target_pairs={{0,8},{8,16},{16,24},{24,0},{1,9},{9,17},{17,25},{25,1},{2,10},{10... | collective-permute-start | bytes 786440 | tf_op jit(solution)/shard_map/ppermute | solution.py:39
  35.6 7.6 %collective-permute-start.9 = (bf16[2,64,1024]{2,1,0:T(8,128)(2,1)S(1)}, bf16[2,64,1024]{2,1,0:T(8,128)(2,1)S(1)}, u32[]{:S(2)}, u32[]{:S(2)}) collective-permute-start(bf16[2,64,1024]{2,1,0:T(8,128)(2,1)S(1)} %south.13.turn), channel_id=1, source_target_pairs={{0,1},{1,2},{2,3},{3,4},{4,5},{5,6},{6,7},{7,0},{8,9},{9,10},{10,1... | collective-permute-start | bytes 786440 | tf_op jit(solution)/shard_map/ppermute | solution.py:39
  40.3 10.4 %collective-permute-start.14 = (bf16[2,64,1024]{2,1,0:T(8,128)(2,1)S(1)}, bf16[2,64,1024]{2,1,0:T(8,128)(2,1)S(1)}, u32[]{:S(2)}, u32[]{:S(2)}) collective-permute-start(bf16[2,64,1024]{2,1,0:T(8,128)(2,1)S(1)} %get-tuple-element.58.turn), channel_id=1, source_target_pairs={{0,8},{8,16},{16,24},{24,0},{1,9},{9,17},{17,25},{25,1},{2,10},{10... | collective-permute-start | bytes 786440 | tf_op jit(solution)/shard_map/ppermute | solution.py:39
  41.7 7.8 %collective-permute-start.15 = (bf16[2,64,1024]{2,1,0:T(8,128)(2,1)S(1)}, bf16[2,64,1024]{2,1,0:T(8,128)(2,1)S(1)}, u32[]{:S(2)}, u32[]{:S(2)}) collective-permute-start(bf16[2,64,1024]{2,1,0:T(8,128)(2,1)S(1)} %south.14.turn), channel_id=1, source_target_pairs={{0,1},{1,2},{2,3},{3,4},{4,5},{5,6},{6,7},{7,0},{8,9},{9,10},{10,1... | collective-permute-start | bytes 786440 | tf_op jit(solution)/shard_map/ppermute | solution.py:39
  45.9 10.4 %collective-permute-start.12 = (bf16[2,64,1024]{2,1,0:T(8,128)(2,1)S(1)}, bf16[2,64,1024]{2,1,0:T(8,128)(2,1)S(1)}, u32[]{:S(2)}, u32[]{:S(2)}) collective-permute-start(bf16[2,64,1024]{2,1,0:T(8,128)(2,1)S(1)} %get-tuple-element.59.turn), channel_id=1, source_target_pairs={{0,8},{8,16},{16,24},{24,0},{1,9},{9,17},{17,25},{25,1},{2,10},{10... | collective-permute-start | bytes 786440 | tf_op jit(solution)/shard_map/ppermute | solution.py:39
  47.3 7.6 %collective-permute-start.13 = (bf16[2,64,1024]{2,1,0:T(8,128)(2,1)S(1)}, bf16[2,64,1024]{2,1,0:T(8,128)(2,1)S(1)}, u32[]{:S(2)}, u32[]{:S(2)}) collective-permute-start(bf16[2,64,1024]{2,1,0:T(8,128)(2,1)S(1)} %south.15.turn), channel_id=1, source_target_pairs={{0,1},{1,2},{2,3},{3,4},{4,5},{5,6},{6,7},{7,0},{8,9},{9,10},{10,1... | collective-permute-start | bytes 786440 | tf_op jit(solution)/shard_map/ppermute | solution.py:39
  51.5 10.4 %collective-permute-start.18 = (bf16[2,64,1024]{2,1,0:T(8,128)(2,1)S(1)}, bf16[2,64,1024]{2,1,0:T(8,128)(2,1)S(1)}, u32[]{:S(2)}, u32[]{:S(2)}) collective-permute-start(bf16[2,64,1024]{2,1,0:T(8,128)(2,1)S(1)} %get-tuple-element.62.turn), channel_id=1, source_target_pairs={{0,8},{8,16},{16,24},{24,0},{1,9},{9,17},{17,25},{25,1},{2,10},{10... | collective-permute-start | bytes 786440 | tf_op jit(solution)/shard_map/ppermute | solution.py:39
  53.1 7.6 %collective-permute-start.19 = (bf16[2,64,1024]{2,1,0:T(8,128)(2,1)S(1)}, bf16[2,64,1024]{2,1,0:T(8,128)(2,1)S(1)}, u32[]{:S(2)}, u32[]{:S(2)}) collective-permute-start(bf16[2,64,1024]{2,1,0:T(8,128)(2,1)S(1)} %south.16.turn), channel_id=1, source_target_pairs={{0,1},{1,2},{2,3},{3,4},{4,5},{5,6},{6,7},{7,0},{8,9},{9,10},{10,1... | collective-permute-start | bytes 786440 | tf_op jit(solution)/shard_map/ppermute | solution.py:39
  57.1 9.5 %collective-permute-start.16 = (bf16[2,64,1024]{2,1,0:T(8,128)(2,1)S(1)}, bf16[2,64,1024]{2,1,0:T(8,128)(2,1)S(1)}, u32[]{:S(2)}, u32[]{:S(2)}) collective-permute-start(bf16[2,64,1024]{2,1,0:T(8,128)(2,1)S(1)} %get-tuple-element.63.turn), channel_id=1, source_target_pairs={{0,8},{8,16},{16,24},{24,0},{1,9},{9,17},{17,25},{25,1},{2,10},{10... | collective-permute-start | bytes 786440 | tf_op jit(solution)/shard_map/ppermute | solution.py:39
  58.5 8.1 %collective-permute-start.17 = (bf16[2,64,1024]{2,1,0:T(8,128)(2,1)S(1)}, bf16[2,64,1024]{2,1,0:T(8,128)(2,1)S(1)}, u32[]{:S(2)}, u32[]{:S(2)}) collective-permute-start(bf16[2,64,1024]{2,1,0:T(8,128)(2,1)S(1)} %south.17.turn), channel_id=1, source_target_pairs={{0,1},{1,2},{2,3},{3,4},{4,5},{5,6},{6,7},{7,0},{8,9},{9,10},{10,1... | collective-permute-start | bytes 786440 | tf_op jit(solution)/shard_map/ppermute | solution.py:39
  62.7 12.6 %collective-permute-start.21 = (bf16[2,64,1024]{2,1,0:T(8,128)(2,1)S(1)}, bf16[2,64,1024]{2,1,0:T(8,128)(2,1)S(1)}, u32[]{:S(2)}, u32[]{:S(2)}) collective-permute-start(bf16[2,64,1024]{2,1,0:T(8,128)(2,1)S(1)} %get-tuple-element.65.turn), channel_id=1, source_target_pairs={{0,8},{8,16},{16,24},{1,9},{9,17},{17,25},{2,10},{10,18},{18,26},{... | collective-permute-start | bytes 786440 | tf_op jit(solution)/shard_map/ppermute | solution.py:44
  65.3 10.0 %collective-permute-start.23 = (bf16[2,64,1024]{2,1,0:T(8,128)(2,1)S(1)}, bf16[2,64,1024]{2,1,0:T(8,128)(2,1)S(1)}, u32[]{:S(2)}, u32[]{:S(2)}) collective-permute-start(bf16[2,64,1024]{2,1,0:T(8,128)(2,1)S(1)} %get-tuple-element.68.q0), channel_id=1, source_target_pairs={{16,0},{8,24},{17,1},{9,25},{18,2},{10,26},{19,3},{11,27},{20,4},{... | collective-permute-start | bytes 786440 | tf_op jit(solution)/shard_map/ppermute | solution.py:357
  67.5 11.5 %collective-permute-start.22 = (bf16[2,64,1024]{2,1,0:T(8,128)(2,1)S(1)}, bf16[2,64,1024]{2,1,0:T(8,128)(2,1)S(1)}, u32[]{:S(2)}, u32[]{:S(2)}) collective-permute-start(bf16[2,64,1024]{2,1,0:T(8,128)(2,1)S(1)} %get-tuple-element.67.turn), channel_id=1, source_target_pairs={{0,8},{8,16},{16,24},{1,9},{9,17},{17,25},{2,10},{10,18},{18,26},{... | collective-permute-start | bytes 786440 | tf_op jit(solution)/shard_map/ppermute | solution.py:44
  71.4 8.3 %collective-permute-start.20 = (bf16[2,64,1024]{2,1,0:T(8,128)(2,1)S(1)}, bf16[2,64,1024]{2,1,0:T(8,128)(2,1)S(1)}, u32[]{:S(2)}, u32[]{:S(2)}) collective-permute-start(bf16[2,64,1024]{2,1,0:T(8,128)(2,1)S(1)} %get-tuple-element.66.q1.a), channel_id=1, source_target_pairs={{16,0},{8,24},{17,1},{9,25},{18,2},{10,26},{19,3},{11,27},{20,4},{... | collective-permute-start | bytes 786440 | tf_op jit(solution)/shard_map/ppermute | solution.py:357
  74.0 10.7 %collective-permute-start.24 = (bf16[2,128,2176]{2,1,0:T(8,128)(2,1)S(1)}, bf16[2,128,2176]{2,1,0:T(8,128)(2,1)S(1)}, u32[]{:S(2)}, u32[]{:S(2)}) collective-permute-start(bf16[2,128,2176]{2,1,0:T(8,128)(2,1)S(1)} %last_south.1.turn), channel_id=1, source_target_pairs={{0,1},{1,2},{2,3},{3,4},{4,5},{5,6},{6,7},{8,9},{9,10},{10,11},{11... | collective-permute-start | bytes 3342344 | tf_op jit(solution)/shard_map/ppermute | solution.py:44
  75.4 9.2 %collective-permute-start.26 = (bf16[2,64,1024]{2,1,0:T(8,128)(2,1)S(1)}, bf16[2,64,1024]{2,1,0:T(8,128)(2,1)S(1)}, u32[]{:S(2)}, u32[]{:S(2)}) collective-permute-start(bf16[2,64,1024]{2,1,0:T(8,128)(2,1)S(1)} %get-tuple-element.69.turn), channel_id=1, source_target_pairs={{0,8},{8,0},{16,24},{24,16},{1,9},{9,1},{17,25},{25,17},{2,10},{10... | collective-permute-start | bytes 786440 | tf_op jit(solution)/shard_map/ppermute | solution.py:368
  77.7 7.0 %collective-permute-start.25 = (bf16[2,128,1024]{2,1,0:T(8,128)(2,1)S(1)}, bf16[2,128,1024]{2,1,0:T(8,128)(2,1)S(1)}, u32[]{:S(2)}, u32[]{:S(2)}) collective-permute-start(bf16[2,128,1024]{2,1,0:T(8,128)(2,1)S(1)} %get-tuple-element.71.q), channel_id=1, source_target_pairs={{1,0},{2,1},{3,2},{4,3},{5,4},{6,5},{7,6},{9,8},{10,9},{11,10},{12... | collective-permute-start | bytes 1572872 | tf_op jit(solution)/shard_map/ppermute | solution.py:44
  80.6 9.7 %collective-permute-start.27 = (bf16[2,64,1024]{2,1,0:T(8,128)(2,1)S(1)}, bf16[2,64,1024]{2,1,0:T(8,128)(2,1)S(1)}, u32[]{:S(2)}, u32[]{:S(2)}) collective-permute-start(bf16[2,64,1024]{2,1,0:T(8,128)(2,1)S(1)} %get-tuple-element.72.turn), channel_id=1, source_target_pairs={{0,8},{8,0},{16,24},{24,16},{1,9},{9,1},{17,25},{25,17},{2,10},{10... | collective-permute-start | bytes 786440 | tf_op jit(solution)/shard_map/ppermute | solution.py:378
  80.7 6.2 %collective-permute-start.28 = (bf16[2,128,128]{2,1,0:T(8,128)(2,1)S(1)}, bf16[2,128,128]{2,1,0:T(8,128)(2,1)S(1)}, u32[]{:S(2)}, u32[]{:S(2)}) collective-permute-start(bf16[2,128,128]{2,1,0:T(8,128)(2,1)S(1)} %get-tuple-element.76), channel_id=1, source_target_pairs={{0,1},{1,2},{2,3},{3,4},{4,5},{5,6},{6,7},{7,0},{8,9},{9,10},{10,1... | collective-permute-start | bytes 196616 | tf_op jit(solution)/shard_map/ppermute | solution.py:39

commit v2 on v1

v2 whole, which is shorter than its diff:
```python
import functools

import jax
import jax.numpy as jnp
from jax import lax
from jax.experimental import pallas as pl
from jax.experimental.pallas import tpu as pltpu
from jax.sharding import PartitionSpec as P

TICKS = 6
PARTS = 2
FIELDS = 3
PIECES = 2
VMEM = pl.BlockSpec(memory_space=pltpu.VMEM)
ANY = pl.BlockSpec(memory_space=pl.ANY)
HBM = pl.BlockSpec(memory_space=pltpu.HBM)


COSTS = dict.fromkeys(
    ("first_south", "east", "south", "last_east0", "last_east1", "middle0", "middle1"), 10**10
)


def kernel_call(name, body, outs, in_specs, out_specs, scratch=(), aliases={}):
    return pl.pallas_call(
        body,
        name=name,
        out_shape=outs,
        in_specs=in_specs,
        out_specs=out_specs,
        scratch_shapes=list(scratch),
        input_output_aliases=aliases,
        compiler_params=pltpu.CompilerParams(vmem_limit_bytes=24 << 20),
        cost_estimate=pl.CostEstimate(flops=COSTS.get(name, 1000), bytes_accessed=1000, transcendentals=0),
    )


def ring(x, axis, distance):
    size = lax.axis_size(axis)
    return lax.ppermute(x, axis, [(i, (i + distance) % size) for i in range(size)])


def line(x, axis, distance):
    size = lax.axis_size(axis)
    return lax.ppermute(
        x, axis, [(i, i + distance) for i in range(size) if 0 <= i + distance < size]
    )


def inside(axis, towards_end=False):
    here = lax.axis_index(axis)
    there = here < lax.axis_size(axis) - 1 if towards_end else here > 0
    return there.astype(jnp.float32)


def f32(x):
    return x.astype(jnp.float32)


def sources_of(info, tick, rows):
    base = tick * FIELDS
    point = info[rows, base + 2 : base + 3].astype(jnp.int32)

    def spread(part, width):
        points = lax.broadcasted_iota(jnp.int32, (point.shape[0], width), 1)
        return jnp.where(points == point, info[rows, base + part : base + part + 1], 0.0)

    return spread


def stacked(q):
    return jnp.concatenate([q[0], q[1]], 0), jnp.concatenate([-q[1], q[0]], 0)


def product(q, maps):
    ahead, turned = stacked(q)
    out = jnp.dot(ahead, maps[0], preferred_element_type=jnp.float32)
    return out + jnp.dot(turned, maps[1], preferred_element_type=jnp.float32)


def map_copies(source, held, sems):
    block = held.shape[2] // PIECES
    copies = []
    for k in range(PIECES):
        place = pl.ds(k * block, block)
        copies.append(
            pltpu.make_async_copy(source.at[0, 0, :, :, place], held.at[:, :, place], sems.at[k])
        )
    return copies


def trace_copies(part, step, sources, targets, sems):
    cut = pl.ds(part * step, step)
    return [
        pltpu.make_async_copy(source.at[0, 0, :, cut], target, sems.at[k])
        for k, (source, target) in enumerate(zip(sources, targets))
    ]


def arriving_product(q, held, copies, out):
    step, block = q.shape[1], held.shape[2] // PIECES
    ahead, turned = stacked(q)
    for k, copy in enumerate(copies):
        copy.wait()
        place = slice(k * block, (k + 1) * block)
        total = jnp.dot(ahead, held[0, :, place], preferred_element_type=jnp.float32)
        total = total + jnp.dot(turned, held[1, :, place], preferred_element_type=jnp.float32)
        out[0, :, place] = total[:step].astype(out.dtype)
        out[1, :, place] = total[step:].astype(out.dtype)


def first_boundary(part, info, w, n, c, q):
    step, width = q.shape[1:]
    corner_width = c.shape[-1]
    spread = sources_of(info, 0, slice(part * step, (part + 1) * step))
    for half in range(2):
        total = f32(w[half]) + f32(n[half]) + spread(half, width)
        q[half] = total.astype(q.dtype)
        head = total[:, :corner_width] + f32(c[half])
        q[half, :, :corner_width] = head.astype(q.dtype)


def first_body(
    plan, amplitude, positions, west, north, corner, east_map,
    q, east, held, info, order, amps, places, w, n, c, table, list_sems, trace_sems, map_sems,
):
    lists = [
        pltpu.make_async_copy(plan, order, list_sems.at[0]),
        pltpu.make_async_copy(amplitude.at[0, 0], amps, list_sems.at[1]),
        pltpu.make_async_copy(positions.at[0, 0], places, list_sems.at[2]),
    ]
    traces = trace_copies(0, q.shape[1], (west, north, corner), (w, n, c), trace_sems)
    blocks = map_copies(east_map, held, map_sems)
    for copy in lists + traces + blocks:
        copy.start()
    span = lax.axis_size("gx") + lax.axis_size("gy") - 2
    start = span - lax.axis_index("gx") - lax.axis_index("gy")
    table[...] = jnp.zeros_like(table)
    for copy in lists:
        copy.wait()
    for tick in range(TICKS):
        batch = order[start + tick]
        base = tick * FIELDS
        table[base : base + 2, :] = amps[batch]
        table[base + 2 : base + 3, :] = places[pl.ds(batch, 1), :].astype(jnp.float32)
    info[...] = table[...].T
    for copy in traces:
        copy.wait()
    first_boundary(0, info, w, n, c, q)
    arriving_product(q[...], held, blocks, east)


def first_south_body(q, info, west, north, corner, maps, turn, out, q1, w, n, c, trace_sems):
    step = q.shape[1]
    traces = trace_copies(1, step, (west, north, corner), (w, n, c), trace_sems)
    for copy in traces:
        copy.start()
    total = product(q[...], maps)
    out[0] = total[:step].astype(out.dtype)
    out[1] = total[step:].astype(out.dtype)
    for copy in traces:
        copy.wait()
    first_boundary(1, info, w, n, c, q1)


def last_east_body(part, w, n, info, maps, turn, q, out, first):
    east_body(TICKS - 1, part, w, n, info, maps, None, turn, q, out)
    start = lax.axis_index("gx") == 0

    @pl.when(start)
    def _():
        first[...] = out[...]

    @pl.when(jnp.logical_not(start))
    def _():
        first[...] = q[...]


def product_body(q, maps, turn, out):
    step = q.shape[1]
    total = product(q[...], maps)
    out[0] = total[:step].astype(out.dtype)
    out[1] = total[step:].astype(out.dtype)


def east_body(tick, part, w, n, info, maps, corner, turn, q, out):
    step, width = q.shape[1:]
    rows = slice(part * step, (part + 1) * step)
    from_west, from_north = inside("gx"), inside("gy")
    spread = sources_of(info, tick, rows)
    for half in range(2):
        total = f32(w[half]) * from_west + f32(n[half]) * from_north + spread(half, width)
        q[half] = total.astype(q.dtype)
        if corner is not None:
            corner_width = corner.shape[-1]
            head = total[:, :corner_width] + f32(corner[0, 0, half, rows])
            q[half, :, :corner_width] = head.astype(q.dtype)
    total = product(q[...], maps)
    out[0] = total[:step].astype(out.dtype)
    out[1] = total[step:].astype(out.dtype)


def east_plain_body(tick, part, w, n, info, maps, turn, q, out):
    east_body(tick, part, w, n, info, maps, None, turn, q, out)


def south_body(corner_width, q, maps, w, turn, out):
    step = q.shape[1]
    from_west = inside("gx")
    total = product(q[...], maps)
    for half in range(2):
        trace = total[half * step : (half + 1) * step]
        out[half] = trace.astype(out.dtype)
        head = trace[:, :corner_width] + f32(w[half, :, :corner_width]) * from_west
        out[half, :, :corner_width] = head.astype(out.dtype)


def last_south_body(q0, q1, maps, w0, w1, turn, tray):
    step, width = q0.shape[1:]
    from_west = inside("gx")
    for p, (q, w) in enumerate(((q0, w0), (q1, w1))):
        rows = slice(p * step, (p + 1) * step)
        tray[:, rows, width : 2 * width] = q[...]
        corner = f32(w[:, :, : tray.shape[2] - 2 * width]) * from_west
        tray[:, rows, 2 * width :] = corner.astype(tray.dtype)
    total = product(tray[:, :, width : 2 * width], maps)
    for half in range(2):
        trace = total[half * 2 * step : (half + 1) * 2 * step]
        tray[half, :, :width] = trace.astype(tray.dtype)


def has_far():
    here, size = lax.axis_index("gx"), lax.axis_size("gx")
    there = jnp.where(here % 2 == 0, here + 2, here - 2)
    return ((there >= 0) & (there < size)).astype(jnp.float32)


def first_middle_body(q0, q1, far, west, turn, total, both):
    total[...] = (f32(q0[...]) + f32(far[...]) * has_far()).astype(total.dtype)
    both[:, : q0.shape[1]] = q0[...]
    both[:, q0.shape[1] :] = q1[...]


def middle_body(q, first0, first1, second0, second1, turn, total, out, head, whole, sem):
    here, step = lax.axis_index("gx"), q.shape[1]
    by_first, by_second = (here == 1).astype(jnp.float32), (here > 1).astype(jnp.float32)
    for p, (first, second) in enumerate(((first0, second0), (first1, second1))):
        trace = f32(first[...]) * by_first + f32(second[...]) * by_second
        whole[:, p * step : (p + 1) * step] = trace.astype(whole.dtype)
    copy = pltpu.make_async_copy(whole, out.at[0, 0], sem)
    copy.start()
    head[...] = whole[:, :, : head.shape[-1]]
    total[...] = (f32(q[...]) + f32(first1[...]) * has_far()).astype(total.dtype)
    copy.wait()


def base_body(q, tray, down, side, turn, rest, first, out, residual, trace, corner, done, sems):
    step, width = side.shape[1:]
    from_north, from_south = inside("gy"), inside("gy", True)

    def along_y(half, rows):
        return (
            4.0 * f32(q[half, rows])
            - f32(tray[half, rows, width : 2 * width]) * from_north
            - f32(down[half, rows]) * from_south
        )

    for half in range(2):
        done[half] = along_y(half, slice(0, step)) - f32(side[half])
    trace[...] = (f32(tray[:, :, :width]) * from_north).astype(trace.dtype)
    corner[...] = (f32(tray[:, :, 2 * width :]) * from_north).astype(corner.dtype)
    copies = [
        pltpu.make_async_copy(done, residual.at[0, 0, :, pl.ds(0, step)], sems.at[0]),
        pltpu.make_async_copy(trace, out.at[0, 0], sems.at[1]),
        pltpu.make_async_copy(corner, first.at[0, 0], sems.at[2]),
    ]
    for copy in copies:
        copy.start()
    for half in range(2):
        rest[half] = along_y(half, slice(step, 2 * step))
    for copy in copies:
        copy.wait()


def final_body(base, side, second, begun, out, corner, rest, held, sems):
    step = side.shape[1]
    held[...] = (f32(second[...]) * inside("gy")).astype(held.dtype)
    copies = [pltpu.make_async_copy(held, corner.at[0, 0], sems.at[0])]
    copies[0].start()
    for half in range(2):
        rest[half] = base[half] - f32(side[half])
        copies.append(
            pltpu.make_async_copy(
                rest.at[half], out.at[0, 0, half, pl.ds(step, step)], sems.at[1 + half]
            )
        )
        copies[-1].start()
    for copy in copies:
        copy.wait()


def on_device(
    plan, amplitude, positions, west_in, north_in, corner_now, corner_next, east_map, south_map
):
    columns = lax.axis_size("gx")
    kind = west_in.dtype
    sources, width = west_in.shape[-2:]
    corner_width = corner_now.shape[-1]
    step = sources // PARTS
    part = jax.ShapeDtypeStruct((2, step, width), kind)
    whole = jax.ShapeDtypeStruct((2, sources, width), kind)
    head = jax.ShapeDtypeStruct((2, sources, corner_width), kind)
    maps = jax.ShapeDtypeStruct((2, width, width), kind)
    info = jax.ShapeDtypeStruct((sources, sources), jnp.float32)
    dma = pltpu.SemaphoreType.DMA

    fixed = [
        pltpu.with_memory_space_constraint(x, pltpu.HBM)
        for x in (plan, amplitude, positions, west_in, north_in, corner_now, east_map, south_map)
    ]
    bench = [pltpu.VMEM(part.shape, kind), pltpu.VMEM(part.shape, kind)]
    bench.append(pltpu.VMEM((2, step, corner_width), kind))
    q0, east, east_held, info = kernel_call(
        "first",
        first_body,
        (part, part, maps, info),
        [HBM] * 7,
        [VMEM] * 4,
        [
            pltpu.SMEM(plan.shape, plan.dtype),
            pltpu.VMEM(amplitude.shape[2:], amplitude.dtype),
            pltpu.VMEM(positions.shape[2:], positions.dtype),
            *bench,
            pltpu.VMEM((sources, sources), jnp.float32),
            dma((3,)),
            dma((3,)),
            dma((PIECES,)),
        ],
    )(*fixed[:-1])
    w0 = ring(east, "gx", 1)
    south_held = south_map.reshape(maps.shape)
    south, q1 = kernel_call(
        "first_south",
        first_south_body,
        (part, part),
        [VMEM] * 2 + [HBM] * 3 + [VMEM, ANY],
        [VMEM] * 2,
        [*bench, dma((3,))],
    )(q0, info, *fixed[3:6], south_held, east)
    n0 = ring(south, "gy", 1)
    east = kernel_call("east", product_body, part, [VMEM, VMEM, ANY], VMEM)(q1, east_held, south)
    w1 = ring(east, "gx", 1)
    south = kernel_call("south", product_body, part, [VMEM, VMEM, ANY], VMEM)(q1, south_held, east)
    n1 = ring(south, "gy", 1)
    west, north = [w0, w1], [n0, n1]
    for tick in range(1, TICKS - 1):
        for p in range(PARTS):
            w, n = west[p], north[p]
            if tick == 1:
                q, east = kernel_call(
                    "east", functools.partial(east_body, tick, p), (part, part), [VMEM] * 5 + [ANY], [VMEM] * 2
                )(w, n, info, east_held, corner_next, south)
            else:
                q, east = kernel_call(
                    "east", functools.partial(east_plain_body, tick, p), (part, part), [VMEM] * 4 + [ANY], [VMEM] * 2
                )(w, n, info, east_held, south)
            west[p] = ring(east, "gx", 1)
            south = kernel_call(
                "south", functools.partial(south_body, corner_width), part, [VMEM] * 3 + [ANY], VMEM
            )(q, south_held, w, east)
            north[p] = ring(south, "gy", 1)
    ahead = [(0, 1), (columns - 1, columns - 2)]
    ahead += [(i, i + 2 if i % 2 else i - 2) for i in range(1, columns - 1)]
    rows = lax.axis_size("gy")
    behind = [(j, j ^ 1) for j in range(rows)]
    for i, to in [(columns - 1, 1)] + [(i, i + 1) for i in range(1, columns - 1)]:
        behind += [(i * rows + j, to * rows + j) for j in range(rows)]
    qs, one, two, last_west, turn = [None] * PARTS, [None] * PARTS, [None] * PARTS, list(west), south
    for p in range(PARTS):
        qs[p], turn, first = kernel_call(
            "last_east%d" % p,
            functools.partial(last_east_body, p),
            (part, part, part),
            [VMEM] * 4 + [ANY],
            [VMEM] * 3,
        )(west[p], north[p], info, east_held, turn)
        one[p] = lax.ppermute(first, "gx", ahead)
        two[p] = lax.ppermute(turn, ("gx", "gy"), behind)
    cell = lambda shape, dtype: jax.ShapeDtypeStruct((1, 1) + shape, dtype)
    pairs = [(i, i ^ 1) for i in range(columns)]
    tray = jax.ShapeDtypeStruct((2, sources, 2 * width + corner_width), kind)
    tray = kernel_call("last_south", last_south_body, tray, [VMEM] * 5 + [ANY], VMEM)(
        qs[0], qs[1], south_held, last_west[0], last_west[1], turn
    )
    total, both = kernel_call(
        "middle0", first_middle_body, (part, whole), [VMEM] * 3 + [ANY] * 2, [VMEM] * 2
    )(qs[0], qs[1], one[0], two[0], tray)
    arrived = line(tray, "gy", 1)
    side0 = lax.ppermute(total, "gx", pairs)
    down = line(both, "gy", -1)
    total, west_out, heads = kernel_call(
        "middle1",
        middle_body,
        (part, cell(whole.shape, kind), head),
        [VMEM] * 5 + [ANY],
        [VMEM, HBM, VMEM],
        [pltpu.VMEM(whole.shape, kind), dma(())],
    )(qs[1], one[0], one[1], two[0], two[1], total)
    side1 = lax.ppermute(total, "gx", pairs)
    second = ring(heads, "gy", 1)
    rest = jax.ShapeDtypeStruct(part.shape, jnp.float32)
    rest, corner_first, north_out, residual = kernel_call(
        "base",
        base_body,
        (
            rest,
            cell(head.shape, kind),
            cell(whole.shape, kind),
            cell(whole.shape, jnp.float32),
        ),
        [VMEM] * 4 + [ANY],
        [VMEM, HBM, HBM, HBM],
        [
            pltpu.VMEM(whole.shape, kind),
            pltpu.VMEM(head.shape, kind),
            pltpu.VMEM(rest.shape, rest.dtype),
            dma((3,)),
        ],
    )(both, arrived, down, side0, total)
    residual, corner_second = kernel_call(
        "final",
        final_body,
        (cell(whole.shape, jnp.float32), cell(head.shape, kind)),
        [VMEM] * 3 + [HBM],
        [HBM, HBM],
        [pltpu.VMEM(part.shape, jnp.float32), pltpu.VMEM(head.shape, kind), dma((3,))],
        {3: 0},
    )(rest, side1, second, pltpu.with_memory_space_constraint(residual, pltpu.HBM))
    return west_out, north_out, corner_first, corner_second, residual


def solution(mesh):
    cell = P("gx", "gy")
    return jax.shard_map(
        on_device,
        mesh=mesh,
        in_specs=(P(),) + (cell,) * 8,
        out_specs=(cell,) * 5,
        check_vma=False,
    )
```

time: 92 us -> 88.5 us (0.962)
  starting transfers between devices: 29.6 us -> 25.8 us
  waiting for transfers between devices: 34.4 us -> 36.8 us
  Pallas kernels: 26.3 us -> 24.6 us
    ppermute x4 -> x2, starting transfers between devices: 9.08 us -> 3.76 us  [line(): lax.ppermute(x, axis, [(i, i + distance) for i in range(size) if 0 <= i +...]
    ppermute x21, starting transfers between devices: 15.6 us -> 17.3 us  [ring(): lax.ppermute(x, axis, [(i, (i + distance) % size) for i in range(size)])]
    pallas_call x5, Pallas kernels: 8.96 us -> 7.26 us  [the longest x1 3.11 us: on_device(): kernel_call('first', first_body, (part, part, maps, info), [HBM] * 7, [VM...]
    ppermute x1, waiting for transfers between devices: 3.42 us -> 4.63 us  [on_device(): side0 = lax.ppermute(total, 'gx', pairs)]
    ppermute x1, starting transfers between devices: 2.24 us -> 1.14 us  [on_device(): side0 = lax.ppermute(total, 'gx', pairs)]
    ppermute x2 -> x4, starting transfers between devices: 2.58 us -> 2.68 us  [the longest x2 2.68 us: on_device(): one[p] = lax.ppermute(first, 'gx', ahead)]
  transfers between devices with their start and end apart: 29 -> 29, of which waited for: 18 -> 21; matrix products, arithmetic and copies ran while one was open for 0% -> 0% of each run, Pallas kernels for 23% -> 23%
where the time goes in v2:
time: 88.5 us; the launch traced here: 88.3 us
  waiting for transfers between devices  36.8 us (42%)
  starting transfers between devices  25.8 us (29%)
  Pallas kernels  24.6 us (28%)
  between operations  1.15 us (1%)
    ppermute x21, waiting for transfers between devices, ring(): lax.ppermute(x, axis, [(i, (i + distance) % size) for i in range(size)])  27.2 us
    ppermute x21, starting transfers between devices, ring(): lax.ppermute(x, axis, [(i, (i + distance) % size) for i in range(size)])  17.3 us
    pallas_call x8, Pallas kernels, on_device(): kernel_call('south', functools.partial(south_body, corner_width), part, [...  5.72 us
    pallas_call x6, Pallas kernels, on_device(): kernel_call('east', functools.partial(east_plain_body, tick, p), (part, p...  5.13 us
    ppermute x1, waiting for transfers between devices, on_device(): side0 = lax.ppermute(total, 'gx', pairs)  4.63 us
    ppermute x2, starting transfers between devices, line(): lax.ppermute(x, axis, [(i, i + distance) for i in range(size) if 0 <= i +...  3.76 us
    ppermute x1, waiting for transfers between devices, on_device(): side1 = lax.ppermute(total, 'gx', pairs)  3.34 us
    pallas_call x1, Pallas kernels, on_device(): kernel_call('first', first_body, (part, part, maps, info), [HBM] * 7, [VM...  3.11 us
  transfers between devices with their start and end apart: 29, of which 21 were waited for; matrix products, arithmetic and copies ran while one was open for 0% of the time, Pallas kernels for 23%

profile of v2, /device:TPU:0, one launch (start us, length us, event | category | flops | bytes accessed | tf_op | source)
XLA Modules:
  0.0 88.3 jit_solution(2201599859445350988)
XLA Ops:
  0.6 3.1 %first.1 = (bf16[2,64,1024]{2,1,0:T(8,128)(2,1)S(1)}, bf16[2,64,1024]{2,1,0:T(8,128)(2,1)S(1)}, bf16[2,1024,1024]{2,1,0:T(8,128)(2,1)S(1)}, f32[128,128]{1,0:T(8,128)S(1)}) custom-call(s32[16]{0:T(128)} %plan.1, f32[1,1,16,2,128]{4,3,2,1,0:T(2,128)} %amplitude.1, s32[1,1,16,128]{3,2,1,0:T(8,128)} %positions.1, bf16[1,1,2,128,1024]{4,3,2,1,0:T(8,128)(2,1)} %west.3, ...), custom_call_target="tpu_custom_call" | custom-call | flops 1000 | bytes 1000 | tf_op jit(solution)/shard_map/first/pallas_call | solution.py:323
  3.8 3.0 %collective-permute-start.2 = (bf16[2,64,1024]{2,1,0:T(8,128)(2,1)S(1)}, bf16[2,64,1024]{2,1,0:T(8,128)(2,1)S(1)}, u32[]{:S(2)}, u32[]{:S(2)}) collective-permute-start(bf16[2,64,1024]{2,1,0:T(8,128)(2,1)S(1)} %get-tuple-element.46.turn), channel_id=1, source_target_pairs={{0,8},{8,16},{16,24},{24,0},{1,9},{9,17},{17,25},{25,1},{2,10},{10... | collective-permute-start | bytes 786440 | tf_op jit(solution)/shard_map/ppermute | solution.py:40
  6.7 1.2 %first_south.1 = (bf16[2,64,1024]{2,1,0:T(8,128)(2,1)S(1)}, bf16[2,64,1024]{2,1,0:T(8,128)(2,1)S(1)}) custom-call(bf16[2,64,1024]{2,1,0:T(8,128)(2,1)S(1)} %get-tuple-element.44.q, f32[128,128]{1,0:T(8,128)S(1)} %get-tuple-element.45.info, bf16[1,1,2,128,1024]{4,3,2,1,0:T(8,128)(2,1)} %west.3, bf16[1,1,2,128,1024]{4,3,2,1,0:T(8,128)(2,1)} %north.3, ...), custom_call_target="tpu_custom_call" | custom-call | flops 10000000000 | bytes 1000 | tf_op jit(solution)/shard_map/first_south/pallas_call | solution.py:342
  8.8 1.5 %collective-permute-start = (bf16[2,64,1024]{2,1,0:T(8,128)(2,1)S(1)}, bf16[2,64,1024]{2,1,0:T(8,128)(2,1)S(1)}, u32[]{:S(2)}, u32[]{:S(2)}) collective-permute-start(bf16[2,64,1024]{2,1,0:T(8,128)(2,1)S(1)} %east.9.turn), channel_id=1, source_target_pairs={{0,8},{8,16},{16,24},{24,0},{1,9},{9,17},{17,25},{25,1},{2,10},{10... | collective-permute-start | bytes 786440 | tf_op jit(solution)/shard_map/ppermute | solution.py:40
  11.1 1.5 %collective-permute-start.1 = (bf16[2,64,1024]{2,1,0:T(8,128)(2,1)S(1)}, bf16[2,64,1024]{2,1,0:T(8,128)(2,1)S(1)}, u32[]{:S(2)}, u32[]{:S(2)}) collective-permute-start(bf16[2,64,1024]{2,1,0:T(8,128)(2,1)S(1)} %south.9.turn), channel_id=1, source_target_pairs={{0,1},{1,2},{2,3},{3,4},{4,5},{5,6},{6,7},{7,0},{8,9},{9,10},{10,1... | collective-permute-start | bytes 786440 | tf_op jit(solution)/shard_map/ppermute | solution.py:40
  12.5 3.1 %collective-permute-done.3.n = bf16[2,64,1024]{2,1,0:T(8,128)(2,1)S(1)} collective-permute-done((bf16[2,64,1024]{2,1,0:T(8,128)(2,1)S(1)}, bf16[2,64,1024]{2,1,0:T(8,128)(2,1)S(1)}, u32[]{:S(2)}, u32[]{:S(2)}) %collective-permute-start.3) | collective-permute-done | bytes 262176 | tf_op jit(solution)/shard_map/ppermute | solution.py:40
  16.5 1.5 %collective-permute-start.6 = (bf16[2,64,1024]{2,1,0:T(8,128)(2,1)S(1)}, bf16[2,64,1024]{2,1,0:T(8,128)(2,1)S(1)}, u32[]{:S(2)}, u32[]{:S(2)}) collective-permute-start(bf16[2,64,1024]{2,1,0:T(8,128)(2,1)S(1)} %get-tuple-element.51.turn), channel_id=1, source_target_pairs={{0,8},{8,16},{16,24},{24,0},{1,9},{9,17},{17,25},{25,1},{2,10},{10... | collective-permute-start | bytes 786440 | tf_op jit(solution)/shard_map/ppermute | solution.py:40
  20.4 1.0 %collective-permute-start.4 = (bf16[2,64,1024]{2,1,0:T(8,128)(2,1)S(1)}, bf16[2,64,1024]{2,1,0:T(8,128)(2,1)S(1)}, u32[]{:S(2)}, u32[]{:S(2)}) collective-permute-start(bf16[2,64,1024]{2,1,0:T(8,128)(2,1)S(1)} %get-tuple-element.52.turn), channel_id=1, source_target_pairs={{0,8},{8,16},{16,24},{24,0},{1,9},{9,17},{17,25},{25,1},{2,10},{10... | collective-permute-start | bytes 786440 | tf_op jit(solution)/shard_map/ppermute | solution.py:40
  22.2 4.2 %collective-permute-done.7.n = bf16[2,64,1024]{2,1,0:T(8,128)(2,1)S(1)} collective-permute-done((bf16[2,64,1024]{2,1,0:T(8,128)(2,1)S(1)}, bf16[2,64,1024]{2,1,0:T(8,128)(2,1)S(1)}, u32[]{:S(2)}, u32[]{:S(2)}) %collective-permute-start.7) | collective-permute-done | bytes 262176 | tf_op jit(solution)/shard_map/ppermute | solution.py:40
  27.3 1.5 %collective-permute-start.10 = (bf16[2,64,1024]{2,1,0:T(8,128)(2,1)S(1)}, bf16[2,64,1024]{2,1,0:T(8,128)(2,1)S(1)}, u32[]{:S(2)}, u32[]{:S(2)}) collective-permute-start(bf16[2,64,1024]{2,1,0:T(8,128)(2,1)S(1)} %get-tuple-element.55.turn), channel_id=1, source_target_pairs={{0,8},{8,16},{16,24},{24,0},{1,9},{9,17},{17,25},{25,1},{2,10},{10... | collective-permute-start | bytes 786440 | tf_op jit(solution)/shard_map/ppermute | solution.py:40
  29.8 2.1 %collective-permute-done.4.w = bf16[2,64,1024]{2,1,0:T(8,128)(2,1)S(1)} collective-permute-done((bf16[2,64,1024]{2,1,0:T(8,128)(2,1)S(1)}, bf16[2,64,1024]{2,1,0:T(8,128)(2,1)S(1)}, u32[]{:S(2)}, u32[]{:S(2)}) %collective-permute-start.4) | collective-permute-done | bytes 262176 | tf_op jit(solution)/shard_map/ppermute | solution.py:40
  34.6 2.6 %collective-permute-done.11.n = bf16[2,64,1024]{2,1,0:T(8,128)(2,1)S(1)} collective-permute-done((bf16[2,64,1024]{2,1,0:T(8,128)(2,1)S(1)}, bf16[2,64,1024]{2,1,0:T(8,128)(2,1)S(1)}, u32[]{:S(2)}, u32[]{:S(2)}) %collective-permute-start.11) | collective-permute-done | bytes 262176 | tf_op jit(solution)/shard_map/ppermute | solution.py:40
  38.4 1.3 %collective-permute-start.14 = (bf16[2,64,1024]{2,1,0:T(8,128)(2,1)S(1)}, bf16[2,64,1024]{2,1,0:T(8,128)(2,1)S(1)}, u32[]{:S(2)}, u32[]{:S(2)}) collective-permute-start(bf16[2,64,1024]{2,1,0:T(8,128)(2,1)S(1)} %get-tuple-element.59.turn), channel_id=1, source_target_pairs={{0,8},{8,16},{16,24},{24,0},{1,9},{9,17},{17,25},{25,1},{2,10},{10... | collective-permute-start | bytes 786440 | tf_op jit(solution)/shard_map/ppermute | solution.py:40
  40.6 1.6 %collective-permute-done.9.n = bf16[2,64,1024]{2,1,0:T(8,128)(2,1)S(1)} collective-permute-done((bf16[2,64,1024]{2,1,0:T(8,128)(2,1)S(1)}, bf16[2,64,1024]{2,1,0:T(8,128)(2,1)S(1)}, u32[]{:S(2)}, u32[]{:S(2)}) %collective-permute-start.9) | collective-permute-done | bytes 262176 | tf_op jit(solution)/shard_map/ppermute | solution.py:40
  44.1 1.5 %collective-permute-start.12 = (bf16[2,64,1024]{2,1,0:T(8,128)(2,1)S(1)}, bf16[2,64,1024]{2,1,0:T(8,128)(2,1)S(1)}, u32[]{:S(2)}, u32[]{:S(2)}) collective-permute-start(bf16[2,64,1024]{2,1,0:T(8,128)(2,1)S(1)} %get-tuple-element.60.turn), channel_id=1, source_target_pairs={{0,8},{8,16},{16,24},{24,0},{1,9},{9,17},{17,25},{25,1},{2,10},{10... | collective-permute-start | bytes 786440 | tf_op jit(solution)/shard_map/ppermute | solution.py:40
  46.4 1.8 %collective-permute-done.15.n = bf16[2,64,1024]{2,1,0:T(8,128)(2,1)S(1)} collective-permute-done((bf16[2,64,1024]{2,1,0:T(8,128)(2,1)S(1)}, bf16[2,64,1024]{2,1,0:T(8,128)(2,1)S(1)}, u32[]{:S(2)}, u32[]{:S(2)}) %collective-permute-start.15) | collective-permute-done | bytes 262176 | tf_op jit(solution)/shard_map/ppermute | solution.py:40
  49.7 1.3 %collective-permute-start.18 = (bf16[2,64,1024]{2,1,0:T(8,128)(2,1)S(1)}, bf16[2,64,1024]{2,1,0:T(8,128)(2,1)S(1)}, u32[]{:S(2)}, u32[]{:S(2)}) collective-permute-start(bf16[2,64,1024]{2,1,0:T(8,128)(2,1)S(1)} %get-tuple-element.63.turn), channel_id=1, source_target_pairs={{0,8},{8,16},{16,24},{24,0},{1,9},{9,17},{17,25},{25,1},{2,10},{10... | collective-permute-start | bytes 786440 | tf_op jit(solution)/shard_map/ppermute | solution.py:40
  51.8 2.1 %collective-permute-done.13.n = bf16[2,64,1024]{2,1,0:T(8,128)(2,1)S(1)} collective-permute-done((bf16[2,64,1024]{2,1,0:T(8,128)(2,1)S(1)}, bf16[2,64,1024]{2,1,0:T(8,128)(2,1)S(1)}, u32[]{:S(2)}, u32[]{:S(2)}) %collective-permute-start.13) | collective-permute-done | bytes 262176 | tf_op jit(solution)/shard_map/ppermute | solution.py:40
  55.3 1.5 %collective-permute-start.16 = (bf16[2,64,1024]{2,1,0:T(8,128)(2,1)S(1)}, bf16[2,64,1024]{2,1,0:T(8,128)(2,1)S(1)}, u32[]{:S(2)}, u32[]{:S(2)}) collective-permute-start(bf16[2,64,1024]{2,1,0:T(8,128)(2,1)S(1)} %get-tuple-element.64.turn), channel_id=1, source_target_pairs={{0,8},{8,16},{16,24},{24,0},{1,9},{9,17},{17,25},{25,1},{2,10},{10... | collective-permute-start | bytes 786440 | tf_op jit(solution)/shard_map/ppermute | solution.py:40
  57.6 1.8 %collective-permute-done.19.n = bf16[2,64,1024]{2,1,0:T(8,128)(2,1)S(1)} collective-permute-done((bf16[2,64,1024]{2,1,0:T(8,128)(2,1)S(1)}, bf16[2,64,1024]{2,1,0:T(8,128)(2,1)S(1)}, u32[]{:S(2)}, u32[]{:S(2)}) %collective-permute-start.19) | collective-permute-done | bytes 262176 | tf_op jit(solution)/shard_map/ppermute | solution.py:40
  60.9 1.3 %collective-permute-start.20 = (bf16[2,64,1024]{2,1,0:T(8,128)(2,1)S(1)}, bf16[2,64,1024]{2,1,0:T(8,128)(2,1)S(1)}, u32[]{:S(2)}, u32[]{:S(2)}) collective-permute-start(bf16[2,64,1024]{2,1,0:T(8,128)(2,1)S(1)} %get-tuple-element.68), channel_id=1, source_target_pairs={{0,8},{24,16},{8,24},{16,0},{1,9},{25,17},{9,25},{17,1},{2,10},{26... | collective-permute-start | bytes 786440 | tf_op jit(solution)/shard_map/ppermute | solution.py:387
  62.3 2.9 %collective-permute-done.17.n = bf16[2,64,1024]{2,1,0:T(8,128)(2,1)S(1)} collective-permute-done((bf16[2,64,1024]{2,1,0:T(8,128)(2,1)S(1)}, bf16[2,64,1024]{2,1,0:T(8,128)(2,1)S(1)}, u32[]{:S(2)}, u32[]{:S(2)}) %collective-permute-start.17) | collective-permute-done | bytes 262176 | tf_op jit(solution)/shard_map/ppermute | solution.py:40
  66.5 1.3 %collective-permute-start.21 = (bf16[2,64,1024]{2,1,0:T(8,128)(2,1)S(1)}, bf16[2,64,1024]{2,1,0:T(8,128)(2,1)S(1)}, u32[]{:S(2)}, u32[]{:S(2)}) collective-permute-start(bf16[2,64,1024]{2,1,0:T(8,128)(2,1)S(1)} %get-tuple-element.69), channel_id=1, source_target_pairs={{0,8},{24,16},{8,24},{16,0},{1,9},{25,17},{9,25},{17,1},{2,10},{26... | collective-permute-start | bytes 786440 | tf_op jit(solution)/shard_map/ppermute | solution.py:387
  67.9 1.3 %last_south.1.turn = bf16[2,128,2176]{2,1,0:T(8,128)(2,1)S(1)} custom-call(bf16[2,64,1024]{2,1,0:T(8,128)(2,1)S(1)} %get-tuple-element.71.q0, bf16[2,64,1024]{2,1,0:T(8,128)(2,1)S(1)} %get-tuple-element.67.q1.q, bf16[2,1024,1024]{2,1,0:T(8,128)(2,1)S(1)} %bitcast.11, bf16[2,64,1024]{2,1,0:T(8,128)(2,1)S(1)} %collective-permute-done.18.w.w0, ...), custom_call_target="tpu_custom_call" | custom-call | flops 1000 | bytes 1000 | tf_op jit(solution)/shard_map/last_south/pallas_call | solution.py:392
  69.2 2.5 %collective-permute-start.24 = (bf16[2,128,2176]{2,1,0:T(8,128)(2,1)S(1)}, bf16[2,128,2176]{2,1,0:T(8,128)(2,1)S(1)}, u32[]{:S(2)}, u32[]{:S(2)}) collective-permute-start(bf16[2,128,2176]{2,1,0:T(8,128)(2,1)S(1)} %last_south.1.turn), channel_id=1, source_target_pairs={{0,1},{1,2},{2,3},{3,4},{4,5},{5,6},{6,7},{8,9},{9,10},{10,11},{11... | collective-permute-start | bytes 3342344 | tf_op jit(solution)/shard_map/ppermute | solution.py:45
  71.8 1.1 %collective-permute-start.26 = (bf16[2,64,1024]{2,1,0:T(8,128)(2,1)S(1)}, bf16[2,64,1024]{2,1,0:T(8,128)(2,1)S(1)}, u32[]{:S(2)}, u32[]{:S(2)}) collective-permute-start(bf16[2,64,1024]{2,1,0:T(8,128)(2,1)S(1)} %get-tuple-element.72.turn), channel_id=1, source_target_pairs={{0,8},{8,0},{16,24},{24,16},{1,9},{9,1},{17,25},{25,17},{2,10},{10... | collective-permute-start | bytes 786440 | tf_op jit(solution)/shard_map/ppermute | solution.py:399
  72.9 1.3 %collective-permute-start.25 = (bf16[2,128,1024]{2,1,0:T(8,128)(2,1)S(1)}, bf16[2,128,1024]{2,1,0:T(8,128)(2,1)S(1)}, u32[]{:S(2)}, u32[]{:S(2)}) collective-permute-start(bf16[2,128,1024]{2,1,0:T(8,128)(2,1)S(1)} %get-tuple-element.74.q), channel_id=1, source_target_pairs={{1,0},{2,1},{3,2},{4,3},{5,4},{6,5},{7,6},{9,8},{10,9},{11,10},{12... | collective-permute-start | bytes 1572872 | tf_op jit(solution)/shard_map/ppermute | solution.py:45
  74.2 1.6 %collective-permute-done.21.first1 = bf16[2,64,1024]{2,1,0:T(8,128)(2,1)S(1)} collective-permute-done((bf16[2,64,1024]{2,1,0:T(8,128)(2,1)S(1)}, bf16[2,64,1024]{2,1,0:T(8,128)(2,1)S(1)}, u32[]{:S(2)}, u32[]{:S(2)}) %collective-permute-start.21) | collective-permute-done | bytes 262176 | tf_op jit(solution)/shard_map/ppermute | solution.py:387
  75.8 1.1 %middle1.1 = (bf16[2,64,1024]{2,1,0:T(8,128)(2,1)S(1)}, bf16[1,1,2,128,1024]{4,3,2,1,0:T(8,128)(2,1)}, bf16[2,128,128]{2,1,0:T(8,128)(2,1)S(1)}) custom-call(bf16[2,64,1024]{2,1,0:T(8,128)(2,1)S(1)} %get-tuple-element.67.q1.q, bf16[2,64,1024]{2,1,0:T(8,128)(2,1)S(1)} %collective-permute-done.20.far.first0, ...), custom_call_target="tpu_custom_call" | custom-call | flops 10000000000 | bytes 1000 | tf_op jit(solution)/shard_map/middle1/pallas_call | solution.py:401
  77.8 4.6 %collective-permute-done.26.side = bf16[2,64,1024]{2,1,0:T(8,128)(2,1)S(1)} collective-permute-done((bf16[2,64,1024]{2,1,0:T(8,128)(2,1)S(1)}, bf16[2,64,1024]{2,1,0:T(8,128)(2,1)S(1)}, u32[]{:S(2)}, u32[]{:S(2)}) %collective-permute-start.26) | collective-permute-done | bytes 262176 | tf_op jit(solution)/shard_map/ppermute | solution.py:399
  82.4 1.2 %base.1 = (f32[2,64,1024]{2,1,0:T(8,128)S(1)}, bf16[1,1,2,128,128]{4,3,2,1,0:T(8,128)(2,1)}, bf16[1,1,2,128,1024]{4,3,2,1,0:T(8,128)(2,1)}, f32[1,1,2,128,1024]{4,3,2,1,0:T(8,128)}) custom-call(bf16[2,128,1024]{2,1,0:T(8,128)(2,1)S(1)} %get-tuple-element.74.q, bf16[2,128,2176]{2,1,0:T(8,128)(2,1)S(1)} %collective-permute-done.24.tray, ...), custom_call_target="tpu_custom_call" | custom-call | flops 1000 | bytes 1000 | tf_op jit(solution)/shard_map/base/pallas_call | solution.py:412
  84.0 3.3 %collective-permute-done.27.side = bf16[2,64,1024]{2,1,0:T(8,128)(2,1)S(1)} collective-permute-done((bf16[2,64,1024]{2,1,0:T(8,128)(2,1)S(1)}, bf16[2,64,1024]{2,1,0:T(8,128)(2,1)S(1)}, u32[]{:S(2)}, u32[]{:S(2)}) %collective-permute-start.27) | collective-permute-done | bytes 262176 | tf_op jit(solution)/shard_map/ppermute | solution.py:409
  (57 shorter events, 24.0 us)
Async XLA Ops:
  0.6 6.1 %copy-start = (bf16[1,1,2,1024,1024]{4,3,2,1,0:T(8,128)(2,1)S(1)}, bf16[1,1,2,1024,1024]{4,3,2,1,0:T(8,128)(2,1)}, u32[]{:S(2)}) copy-start(bf16[1,1,2,1024,1024]{4,3,2,1,0:T(8,128)(2,1)} %param.17) | copy-start | bytes 12582916
  3.8 11.9 %collective-permute-start.2 = (bf16[2,64,1024]{2,1,0:T(8,128)(2,1)S(1)}, bf16[2,64,1024]{2,1,0:T(8,128)(2,1)S(1)}, u32[]{:S(2)}, u32[]{:S(2)}) collective-permute-start(bf16[2,64,1024]{2,1,0:T(8,128)(2,1)S(1)} %get-tuple-element.46.turn), channel_id=1, source_target_pairs={{0,8},{8,16},{16,24},{24,0},{1,9},{9,17},{17,25},{25,1},{2,10},{10... | collective-permute-start | bytes 786440 | tf_op jit(solution)/shard_map/ppermute | solution.py:40
  8.0 7.6 %collective-permute-start.3 = (bf16[2,64,1024]{2,1,0:T(8,128)(2,1)S(1)}, bf16[2,64,1024]{2,1,0:T(8,128)(2,1)S(1)}, u32[]{:S(2)}, u32[]{:S(2)}) collective-permute-start(bf16[2,64,1024]{2,1,0:T(8,128)(2,1)S(1)} %get-tuple-element.49.turn), channel_id=1, source_target_pairs={{0,1},{1,2},{2,3},{3,4},{4,5},{5,6},{6,7},{7,0},{8,9},{9,10},{10,1... | collective-permute-start | bytes 786440 | tf_op jit(solution)/shard_map/ppermute | solution.py:40
  8.8 6.9 %copy-start.1 = (bf16[1,1,2,128,128]{4,3,2,1,0:T(8,128)(2,1)S(1)}, bf16[1,1,2,128,128]{4,3,2,1,0:T(8,128)(2,1)}, u32[]{:S(2)}) copy-start(bf16[1,1,2,128,128]{4,3,2,1,0:T(8,128)(2,1)} %corner.7) | copy-start | bytes 196612
  8.8 10.7 %collective-permute-start = (bf16[2,64,1024]{2,1,0:T(8,128)(2,1)S(1)}, bf16[2,64,1024]{2,1,0:T(8,128)(2,1)S(1)}, u32[]{:S(2)}, u32[]{:S(2)}) collective-permute-start(bf16[2,64,1024]{2,1,0:T(8,128)(2,1)S(1)} %east.9.turn), channel_id=1, source_target_pairs={{0,8},{8,16},{16,24},{24,0},{1,9},{9,17},{17,25},{25,1},{2,10},{10... | collective-permute-start | bytes 786440 | tf_op jit(solution)/shard_map/ppermute | solution.py:40
  11.1 7.8 %collective-permute-start.1 = (bf16[2,64,1024]{2,1,0:T(8,128)(2,1)S(1)}, bf16[2,64,1024]{2,1,0:T(8,128)(2,1)S(1)}, u32[]{:S(2)}, u32[]{:S(2)}) collective-permute-start(bf16[2,64,1024]{2,1,0:T(8,128)(2,1)S(1)} %south.9.turn), channel_id=1, source_target_pairs={{0,1},{1,2},{2,3},{3,4},{4,5},{5,6},{6,7},{7,0},{8,9},{9,10},{10,1... | collective-permute-start | bytes 786440 | tf_op jit(solution)/shard_map/ppermute | solution.py:40
  16.5 9.9 %collective-permute-start.6 = (bf16[2,64,1024]{2,1,0:T(8,128)(2,1)S(1)}, bf16[2,64,1024]{2,1,0:T(8,128)(2,1)S(1)}, u32[]{:S(2)}, u32[]{:S(2)}) collective-permute-start(bf16[2,64,1024]{2,1,0:T(8,128)(2,1)S(1)} %get-tuple-element.51.turn), channel_id=1, source_target_pairs={{0,8},{8,16},{16,24},{24,0},{1,9},{9,17},{17,25},{25,1},{2,10},{10... | collective-permute-start | bytes 786440 | tf_op jit(solution)/shard_map/ppermute | solution.py:40
  18.8 7.6 %collective-permute-start.7 = (bf16[2,64,1024]{2,1,0:T(8,128)(2,1)S(1)}, bf16[2,64,1024]{2,1,0:T(8,128)(2,1)S(1)}, u32[]{:S(2)}, u32[]{:S(2)}) collective-permute-start(bf16[2,64,1024]{2,1,0:T(8,128)(2,1)S(1)} %south.10.turn), channel_id=1, source_target_pairs={{0,1},{1,2},{2,3},{3,4},{4,5},{5,6},{6,7},{7,0},{8,9},{9,10},{10,1... | collective-permute-start | bytes 786440 | tf_op jit(solution)/shard_map/ppermute | solution.py:40
  20.4 11.6 %collective-permute-start.4 = (bf16[2,64,1024]{2,1,0:T(8,128)(2,1)S(1)}, bf16[2,64,1024]{2,1,0:T(8,128)(2,1)S(1)}, u32[]{:S(2)}, u32[]{:S(2)}) collective-permute-start(bf16[2,64,1024]{2,1,0:T(8,128)(2,1)S(1)} %get-tuple-element.52.turn), channel_id=1, source_target_pairs={{0,8},{8,16},{16,24},{24,0},{1,9},{9,17},{17,25},{25,1},{2,10},{10... | collective-permute-start | bytes 786440 | tf_op jit(solution)/shard_map/ppermute | solution.py:40
  22.2 7.6 %collective-permute-start.5 = (bf16[2,64,1024]{2,1,0:T(8,128)(2,1)S(1)}, bf16[2,64,1024]{2,1,0:T(8,128)(2,1)S(1)}, u32[]{:S(2)}, u32[]{:S(2)}) collective-permute-start(bf16[2,64,1024]{2,1,0:T(8,128)(2,1)S(1)} %south.11.turn), channel_id=1, source_target_pairs={{0,1},{1,2},{2,3},{3,4},{4,5},{5,6},{6,7},{7,0},{8,9},{9,10},{10,1... | collective-permute-start | bytes 786440 | tf_op jit(solution)/shard_map/ppermute | solution.py:40
  27.3 10.3 %collective-permute-start.10 = (bf16[2,64,1024]{2,1,0:T(8,128)(2,1)S(1)}, bf16[2,64,1024]{2,1,0:T(8,128)(2,1)S(1)}, u32[]{:S(2)}, u32[]{:S(2)}) collective-permute-start(bf16[2,64,1024]{2,1,0:T(8,128)(2,1)S(1)} %get-tuple-element.55.turn), channel_id=1, source_target_pairs={{0,8},{8,16},{16,24},{24,0},{1,9},{9,17},{17,25},{25,1},{2,10},{10... | collective-permute-start | bytes 786440 | tf_op jit(solution)/shard_map/ppermute | solution.py:40
  29.6 7.6 %collective-permute-start.11 = (bf16[2,64,1024]{2,1,0:T(8,128)(2,1)S(1)}, bf16[2,64,1024]{2,1,0:T(8,128)(2,1)S(1)}, u32[]{:S(2)}, u32[]{:S(2)}) collective-permute-start(bf16[2,64,1024]{2,1,0:T(8,128)(2,1)S(1)} %south.12.turn), channel_id=1, source_target_pairs={{0,1},{1,2},{2,3},{3,4},{4,5},{5,6},{6,7},{7,0},{8,9},{9,10},{10,1... | collective-permute-start | bytes 786440 | tf_op jit(solution)/shard_map/ppermute | solution.py:40
  32.8 10.4 %collective-permute-start.8 = (bf16[2,64,1024]{2,1,0:T(8,128)(2,1)S(1)}, bf16[2,64,1024]{2,1,0:T(8,128)(2,1)S(1)}, u32[]{:S(2)}, u32[]{:S(2)}) collective-permute-start(bf16[2,64,1024]{2,1,0:T(8,128)(2,1)S(1)} %get-tuple-element.56.turn), channel_id=1, source_target_pairs={{0,8},{8,16},{16,24},{24,0},{1,9},{9,17},{17,25},{25,1},{2,10},{10... | collective-permute-start | bytes 786440 | tf_op jit(solution)/shard_map/ppermute | solution.py:40
  34.6 7.6 %collective-permute-start.9 = (bf16[2,64,1024]{2,1,0:T(8,128)(2,1)S(1)}, bf16[2,64,1024]{2,1,0:T(8,128)(2,1)S(1)}, u32[]{:S(2)}, u32[]{:S(2)}) collective-permute-start(bf16[2,64,1024]{2,1,0:T(8,128)(2,1)S(1)} %south.13.turn), channel_id=1, source_target_pairs={{0,1},{1,2},{2,3},{3,4},{4,5},{5,6},{6,7},{7,0},{8,9},{9,10},{10,1... | collective-permute-start | bytes 786440 | tf_op jit(solution)/shard_map/ppermute | solution.py:40
  38.4 10.4 %collective-permute-start.14 = (bf16[2,64,1024]{2,1,0:T(8,128)(2,1)S(1)}, bf16[2,64,1024]{2,1,0:T(8,128)(2,1)S(1)}, u32[]{:S(2)}, u32[]{:S(2)}) collective-permute-start(bf16[2,64,1024]{2,1,0:T(8,128)(2,1)S(1)} %get-tuple-element.59.turn), channel_id=1, source_target_pairs={{0,8},{8,16},{16,24},{24,0},{1,9},{9,17},{17,25},{25,1},{2,10},{10... | collective-permute-start | bytes 786440 | tf_op jit(solution)/shard_map/ppermute | solution.py:40
  40.5 7.6 %collective-permute-start.15 = (bf16[2,64,1024]{2,1,0:T(8,128)(2,1)S(1)}, bf16[2,64,1024]{2,1,0:T(8,128)(2,1)S(1)}, u32[]{:S(2)}, u32[]{:S(2)}) collective-permute-start(bf16[2,64,1024]{2,1,0:T(8,128)(2,1)S(1)} %south.14.turn), channel_id=1, source_target_pairs={{0,1},{1,2},{2,3},{3,4},{4,5},{5,6},{6,7},{7,0},{8,9},{9,10},{10,1... | collective-permute-start | bytes 786440 | tf_op jit(solution)/shard_map/ppermute | solution.py:40
  44.1 10.4 %collective-permute-start.12 = (bf16[2,64,1024]{2,1,0:T(8,128)(2,1)S(1)}, bf16[2,64,1024]{2,1,0:T(8,128)(2,1)S(1)}, u32[]{:S(2)}, u32[]{:S(2)}) collective-permute-start(bf16[2,64,1024]{2,1,0:T(8,128)(2,1)S(1)} %get-tuple-element.60.turn), channel_id=1, source_target_pairs={{0,8},{8,16},{16,24},{24,0},{1,9},{9,17},{17,25},{25,1},{2,10},{10... | collective-permute-start | bytes 786440 | tf_op jit(solution)/shard_map/ppermute | solution.py:40
  46.3 7.6 %collective-permute-start.13 = (bf16[2,64,1024]{2,1,0:T(8,128)(2,1)S(1)}, bf16[2,64,1024]{2,1,0:T(8,128)(2,1)S(1)}, u32[]{:S(2)}, u32[]{:S(2)}) collective-permute-start(bf16[2,64,1024]{2,1,0:T(8,128)(2,1)S(1)} %south.15.turn), channel_id=1, source_target_pairs={{0,1},{1,2},{2,3},{3,4},{4,5},{5,6},{6,7},{7,0},{8,9},{9,10},{10,1... | collective-permute-start | bytes 786440 | tf_op jit(solution)/shard_map/ppermute | solution.py:40
  49.7 10.4 %collective-permute-start.18 = (bf16[2,64,1024]{2,1,0:T(8,128)(2,1)S(1)}, bf16[2,64,1024]{2,1,0:T(8,128)(2,1)S(1)}, u32[]{:S(2)}, u32[]{:S(2)}) collective-permute-start(bf16[2,64,1024]{2,1,0:T(8,128)(2,1)S(1)} %get-tuple-element.63.turn), channel_id=1, source_target_pairs={{0,8},{8,16},{16,24},{24,0},{1,9},{9,17},{17,25},{25,1},{2,10},{10... | collective-permute-start | bytes 786440 | tf_op jit(solution)/shard_map/ppermute | solution.py:40
  51.7 7.6 %collective-permute-start.19 = (bf16[2,64,1024]{2,1,0:T(8,128)(2,1)S(1)}, bf16[2,64,1024]{2,1,0:T(8,128)(2,1)S(1)}, u32[]{:S(2)}, u32[]{:S(2)}) collective-permute-start(bf16[2,64,1024]{2,1,0:T(8,128)(2,1)S(1)} %south.16.turn), channel_id=1, source_target_pairs={{0,1},{1,2},{2,3},{3,4},{4,5},{5,6},{6,7},{7,0},{8,9},{9,10},{10,1... | collective-permute-start | bytes 786440 | tf_op jit(solution)/shard_map/ppermute | solution.py:40
  55.3 10.4 %collective-permute-start.16 = (bf16[2,64,1024]{2,1,0:T(8,128)(2,1)S(1)}, bf16[2,64,1024]{2,1,0:T(8,128)(2,1)S(1)}, u32[]{:S(2)}, u32[]{:S(2)}) collective-permute-start(bf16[2,64,1024]{2,1,0:T(8,128)(2,1)S(1)} %get-tuple-element.64.turn), channel_id=1, source_target_pairs={{0,8},{8,16},{16,24},{24,0},{1,9},{9,17},{17,25},{25,1},{2,10},{10... | collective-permute-start | bytes 786440 | tf_op jit(solution)/shard_map/ppermute | solution.py:40
  57.5 7.6 %collective-permute-start.17 = (bf16[2,64,1024]{2,1,0:T(8,128)(2,1)S(1)}, bf16[2,64,1024]{2,1,0:T(8,128)(2,1)S(1)}, u32[]{:S(2)}, u32[]{:S(2)}) collective-permute-start(bf16[2,64,1024]{2,1,0:T(8,128)(2,1)S(1)} %south.17.turn), channel_id=1, source_target_pairs={{0,1},{1,2},{2,3},{3,4},{4,5},{5,6},{6,7},{7,0},{8,9},{9,10},{10,1... | collective-permute-start | bytes 786440 | tf_op jit(solution)/shard_map/ppermute | solution.py:40
  60.9 10.7 %collective-permute-start.20 = (bf16[2,64,1024]{2,1,0:T(8,128)(2,1)S(1)}, bf16[2,64,1024]{2,1,0:T(8,128)(2,1)S(1)}, u32[]{:S(2)}, u32[]{:S(2)}) collective-permute-start(bf16[2,64,1024]{2,1,0:T(8,128)(2,1)S(1)} %get-tuple-element.68), channel_id=1, source_target_pairs={{0,8},{24,16},{8,24},{16,0},{1,9},{25,17},{9,25},{17,1},{2,10},{26... | collective-permute-start | bytes 786440 | tf_op jit(solution)/shard_map/ppermute | solution.py:387
  62.3 9.4 %collective-permute-start.22 = (bf16[2,64,1024]{2,1,0:T(8,128)(2,1)S(1)}, bf16[2,64,1024]{2,1,0:T(8,128)(2,1)S(1)}, u32[]{:S(2)}, u32[]{:S(2)}) collective-permute-start(bf16[2,64,1024]{2,1,0:T(8,128)(2,1)S(1)} %get-tuple-element.66.turn), channel_id=1, source_target_pairs={{0,1},{1,0},{2,3},{3,2},{4,5},{5,4},{6,7},{7,6},{24,8},{25,9},{26,... | collective-permute-start | bytes 786440 | tf_op jit(solution)/shard_map/ppermute | solution.py:388
  66.5 9.3 %collective-permute-start.21 = (bf16[2,64,1024]{2,1,0:T(8,128)(2,1)S(1)}, bf16[2,64,1024]{2,1,0:T(8,128)(2,1)S(1)}, u32[]{:S(2)}, u32[]{:S(2)}) collective-permute-start(bf16[2,64,1024]{2,1,0:T(8,128)(2,1)S(1)} %get-tuple-element.69), channel_id=1, source_target_pairs={{0,8},{24,16},{8,24},{16,0},{1,9},{25,17},{9,25},{17,1},{2,10},{26... | collective-permute-start | bytes 786440 | tf_op jit(solution)/shard_map/ppermute | solution.py:387
  67.9 7.9 %collective-permute-start.23 = (bf16[2,64,1024]{2,1,0:T(8,128)(2,1)S(1)}, bf16[2,64,1024]{2,1,0:T(8,128)(2,1)S(1)}, u32[]{:S(2)}, u32[]{:S(2)}) collective-permute-start(bf16[2,64,1024]{2,1,0:T(8,128)(2,1)S(1)} %get-tuple-element.70.turn), channel_id=1, source_target_pairs={{0,1},{1,0},{2,3},{3,2},{4,5},{5,4},{6,7},{7,6},{24,8},{25,9},{26,... | collective-permute-start | bytes 786440 | tf_op jit(solution)/shard_map/ppermute | solution.py:388
  69.2 13.2 %collective-permute-start.24 = (bf16[2,128,2176]{2,1,0:T(8,128)(2,1)S(1)}, bf16[2,128,2176]{2,1,0:T(8,128)(2,1)S(1)}, u32[]{:S(2)}, u32[]{:S(2)}) collective-permute-start(bf16[2,128,2176]{2,1,0:T(8,128)(2,1)S(1)} %last_south.1.turn), channel_id=1, source_target_pairs={{0,1},{1,2},{2,3},{3,4},{4,5},{5,6},{6,7},{8,9},{9,10},{10,11},{11... | collective-permute-start | bytes 3342344 | tf_op jit(solution)/shard_map/ppermute | solution.py:45
  71.8 10.6 %collective-permute-start.26 = (bf16[2,64,1024]{2,1,0:T(8,128)(2,1)S(1)}, bf16[2,64,1024]{2,1,0:T(8,128)(2,1)S(1)}, u32[]{:S(2)}, u32[]{:S(2)}) collective-permute-start(bf16[2,64,1024]{2,1,0:T(8,128)(2,1)S(1)} %get-tuple-element.72.turn), channel_id=1, source_target_pairs={{0,8},{8,0},{16,24},{24,16},{1,9},{9,1},{17,25},{25,17},{2,10},{10... | collective-permute-start | bytes 786440 | tf_op jit(solution)/shard_map/ppermute | solution.py:399
  72.9 9.5 %collective-permute-start.25 = (bf16[2,128,1024]{2,1,0:T(8,128)(2,1)S(1)}, bf16[2,128,1024]{2,1,0:T(8,128)(2,1)S(1)}, u32[]{:S(2)}, u32[]{:S(2)}) collective-permute-start(bf16[2,128,1024]{2,1,0:T(8,128)(2,1)S(1)} %get-tuple-element.74.q), channel_id=1, source_target_pairs={{1,0},{2,1},{3,2},{4,3},{5,4},{6,5},{7,6},{9,8},{10,9},{11,10},{12... | collective-permute-start | bytes 1572872 | tf_op jit(solution)/shard_map/ppermute | solution.py:45
  76.9 10.4 %collective-permute-start.27 = (bf16[2,64,1024]{2,1,0:T(8,128)(2,1)S(1)}, bf16[2,64,1024]{2,1,0:T(8,128)(2,1)S(1)}, u32[]{:S(2)}, u32[]{:S(2)}) collective-permute-start(bf16[2,64,1024]{2,1,0:T(8,128)(2,1)S(1)} %get-tuple-element.75.turn), channel_id=1, source_target_pairs={{0,8},{8,0},{16,24},{24,16},{1,9},{9,1},{17,25},{25,17},{2,10},{10... | collective-permute-start | bytes 786440 | tf_op jit(solution)/shard_map/ppermute | solution.py:409
  77.8 6.2 %collective-permute-start.28 = (bf16[2,128,128]{2,1,0:T(8,128)(2,1)S(1)}, bf16[2,128,128]{2,1,0:T(8,128)(2,1)S(1)}, u32[]{:S(2)}, u32[]{:S(2)}) collective-permute-start(bf16[2,128,128]{2,1,0:T(8,128)(2,1)S(1)} %get-tuple-element.79), channel_id=1, source_target_pairs={{0,1},{1,2},{2,3},{3,4},{4,5},{5,6},{6,7},{7,0},{8,9},{9,10},{10,1... | collective-permute-start | bytes 196616 | tf_op jit(solution)/shard_map/ppermute | solution.py:40

commit v3 on v2

--- a/solution.py
+++ b/solution.py
@@ -10,14 +10,13 @@
 TICKS = 6
 PARTS = 2
 FIELDS = 3
-PIECES = 2
 VMEM = pl.BlockSpec(memory_space=pltpu.VMEM)
 ANY = pl.BlockSpec(memory_space=pl.ANY)
 HBM = pl.BlockSpec(memory_space=pltpu.HBM)
 
 
 COSTS = dict.fromkeys(
-    ("first_south", "east", "south", "last_east0", "last_east1", "middle0", "middle1"), 10**10
+    ("first_south", "east", "south", "last_east0", "early_south", "last_east1", "middle0", "middle1"), 10**10
 )
 
 
@@ -79,14 +78,13 @@
 
 
 def map_copies(source, held, sems):
-    block = held.shape[2] // PIECES
-    copies = []
-    for k in range(PIECES):
-        place = pl.ds(k * block, block)
-        copies.append(
-            pltpu.make_async_copy(source.at[0, 0, :, :, place], held.at[:, :, place], sems.at[k])
-        )
-    return copies
+    block = held.shape[2] // 2
+    left, right = pl.ds(0, block), pl.ds(block, block)
+    places = [(pl.ds(0, 2 * block), left), (pl.ds(0, block), right), (pl.ds(block, block), right)]
+    return [
+        pltpu.make_async_copy(source.at[0, 0, :, rows, cols], held.at[:, rows, cols], sems.at[k])
+        for k, (rows, cols) in enumerate(places)
+    ]
 
 
 def trace_copies(part, step, sources, targets, sems):
@@ -97,16 +95,25 @@
     ]
 
 
-def arriving_product(q, held, copies, out):
-    step, block = q.shape[1], held.shape[2] // PIECES
+def arriving_product(q, held, copies, out, part):
+    step, block = q.shape[1], held.shape[2] // 2
     ahead, turned = stacked(q)
-    for k, copy in enumerate(copies):
-        copy.wait()
-        place = slice(k * block, (k + 1) * block)
-        total = jnp.dot(ahead, held[0, :, place], preferred_element_type=jnp.float32)
-        total = total + jnp.dot(turned, held[1, :, place], preferred_element_type=jnp.float32)
-        out[0, :, place] = total[:step].astype(out.dtype)
-        out[1, :, place] = total[step:].astype(out.dtype)
+
+    def term(rows, cols):
+        total = jnp.dot(ahead[:, rows], held[0, rows, cols], preferred_element_type=jnp.float32)
+        return total + jnp.dot(turned[:, rows], held[1, rows, cols], preferred_element_type=jnp.float32)
+
+    def put(total, cols):
+        out[0, :, cols] = total[:step].astype(out.dtype)
+        out[1, :, cols] = total[step:].astype(out.dtype)
+
+    left, right = slice(0, block), slice(block, 2 * block)
+    copies[0].wait()
+    put(term(slice(0, 2 * block), left), left)
+    copies[1].wait()
+    part[...] = term(left, right)
+    copies[2].wait()
+    put(part[...] + term(right, right), right)
 
 
 def first_boundary(part, info, w, n, c, q):
@@ -122,7 +129,7 @@
 
 def first_body(
     plan, amplitude, positions, west, north, corner, east_map,
-    q, east, held, info, order, amps, places, w, n, c, table, list_sems, trace_sems, map_sems,
+    q, east, held, info, order, amps, places, w, n, c, table, half, list_sems, trace_sems, map_sems,
 ):
     lists = [
         pltpu.make_async_copy(plan, order, list_sems.at[0]),
@@ -147,7 +154,7 @@
     for copy in traces:
         copy.wait()
     first_boundary(0, info, w, n, c, q)
-    arriving_product(q[...], held, blocks, east)
+    arriving_product(q[...], held, blocks, east, half)
 
 
 def first_south_body(q, info, west, north, corner, maps, turn, out, q1, w, n, c, trace_sems):
@@ -215,7 +222,11 @@
         out[half, :, :corner_width] = head.astype(out.dtype)
 
 
-def last_south_body(q0, q1, maps, w0, w1, turn, tray):
+def early_south_body(q, maps, first, turn, out):
+    product_body(q, maps, turn, out)
+
+
+def last_south_body(q0, q1, south0, maps, w0, w1, turn, tray):
     step, width = q0.shape[1:]
     from_west = inside("gx")
     for p, (q, w) in enumerate(((q0, w0), (q1, w1))):
@@ -223,10 +234,10 @@
         tray[:, rows, width : 2 * width] = q[...]
         corner = f32(w[:, :, : tray.shape[2] - 2 * width]) * from_west
         tray[:, rows, 2 * width :] = corner.astype(tray.dtype)
-    total = product(tray[:, :, width : 2 * width], maps)
-    for half in range(2):
-        trace = total[half * 2 * step : (half + 1) * 2 * step]
-        tray[half, :, :width] = trace.astype(tray.dtype)
+    tray[:, :step, :width] = south0[...]
+    total = product(q1[...], maps)
+    for half in range(2):
+        tray[half, step:, :width] = total[half * step : (half + 1) * step].astype(tray.dtype)
 
 
 def has_far():
@@ -265,17 +276,18 @@
             - f32(down[half, rows]) * from_south
         )
 
-    for half in range(2):
-        done[half] = along_y(half, slice(0, step)) - f32(side[half])
-    trace[...] = (f32(tray[:, :, :width]) * from_north).astype(trace.dtype)
-    corner[...] = (f32(tray[:, :, 2 * width :]) * from_north).astype(corner.dtype)
     copies = [
-        pltpu.make_async_copy(done, residual.at[0, 0, :, pl.ds(0, step)], sems.at[0]),
-        pltpu.make_async_copy(trace, out.at[0, 0], sems.at[1]),
+        pltpu.make_async_copy(trace, out.at[0, 0], sems.at[0]),
+        pltpu.make_async_copy(done, residual.at[0, 0, :, pl.ds(0, step)], sems.at[1]),
         pltpu.make_async_copy(corner, first.at[0, 0], sems.at[2]),
     ]
-    for copy in copies:
-        copy.start()
+    trace[...] = (f32(tray[:, :, :width]) * from_north).astype(trace.dtype)
+    copies[0].start()
+    for half in range(2):
+        done[half] = along_y(half, slice(0, step)) - f32(side[half])
+    copies[1].start()
+    corner[...] = (f32(tray[:, :, 2 * width :]) * from_north).astype(corner.dtype)
+    copies[2].start()
     for half in range(2):
         rest[half] = along_y(half, slice(step, 2 * step))
     for copy in copies:
@@ -284,17 +296,18 @@
 
 def final_body(base, side, second, begun, out, corner, rest, held, sems):
     step = side.shape[1]
-    held[...] = (f32(second[...]) * inside("gy")).astype(held.dtype)
-    copies = [pltpu.make_async_copy(held, corner.at[0, 0], sems.at[0])]
-    copies[0].start()
+    copies = []
     for half in range(2):
         rest[half] = base[half] - f32(side[half])
         copies.append(
             pltpu.make_async_copy(
-                rest.at[half], out.at[0, 0, half, pl.ds(step, step)], sems.at[1 + half]
+                rest.at[half], out.at[0, 0, half, pl.ds(step, step)], sems.at[half]
             )
         )
-        copies[-1].start()
+        copies[half].start()
+    held[...] = (f32(second[...]) * inside("gy")).astype(held.dtype)
+    copies.append(pltpu.make_async_copy(held, corner.at[0, 0], sems.at[2]))
+    copies[2].start()
     for copy in copies:
         copy.wait()
 
@@ -332,9 +345,10 @@
             pltpu.VMEM(positions.shape[2:], positions.dtype),
             *bench,
             pltpu.VMEM((sources, sources), jnp.float32),
+            pltpu.VMEM((2 * step, width // 2), jnp.float32),
             dma((3,)),
             dma((3,)),
-            dma((PIECES,)),
+            dma((3,)),
         ],
     )(*fixed[:-1])
     w0 = ring(east, "gx", 1)
@@ -386,11 +400,15 @@
         )(west[p], north[p], info, east_held, turn)
         one[p] = lax.ppermute(first, "gx", ahead)
         two[p] = lax.ppermute(turn, ("gx", "gy"), behind)
+        if p == 0:
+            south0 = turn = kernel_call(
+                "early_south", early_south_body, part, [VMEM, VMEM, ANY, ANY], VMEM
+            )(qs[0], south_held, first, turn)
     cell = lambda shape, dtype: jax.ShapeDtypeStruct((1, 1) + shape, dtype)
     pairs = [(i, i ^ 1) for i in range(columns)]
     tray = jax.ShapeDtypeStruct((2, sources, 2 * width + corner_width), kind)
-    tray = kernel_call("last_south", last_south_body, tray, [VMEM] * 5 + [ANY], VMEM)(
-        qs[0], qs[1], south_held, last_west[0], last_west[1], turn
+    tray = kernel_call("last_south", last_south_body, tray, [VMEM] * 6 + [ANY], VMEM)(
+        qs[0], qs[1], south0, south_held, last_west[0], last_west[1], turn
     )
     total, both = kernel_call(
         "middle0", first_middle_body, (part, whole), [VMEM] * 3 + [ANY] * 2, [VMEM] * 2

time: 88.5 us -> 88.4 us (level)
  transfers between devices with their start and end apart: 29 -> 29, of which waited for: 21 -> 21; matrix products, arithmetic and copies ran while one was open for 0% -> 0% of each run, Pallas kernels for 23% -> 24%
where the time goes in v3:
time: 88.4 us; the launch traced here: 88.2 us
  waiting for transfers between devices  36.5 us (41%)
  starting transfers between devices  25.8 us (29%)
  Pallas kernels  24.7 us (28%)
  between operations  1.16 us (1%)
    ppermute x21, waiting for transfers between devices, ring(): lax.ppermute(x, axis, [(i, (i + distance) % size) for i in range(size)])  26.4 us
    ppermute x21, starting transfers between devices, ring(): lax.ppermute(x, axis, [(i, (i + distance) % size) for i in range(size)])  17.3 us
    pallas_call x8, Pallas kernels, on_device(): kernel_call('south', functools.partial(south_body, corner_width), part, [...  5.73 us
    pallas_call x6, Pallas kernels, on_device(): kernel_call('east', functools.partial(east_plain_body, tick, p), (part, p...  5.13 us
    ppermute x1, waiting for transfers between devices, on_device(): side0 = lax.ppermute(total, 'gx', pairs)  4.9 us
    ppermute x2, starting transfers between devices, line(): lax.ppermute(x, axis, [(i, i + distance) for i in range(size) if 0 <= i +...  3.77 us
    ppermute x1, waiting for transfers between devices, on_device(): side1 = lax.ppermute(total, 'gx', pairs)  3.2 us
    pallas_call x1, Pallas kernels, on_device(): kernel_call('first', first_body, (part, part, maps, info), [HBM] * 7, [VM...  2.99 us
  transfers between devices with their start and end apart: 29, of which 21 were waited for; matrix products, arithmetic and copies ran while one was open for 0% of the time, Pallas kernels for 24%

profile of v3, /device:TPU:0, one launch (start us, length us, event | category | flops | bytes accessed | tf_op | source)
XLA Modules:
  0.0 88.2 jit_solution(16069466129819552283)
XLA Ops:
  0.6 3.0 %first.1 = (bf16[2,64,1024]{2,1,0:T(8,128)(2,1)S(1)}, bf16[2,64,1024]{2,1,0:T(8,128)(2,1)S(1)}, bf16[2,1024,1024]{2,1,0:T(8,128)(2,1)S(1)}, f32[128,128]{1,0:T(8,128)S(1)}) custom-call(s32[16]{0:T(128)} %plan.1, f32[1,1,16,2,128]{4,3,2,1,0:T(2,128)} %amplitude.1, s32[1,1,16,128]{3,2,1,0:T(8,128)} %positions.1, bf16[1,1,2,128,1024]{4,3,2,1,0:T(8,128)(2,1)} %west.3, ...), custom_call_target="tpu_custom_call" | custom-call | flops 1000 | bytes 1000 | tf_op jit(solution)/shard_map/first/pallas_call | solution.py:336
  3.6 3.0 %collective-permute-start.2 = (bf16[2,64,1024]{2,1,0:T(8,128)(2,1)S(1)}, bf16[2,64,1024]{2,1,0:T(8,128)(2,1)S(1)}, u32[]{:S(2)}, u32[]{:S(2)}) collective-permute-start(bf16[2,64,1024]{2,1,0:T(8,128)(2,1)S(1)} %get-tuple-element.46.turn), channel_id=1, source_target_pairs={{0,8},{8,16},{16,24},{24,0},{1,9},{9,17},{17,25},{25,1},{2,10},{10... | collective-permute-start | bytes 786440 | tf_op jit(solution)/shard_map/ppermute | solution.py:39
  6.6 1.2 %first_south.1 = (bf16[2,64,1024]{2,1,0:T(8,128)(2,1)S(1)}, bf16[2,64,1024]{2,1,0:T(8,128)(2,1)S(1)}) custom-call(bf16[2,64,1024]{2,1,0:T(8,128)(2,1)S(1)} %get-tuple-element.44.q, f32[128,128]{1,0:T(8,128)S(1)} %get-tuple-element.45.info, bf16[1,1,2,128,1024]{4,3,2,1,0:T(8,128)(2,1)} %west.3, bf16[1,1,2,128,1024]{4,3,2,1,0:T(8,128)(2,1)} %north.3, ...), custom_call_target="tpu_custom_call" | custom-call | flops 10000000000 | bytes 1000 | tf_op jit(solution)/shard_map/first_south/pallas_call | solution.py:356
  8.7 1.5 %collective-permute-start = (bf16[2,64,1024]{2,1,0:T(8,128)(2,1)S(1)}, bf16[2,64,1024]{2,1,0:T(8,128)(2,1)S(1)}, u32[]{:S(2)}, u32[]{:S(2)}) collective-permute-start(bf16[2,64,1024]{2,1,0:T(8,128)(2,1)S(1)} %east.9.turn), channel_id=1, source_target_pairs={{0,8},{8,16},{16,24},{24,0},{1,9},{9,17},{17,25},{25,1},{2,10},{10... | collective-permute-start | bytes 786440 | tf_op jit(solution)/shard_map/ppermute | solution.py:39
  11.0 1.5 %collective-permute-start.1 = (bf16[2,64,1024]{2,1,0:T(8,128)(2,1)S(1)}, bf16[2,64,1024]{2,1,0:T(8,128)(2,1)S(1)}, u32[]{:S(2)}, u32[]{:S(2)}) collective-permute-start(bf16[2,64,1024]{2,1,0:T(8,128)(2,1)S(1)} %south.9.turn), channel_id=1, source_target_pairs={{0,1},{1,2},{2,3},{3,4},{4,5},{5,6},{6,7},{7,0},{8,9},{9,10},{10,1... | collective-permute-start | bytes 786440 | tf_op jit(solution)/shard_map/ppermute | solution.py:39
  12.4 3.1 %collective-permute-done.3.n = bf16[2,64,1024]{2,1,0:T(8,128)(2,1)S(1)} collective-permute-done((bf16[2,64,1024]{2,1,0:T(8,128)(2,1)S(1)}, bf16[2,64,1024]{2,1,0:T(8,128)(2,1)S(1)}, u32[]{:S(2)}, u32[]{:S(2)}) %collective-permute-start.3) | collective-permute-done | bytes 262176 | tf_op jit(solution)/shard_map/ppermute | solution.py:39
  16.4 1.5 %collective-permute-start.6 = (bf16[2,64,1024]{2,1,0:T(8,128)(2,1)S(1)}, bf16[2,64,1024]{2,1,0:T(8,128)(2,1)S(1)}, u32[]{:S(2)}, u32[]{:S(2)}) collective-permute-start(bf16[2,64,1024]{2,1,0:T(8,128)(2,1)S(1)} %get-tuple-element.51.turn), channel_id=1, source_target_pairs={{0,8},{8,16},{16,24},{24,0},{1,9},{9,17},{17,25},{25,1},{2,10},{10... | collective-permute-start | bytes 786440 | tf_op jit(solution)/shard_map/ppermute | solution.py:39
  20.3 1.0 %collective-permute-start.4 = (bf16[2,64,1024]{2,1,0:T(8,128)(2,1)S(1)}, bf16[2,64,1024]{2,1,0:T(8,128)(2,1)S(1)}, u32[]{:S(2)}, u32[]{:S(2)}) collective-permute-start(bf16[2,64,1024]{2,1,0:T(8,128)(2,1)S(1)} %get-tuple-element.52.turn), channel_id=1, source_target_pairs={{0,8},{8,16},{16,24},{24,0},{1,9},{9,17},{17,25},{25,1},{2,10},{10... | collective-permute-start | bytes 786440 | tf_op jit(solution)/shard_map/ppermute | solution.py:39
  22.1 4.2 %collective-permute-done.7.n = bf16[2,64,1024]{2,1,0:T(8,128)(2,1)S(1)} collective-permute-done((bf16[2,64,1024]{2,1,0:T(8,128)(2,1)S(1)}, bf16[2,64,1024]{2,1,0:T(8,128)(2,1)S(1)}, u32[]{:S(2)}, u32[]{:S(2)}) %collective-permute-start.7) | collective-permute-done | bytes 262176 | tf_op jit(solution)/shard_map/ppermute | solution.py:39
  27.2 1.5 %collective-permute-start.10 = (bf16[2,64,1024]{2,1,0:T(8,128)(2,1)S(1)}, bf16[2,64,1024]{2,1,0:T(8,128)(2,1)S(1)}, u32[]{:S(2)}, u32[]{:S(2)}) collective-permute-start(bf16[2,64,1024]{2,1,0:T(8,128)(2,1)S(1)} %get-tuple-element.55.turn), channel_id=1, source_target_pairs={{0,8},{8,16},{16,24},{24,0},{1,9},{9,17},{17,25},{25,1},{2,10},{10... | collective-permute-start | bytes 786440 | tf_op jit(solution)/shard_map/ppermute | solution.py:39
  29.7 2.1 %collective-permute-done.4.w = bf16[2,64,1024]{2,1,0:T(8,128)(2,1)S(1)} collective-permute-done((bf16[2,64,1024]{2,1,0:T(8,128)(2,1)S(1)}, bf16[2,64,1024]{2,1,0:T(8,128)(2,1)S(1)}, u32[]{:S(2)}, u32[]{:S(2)}) %collective-permute-start.4) | collective-permute-done | bytes 262176 | tf_op jit(solution)/shard_map/ppermute | solution.py:39
  32.7 1.0 %collective-permute-start.8 = (bf16[2,64,1024]{2,1,0:T(8,128)(2,1)S(1)}, bf16[2,64,1024]{2,1,0:T(8,128)(2,1)S(1)}, u32[]{:S(2)}, u32[]{:S(2)}) collective-permute-start(bf16[2,64,1024]{2,1,0:T(8,128)(2,1)S(1)} %get-tuple-element.56.turn), channel_id=1, source_target_pairs={{0,8},{8,16},{16,24},{24,0},{1,9},{9,17},{17,25},{25,1},{2,10},{10... | collective-permute-start | bytes 786440 | tf_op jit(solution)/shard_map/ppermute | solution.py:39
  34.5 2.6 %collective-permute-done.11.n = bf16[2,64,1024]{2,1,0:T(8,128)(2,1)S(1)} collective-permute-done((bf16[2,64,1024]{2,1,0:T(8,128)(2,1)S(1)}, bf16[2,64,1024]{2,1,0:T(8,128)(2,1)S(1)}, u32[]{:S(2)}, u32[]{:S(2)}) %collective-permute-start.11) | collective-permute-done | bytes 262176 | tf_op jit(solution)/shard_map/ppermute | solution.py:39
  38.3 1.3 %collective-permute-start.14 = (bf16[2,64,1024]{2,1,0:T(8,128)(2,1)S(1)}, bf16[2,64,1024]{2,1,0:T(8,128)(2,1)S(1)}, u32[]{:S(2)}, u32[]{:S(2)}) collective-permute-start(bf16[2,64,1024]{2,1,0:T(8,128)(2,1)S(1)} %get-tuple-element.59.turn), channel_id=1, source_target_pairs={{0,8},{8,16},{16,24},{24,0},{1,9},{9,17},{17,25},{25,1},{2,10},{10... | collective-permute-start | bytes 786440 | tf_op jit(solution)/shard_map/ppermute | solution.py:39
  40.4 1.7 %collective-permute-done.9.n = bf16[2,64,1024]{2,1,0:T(8,128)(2,1)S(1)} collective-permute-done((bf16[2,64,1024]{2,1,0:T(8,128)(2,1)S(1)}, bf16[2,64,1024]{2,1,0:T(8,128)(2,1)S(1)}, u32[]{:S(2)}, u32[]{:S(2)}) %collective-permute-start.9) | collective-permute-done | bytes 262176 | tf_op jit(solution)/shard_map/ppermute | solution.py:39
  44.0 1.5 %collective-permute-start.12 = (bf16[2,64,1024]{2,1,0:T(8,128)(2,1)S(1)}, bf16[2,64,1024]{2,1,0:T(8,128)(2,1)S(1)}, u32[]{:S(2)}, u32[]{:S(2)}) collective-permute-start(bf16[2,64,1024]{2,1,0:T(8,128)(2,1)S(1)} %get-tuple-element.60.turn), channel_id=1, source_target_pairs={{0,8},{8,16},{16,24},{24,0},{1,9},{9,17},{17,25},{25,1},{2,10},{10... | collective-permute-start | bytes 786440 | tf_op jit(solution)/shard_map/ppermute | solution.py:39
  46.2 1.8 %collective-permute-done.15.n = bf16[2,64,1024]{2,1,0:T(8,128)(2,1)S(1)} collective-permute-done((bf16[2,64,1024]{2,1,0:T(8,128)(2,1)S(1)}, bf16[2,64,1024]{2,1,0:T(8,128)(2,1)S(1)}, u32[]{:S(2)}, u32[]{:S(2)}) %collective-permute-start.15) | collective-permute-done | bytes 262176 | tf_op jit(solution)/shard_map/ppermute | solution.py:39
  49.6 1.3 %collective-permute-start.18 = (bf16[2,64,1024]{2,1,0:T(8,128)(2,1)S(1)}, bf16[2,64,1024]{2,1,0:T(8,128)(2,1)S(1)}, u32[]{:S(2)}, u32[]{:S(2)}) collective-permute-start(bf16[2,64,1024]{2,1,0:T(8,128)(2,1)S(1)} %get-tuple-element.63.turn), channel_id=1, source_target_pairs={{0,8},{8,16},{16,24},{24,0},{1,9},{9,17},{17,25},{25,1},{2,10},{10... | collective-permute-start | bytes 786440 | tf_op jit(solution)/shard_map/ppermute | solution.py:39
  51.7 2.1 %collective-permute-done.13.n = bf16[2,64,1024]{2,1,0:T(8,128)(2,1)S(1)} collective-permute-done((bf16[2,64,1024]{2,1,0:T(8,128)(2,1)S(1)}, bf16[2,64,1024]{2,1,0:T(8,128)(2,1)S(1)}, u32[]{:S(2)}, u32[]{:S(2)}) %collective-permute-start.13) | collective-permute-done | bytes 262176 | tf_op jit(solution)/shard_map/ppermute | solution.py:39
  55.2 1.5 %collective-permute-start.16 = (bf16[2,64,1024]{2,1,0:T(8,128)(2,1)S(1)}, bf16[2,64,1024]{2,1,0:T(8,128)(2,1)S(1)}, u32[]{:S(2)}, u32[]{:S(2)}) collective-permute-start(bf16[2,64,1024]{2,1,0:T(8,128)(2,1)S(1)} %get-tuple-element.64.turn), channel_id=1, source_target_pairs={{0,8},{8,16},{16,24},{24,0},{1,9},{9,17},{17,25},{25,1},{2,10},{10... | collective-permute-start | bytes 786440 | tf_op jit(solution)/shard_map/ppermute | solution.py:39
  57.5 1.8 %collective-permute-done.19.n = bf16[2,64,1024]{2,1,0:T(8,128)(2,1)S(1)} collective-permute-done((bf16[2,64,1024]{2,1,0:T(8,128)(2,1)S(1)}, bf16[2,64,1024]{2,1,0:T(8,128)(2,1)S(1)}, u32[]{:S(2)}, u32[]{:S(2)}) %collective-permute-start.19) | collective-permute-done | bytes 262176 | tf_op jit(solution)/shard_map/ppermute | solution.py:39
  60.8 1.3 %collective-permute-start.20 = (bf16[2,64,1024]{2,1,0:T(8,128)(2,1)S(1)}, bf16[2,64,1024]{2,1,0:T(8,128)(2,1)S(1)}, u32[]{:S(2)}, u32[]{:S(2)}) collective-permute-start(bf16[2,64,1024]{2,1,0:T(8,128)(2,1)S(1)} %get-tuple-element.67.first), channel_id=1, source_target_pairs={{0,8},{24,16},{8,24},{16,0},{1,9},{25,17},{9,25},{17,1},{2,10},{26... | collective-permute-start | bytes 786440 | tf_op jit(solution)/shard_map/ppermute | solution.py:401
  62.9 2.2 %collective-permute-done.17.n = bf16[2,64,1024]{2,1,0:T(8,128)(2,1)S(1)} collective-permute-done((bf16[2,64,1024]{2,1,0:T(8,128)(2,1)S(1)}, bf16[2,64,1024]{2,1,0:T(8,128)(2,1)S(1)}, u32[]{:S(2)}, u32[]{:S(2)}) %collective-permute-start.17) | collective-permute-done | bytes 262176 | tf_op jit(solution)/shard_map/ppermute | solution.py:39
  66.4 1.3 %collective-permute-start.21 = (bf16[2,64,1024]{2,1,0:T(8,128)(2,1)S(1)}, bf16[2,64,1024]{2,1,0:T(8,128)(2,1)S(1)}, u32[]{:S(2)}, u32[]{:S(2)}) collective-permute-start(bf16[2,64,1024]{2,1,0:T(8,128)(2,1)S(1)} %get-tuple-element.70), channel_id=1, source_target_pairs={{0,8},{24,16},{8,24},{16,0},{1,9},{25,17},{9,25},{17,1},{2,10},{26... | collective-permute-start | bytes 786440 | tf_op jit(solution)/shard_map/ppermute | solution.py:401
  68.6 2.5 %collective-permute-start.24 = (bf16[2,128,2176]{2,1,0:T(8,128)(2,1)S(1)}, bf16[2,128,2176]{2,1,0:T(8,128)(2,1)S(1)}, u32[]{:S(2)}, u32[]{:S(2)}) collective-permute-start(bf16[2,128,2176]{2,1,0:T(8,128)(2,1)S(1)} %last_south.1.turn), channel_id=1, source_target_pairs={{0,1},{1,2},{2,3},{3,4},{4,5},{5,6},{6,7},{8,9},{9,10},{10,11},{11... | collective-permute-start | bytes 3342344 | tf_op jit(solution)/shard_map/ppermute | solution.py:44
  71.2 1.2 %collective-permute-start.26 = (bf16[2,64,1024]{2,1,0:T(8,128)(2,1)S(1)}, bf16[2,64,1024]{2,1,0:T(8,128)(2,1)S(1)}, u32[]{:S(2)}, u32[]{:S(2)}) collective-permute-start(bf16[2,64,1024]{2,1,0:T(8,128)(2,1)S(1)} %get-tuple-element.72.turn), channel_id=1, source_target_pairs={{0,8},{8,0},{16,24},{24,16},{1,9},{9,1},{17,25},{25,17},{2,10},{10... | collective-permute-start | bytes 786440 | tf_op jit(solution)/shard_map/ppermute | solution.py:417
  72.4 1.3 %collective-permute-start.25 = (bf16[2,128,1024]{2,1,0:T(8,128)(2,1)S(1)}, bf16[2,128,1024]{2,1,0:T(8,128)(2,1)S(1)}, u32[]{:S(2)}, u32[]{:S(2)}) collective-permute-start(bf16[2,128,1024]{2,1,0:T(8,128)(2,1)S(1)} %get-tuple-element.74.q), channel_id=1, source_target_pairs={{1,0},{2,1},{3,2},{4,3},{5,4},{6,5},{7,6},{9,8},{10,9},{11,10},{12... | collective-permute-start | bytes 1572872 | tf_op jit(solution)/shard_map/ppermute | solution.py:44
  73.7 2.0 %collective-permute-done.21.first1 = bf16[2,64,1024]{2,1,0:T(8,128)(2,1)S(1)} collective-permute-done((bf16[2,64,1024]{2,1,0:T(8,128)(2,1)S(1)}, bf16[2,64,1024]{2,1,0:T(8,128)(2,1)S(1)}, u32[]{:S(2)}, u32[]{:S(2)}) %collective-permute-start.21) | collective-permute-done | bytes 262176 | tf_op jit(solution)/shard_map/ppermute | solution.py:401
  75.7 1.1 %middle1.1 = (bf16[2,64,1024]{2,1,0:T(8,128)(2,1)S(1)}, bf16[1,1,2,128,1024]{4,3,2,1,0:T(8,128)(2,1)}, bf16[2,128,128]{2,1,0:T(8,128)(2,1)S(1)}) custom-call(bf16[2,64,1024]{2,1,0:T(8,128)(2,1)S(1)} %get-tuple-element.69.q1.q, bf16[2,64,1024]{2,1,0:T(8,128)(2,1)S(1)} %collective-permute-done.20.far.first0, ...), custom_call_target="tpu_custom_call" | custom-call | flops 10000000000 | bytes 1000 | tf_op jit(solution)/shard_map/middle1/pallas_call | solution.py:419
  77.8 4.9 %collective-permute-done.26.side = bf16[2,64,1024]{2,1,0:T(8,128)(2,1)S(1)} collective-permute-done((bf16[2,64,1024]{2,1,0:T(8,128)(2,1)S(1)}, bf16[2,64,1024]{2,1,0:T(8,128)(2,1)S(1)}, u32[]{:S(2)}, u32[]{:S(2)}) %collective-permute-start.26) | collective-permute-done | bytes 262176 | tf_op jit(solution)/shard_map/ppermute | solution.py:417
  82.7 1.1 %base.1 = (f32[2,64,1024]{2,1,0:T(8,128)S(1)}, bf16[1,1,2,128,128]{4,3,2,1,0:T(8,128)(2,1)}, bf16[1,1,2,128,1024]{4,3,2,1,0:T(8,128)(2,1)}, f32[1,1,2,128,1024]{4,3,2,1,0:T(8,128)}) custom-call(bf16[2,128,1024]{2,1,0:T(8,128)(2,1)S(1)} %get-tuple-element.74.q, bf16[2,128,2176]{2,1,0:T(8,128)(2,1)S(1)} %collective-permute-done.24.tray, ...), custom_call_target="tpu_custom_call" | custom-call | flops 1000 | bytes 1000 | tf_op jit(solution)/shard_map/base/pallas_call | solution.py:430
  84.0 3.2 %collective-permute-done.27.side = bf16[2,64,1024]{2,1,0:T(8,128)(2,1)S(1)} collective-permute-done((bf16[2,64,1024]{2,1,0:T(8,128)(2,1)S(1)}, bf16[2,64,1024]{2,1,0:T(8,128)(2,1)S(1)}, u32[]{:S(2)}, u32[]{:S(2)}) %collective-permute-start.27) | collective-permute-done | bytes 262176 | tf_op jit(solution)/shard_map/ppermute | solution.py:427
  (58 shorter events, 24.6 us)
Async XLA Ops:
  0.6 6.0 %copy-start = (bf16[1,1,2,1024,1024]{4,3,2,1,0:T(8,128)(2,1)S(1)}, bf16[1,1,2,1024,1024]{4,3,2,1,0:T(8,128)(2,1)}, u32[]{:S(2)}) copy-start(bf16[1,1,2,1024,1024]{4,3,2,1,0:T(8,128)(2,1)} %param.17) | copy-start | bytes 12582916
  3.6 11.9 %collective-permute-start.2 = (bf16[2,64,1024]{2,1,0:T(8,128)(2,1)S(1)}, bf16[2,64,1024]{2,1,0:T(8,128)(2,1)S(1)}, u32[]{:S(2)}, u32[]{:S(2)}) collective-permute-start(bf16[2,64,1024]{2,1,0:T(8,128)(2,1)S(1)} %get-tuple-element.46.turn), channel_id=1, source_target_pairs={{0,8},{8,16},{16,24},{24,0},{1,9},{9,17},{17,25},{25,1},{2,10},{10... | collective-permute-start | bytes 786440 | tf_op jit(solution)/shard_map/ppermute | solution.py:39
  7.9 7.6 %collective-permute-start.3 = (bf16[2,64,1024]{2,1,0:T(8,128)(2,1)S(1)}, bf16[2,64,1024]{2,1,0:T(8,128)(2,1)S(1)}, u32[]{:S(2)}, u32[]{:S(2)}) collective-permute-start(bf16[2,64,1024]{2,1,0:T(8,128)(2,1)S(1)} %get-tuple-element.49.turn), channel_id=1, source_target_pairs={{0,1},{1,2},{2,3},{3,4},{4,5},{5,6},{6,7},{7,0},{8,9},{9,10},{10,1... | collective-permute-start | bytes 786440 | tf_op jit(solution)/shard_map/ppermute | solution.py:39
  8.7 6.9 %copy-start.1 = (bf16[1,1,2,128,128]{4,3,2,1,0:T(8,128)(2,1)S(1)}, bf16[1,1,2,128,128]{4,3,2,1,0:T(8,128)(2,1)}, u32[]{:S(2)}) copy-start(bf16[1,1,2,128,128]{4,3,2,1,0:T(8,128)(2,1)} %corner.7) | copy-start | bytes 196612
  8.7 10.7 %collective-permute-start = (bf16[2,64,1024]{2,1,0:T(8,128)(2,1)S(1)}, bf16[2,64,1024]{2,1,0:T(8,128)(2,1)S(1)}, u32[]{:S(2)}, u32[]{:S(2)}) collective-permute-start(bf16[2,64,1024]{2,1,0:T(8,128)(2,1)S(1)} %east.9.turn), channel_id=1, source_target_pairs={{0,8},{8,16},{16,24},{24,0},{1,9},{9,17},{17,25},{25,1},{2,10},{10... | collective-permute-start | bytes 786440 | tf_op jit(solution)/shard_map/ppermute | solution.py:39
  11.0 7.8 %collective-permute-start.1 = (bf16[2,64,1024]{2,1,0:T(8,128)(2,1)S(1)}, bf16[2,64,1024]{2,1,0:T(8,128)(2,1)S(1)}, u32[]{:S(2)}, u32[]{:S(2)}) collective-permute-start(bf16[2,64,1024]{2,1,0:T(8,128)(2,1)S(1)} %south.9.turn), channel_id=1, source_target_pairs={{0,1},{1,2},{2,3},{3,4},{4,5},{5,6},{6,7},{7,0},{8,9},{9,10},{10,1... | collective-permute-start | bytes 786440 | tf_op jit(solution)/shard_map/ppermute | solution.py:39
  16.4 9.9 %collective-permute-start.6 = (bf16[2,64,1024]{2,1,0:T(8,128)(2,1)S(1)}, bf16[2,64,1024]{2,1,0:T(8,128)(2,1)S(1)}, u32[]{:S(2)}, u32[]{:S(2)}) collective-permute-start(bf16[2,64,1024]{2,1,0:T(8,128)(2,1)S(1)} %get-tuple-element.51.turn), channel_id=1, source_target_pairs={{0,8},{8,16},{16,24},{24,0},{1,9},{9,17},{17,25},{25,1},{2,10},{10... | collective-permute-start | bytes 786440 | tf_op jit(solution)/shard_map/ppermute | solution.py:39
  18.7 7.6 %collective-permute-start.7 = (bf16[2,64,1024]{2,1,0:T(8,128)(2,1)S(1)}, bf16[2,64,1024]{2,1,0:T(8,128)(2,1)S(1)}, u32[]{:S(2)}, u32[]{:S(2)}) collective-permute-start(bf16[2,64,1024]{2,1,0:T(8,128)(2,1)S(1)} %south.10.turn), channel_id=1, source_target_pairs={{0,1},{1,2},{2,3},{3,4},{4,5},{5,6},{6,7},{7,0},{8,9},{9,10},{10,1... | collective-permute-start | bytes 786440 | tf_op jit(solution)/shard_map/ppermute | solution.py:39
  20.3 11.6 %collective-permute-start.4 = (bf16[2,64,1024]{2,1,0:T(8,128)(2,1)S(1)}, bf16[2,64,1024]{2,1,0:T(8,128)(2,1)S(1)}, u32[]{:S(2)}, u32[]{:S(2)}) collective-permute-start(bf16[2,64,1024]{2,1,0:T(8,128)(2,1)S(1)} %get-tuple-element.52.turn), channel_id=1, source_target_pairs={{0,8},{8,16},{16,24},{24,0},{1,9},{9,17},{17,25},{25,1},{2,10},{10... | collective-permute-start | bytes 786440 | tf_op jit(solution)/shard_map/ppermute | solution.py:39
  22.1 7.6 %collective-permute-start.5 = (bf16[2,64,1024]{2,1,0:T(8,128)(2,1)S(1)}, bf16[2,64,1024]{2,1,0:T(8,128)(2,1)S(1)}, u32[]{:S(2)}, u32[]{:S(2)}) collective-permute-start(bf16[2,64,1024]{2,1,0:T(8,128)(2,1)S(1)} %south.11.turn), channel_id=1, source_target_pairs={{0,1},{1,2},{2,3},{3,4},{4,5},{5,6},{6,7},{7,0},{8,9},{9,10},{10,1... | collective-permute-start | bytes 786440 | tf_op jit(solution)/shard_map/ppermute | solution.py:39
  27.2 10.3 %collective-permute-start.10 = (bf16[2,64,1024]{2,1,0:T(8,128)(2,1)S(1)}, bf16[2,64,1024]{2,1,0:T(8,128)(2,1)S(1)}, u32[]{:S(2)}, u32[]{:S(2)}) collective-permute-start(bf16[2,64,1024]{2,1,0:T(8,128)(2,1)S(1)} %get-tuple-element.55.turn), channel_id=1, source_target_pairs={{0,8},{8,16},{16,24},{24,0},{1,9},{9,17},{17,25},{25,1},{2,10},{10... | collective-permute-start | bytes 786440 | tf_op jit(solution)/shard_map/ppermute | solution.py:39
  29.5 7.6 %collective-permute-start.11 = (bf16[2,64,1024]{2,1,0:T(8,128)(2,1)S(1)}, bf16[2,64,1024]{2,1,0:T(8,128)(2,1)S(1)}, u32[]{:S(2)}, u32[]{:S(2)}) collective-permute-start(bf16[2,64,1024]{2,1,0:T(8,128)(2,1)S(1)} %south.12.turn), channel_id=1, source_target_pairs={{0,1},{1,2},{2,3},{3,4},{4,5},{5,6},{6,7},{7,0},{8,9},{9,10},{10,1... | collective-permute-start | bytes 786440 | tf_op jit(solution)/shard_map/ppermute | solution.py:39
  32.7 10.4 %collective-permute-start.8 = (bf16[2,64,1024]{2,1,0:T(8,128)(2,1)S(1)}, bf16[2,64,1024]{2,1,0:T(8,128)(2,1)S(1)}, u32[]{:S(2)}, u32[]{:S(2)}) collective-permute-start(bf16[2,64,1024]{2,1,0:T(8,128)(2,1)S(1)} %get-tuple-element.56.turn), channel_id=1, source_target_pairs={{0,8},{8,16},{16,24},{24,0},{1,9},{9,17},{17,25},{25,1},{2,10},{10... | collective-permute-start | bytes 786440 | tf_op jit(solution)/shard_map/ppermute | solution.py:39
  34.5 7.6 %collective-permute-start.9 = (bf16[2,64,1024]{2,1,0:T(8,128)(2,1)S(1)}, bf16[2,64,1024]{2,1,0:T(8,128)(2,1)S(1)}, u32[]{:S(2)}, u32[]{:S(2)}) collective-permute-start(bf16[2,64,1024]{2,1,0:T(8,128)(2,1)S(1)} %south.13.turn), channel_id=1, source_target_pairs={{0,1},{1,2},{2,3},{3,4},{4,5},{5,6},{6,7},{7,0},{8,9},{9,10},{10,1... | collective-permute-start | bytes 786440 | tf_op jit(solution)/shard_map/ppermute | solution.py:39
  38.3 10.4 %collective-permute-start.14 = (bf16[2,64,1024]{2,1,0:T(8,128)(2,1)S(1)}, bf16[2,64,1024]{2,1,0:T(8,128)(2,1)S(1)}, u32[]{:S(2)}, u32[]{:S(2)}) collective-permute-start(bf16[2,64,1024]{2,1,0:T(8,128)(2,1)S(1)} %get-tuple-element.59.turn), channel_id=1, source_target_pairs={{0,8},{8,16},{16,24},{24,0},{1,9},{9,17},{17,25},{25,1},{2,10},{10... | collective-permute-start | bytes 786440 | tf_op jit(solution)/shard_map/ppermute | solution.py:39
  40.4 7.6 %collective-permute-start.15 = (bf16[2,64,1024]{2,1,0:T(8,128)(2,1)S(1)}, bf16[2,64,1024]{2,1,0:T(8,128)(2,1)S(1)}, u32[]{:S(2)}, u32[]{:S(2)}) collective-permute-start(bf16[2,64,1024]{2,1,0:T(8,128)(2,1)S(1)} %south.14.turn), channel_id=1, source_target_pairs={{0,1},{1,2},{2,3},{3,4},{4,5},{5,6},{6,7},{7,0},{8,9},{9,10},{10,1... | collective-permute-start | bytes 786440 | tf_op jit(solution)/shard_map/ppermute | solution.py:39
  44.0 10.4 %collective-permute-start.12 = (bf16[2,64,1024]{2,1,0:T(8,128)(2,1)S(1)}, bf16[2,64,1024]{2,1,0:T(8,128)(2,1)S(1)}, u32[]{:S(2)}, u32[]{:S(2)}) collective-permute-start(bf16[2,64,1024]{2,1,0:T(8,128)(2,1)S(1)} %get-tuple-element.60.turn), channel_id=1, source_target_pairs={{0,8},{8,16},{16,24},{24,0},{1,9},{9,17},{17,25},{25,1},{2,10},{10... | collective-permute-start | bytes 786440 | tf_op jit(solution)/shard_map/ppermute | solution.py:39
  46.2 7.6 %collective-permute-start.13 = (bf16[2,64,1024]{2,1,0:T(8,128)(2,1)S(1)}, bf16[2,64,1024]{2,1,0:T(8,128)(2,1)S(1)}, u32[]{:S(2)}, u32[]{:S(2)}) collective-permute-start(bf16[2,64,1024]{2,1,0:T(8,128)(2,1)S(1)} %south.15.turn), channel_id=1, source_target_pairs={{0,1},{1,2},{2,3},{3,4},{4,5},{5,6},{6,7},{7,0},{8,9},{9,10},{10,1... | collective-permute-start | bytes 786440 | tf_op jit(solution)/shard_map/ppermute | solution.py:39
  49.6 10.4 %collective-permute-start.18 = (bf16[2,64,1024]{2,1,0:T(8,128)(2,1)S(1)}, bf16[2,64,1024]{2,1,0:T(8,128)(2,1)S(1)}, u32[]{:S(2)}, u32[]{:S(2)}) collective-permute-start(bf16[2,64,1024]{2,1,0:T(8,128)(2,1)S(1)} %get-tuple-element.63.turn), channel_id=1, source_target_pairs={{0,8},{8,16},{16,24},{24,0},{1,9},{9,17},{17,25},{25,1},{2,10},{10... | collective-permute-start | bytes 786440 | tf_op jit(solution)/shard_map/ppermute | solution.py:39
  51.6 7.6 %collective-permute-start.19 = (bf16[2,64,1024]{2,1,0:T(8,128)(2,1)S(1)}, bf16[2,64,1024]{2,1,0:T(8,128)(2,1)S(1)}, u32[]{:S(2)}, u32[]{:S(2)}) collective-permute-start(bf16[2,64,1024]{2,1,0:T(8,128)(2,1)S(1)} %south.16.turn), channel_id=1, source_target_pairs={{0,1},{1,2},{2,3},{3,4},{4,5},{5,6},{6,7},{7,0},{8,9},{9,10},{10,1... | collective-permute-start | bytes 786440 | tf_op jit(solution)/shard_map/ppermute | solution.py:39
  55.2 10.4 %collective-permute-start.16 = (bf16[2,64,1024]{2,1,0:T(8,128)(2,1)S(1)}, bf16[2,64,1024]{2,1,0:T(8,128)(2,1)S(1)}, u32[]{:S(2)}, u32[]{:S(2)}) collective-permute-start(bf16[2,64,1024]{2,1,0:T(8,128)(2,1)S(1)} %get-tuple-element.64.turn), channel_id=1, source_target_pairs={{0,8},{8,16},{16,24},{24,0},{1,9},{9,17},{17,25},{25,1},{2,10},{10... | collective-permute-start | bytes 786440 | tf_op jit(solution)/shard_map/ppermute | solution.py:39
  57.4 7.6 %collective-permute-start.17 = (bf16[2,64,1024]{2,1,0:T(8,128)(2,1)S(1)}, bf16[2,64,1024]{2,1,0:T(8,128)(2,1)S(1)}, u32[]{:S(2)}, u32[]{:S(2)}) collective-permute-start(bf16[2,64,1024]{2,1,0:T(8,128)(2,1)S(1)} %south.17.turn), channel_id=1, source_target_pairs={{0,1},{1,2},{2,3},{3,4},{4,5},{5,6},{6,7},{7,0},{8,9},{9,10},{10,1... | collective-permute-start | bytes 786440 | tf_op jit(solution)/shard_map/ppermute | solution.py:39
  60.8 10.3 %collective-permute-start.20 = (bf16[2,64,1024]{2,1,0:T(8,128)(2,1)S(1)}, bf16[2,64,1024]{2,1,0:T(8,128)(2,1)S(1)}, u32[]{:S(2)}, u32[]{:S(2)}) collective-permute-start(bf16[2,64,1024]{2,1,0:T(8,128)(2,1)S(1)} %get-tuple-element.67.first), channel_id=1, source_target_pairs={{0,8},{24,16},{8,24},{16,0},{1,9},{25,17},{9,25},{17,1},{2,10},{26... | collective-permute-start | bytes 786440 | tf_op jit(solution)/shard_map/ppermute | solution.py:401
  62.1 9.0 %collective-permute-start.22 = (bf16[2,64,1024]{2,1,0:T(8,128)(2,1)S(1)}, bf16[2,64,1024]{2,1,0:T(8,128)(2,1)S(1)}, u32[]{:S(2)}, u32[]{:S(2)}) collective-permute-start(bf16[2,64,1024]{2,1,0:T(8,128)(2,1)S(1)} %get-tuple-element.68.turn), channel_id=1, source_target_pairs={{0,1},{1,0},{2,3},{3,2},{4,5},{5,4},{6,7},{7,6},{24,8},{25,9},{26,... | collective-permute-start | bytes 786440 | tf_op jit(solution)/shard_map/ppermute | solution.py:402
  66.4 9.2 %collective-permute-start.21 = (bf16[2,64,1024]{2,1,0:T(8,128)(2,1)S(1)}, bf16[2,64,1024]{2,1,0:T(8,128)(2,1)S(1)}, u32[]{:S(2)}, u32[]{:S(2)}) collective-permute-start(bf16[2,64,1024]{2,1,0:T(8,128)(2,1)S(1)} %get-tuple-element.70), channel_id=1, source_target_pairs={{0,8},{24,16},{8,24},{16,0},{1,9},{25,17},{9,25},{17,1},{2,10},{26... | collective-permute-start | bytes 786440 | tf_op jit(solution)/shard_map/ppermute | solution.py:401
  67.8 7.9 %collective-permute-start.23 = (bf16[2,64,1024]{2,1,0:T(8,128)(2,1)S(1)}, bf16[2,64,1024]{2,1,0:T(8,128)(2,1)S(1)}, u32[]{:S(2)}, u32[]{:S(2)}) collective-permute-start(bf16[2,64,1024]{2,1,0:T(8,128)(2,1)S(1)} %get-tuple-element.71.turn), channel_id=1, source_target_pairs={{0,1},{1,0},{2,3},{3,2},{4,5},{5,4},{6,7},{7,6},{24,8},{25,9},{26,... | collective-permute-start | bytes 786440 | tf_op jit(solution)/shard_map/ppermute | solution.py:402
  68.6 14.1 %collective-permute-start.24 = (bf16[2,128,2176]{2,1,0:T(8,128)(2,1)S(1)}, bf16[2,128,2176]{2,1,0:T(8,128)(2,1)S(1)}, u32[]{:S(2)}, u32[]{:S(2)}) collective-permute-start(bf16[2,128,2176]{2,1,0:T(8,128)(2,1)S(1)} %last_south.1.turn), channel_id=1, source_target_pairs={{0,1},{1,2},{2,3},{3,4},{4,5},{5,6},{6,7},{8,9},{9,10},{10,11},{11... | collective-permute-start | bytes 3342344 | tf_op jit(solution)/shard_map/ppermute | solution.py:44
  71.2 11.5 %collective-permute-start.26 = (bf16[2,64,1024]{2,1,0:T(8,128)(2,1)S(1)}, bf16[2,64,1024]{2,1,0:T(8,128)(2,1)S(1)}, u32[]{:S(2)}, u32[]{:S(2)}) collective-permute-start(bf16[2,64,1024]{2,1,0:T(8,128)(2,1)S(1)} %get-tuple-element.72.turn), channel_id=1, source_target_pairs={{0,8},{8,0},{16,24},{24,16},{1,9},{9,1},{17,25},{25,17},{2,10},{10... | collective-permute-start | bytes 786440 | tf_op jit(solution)/shard_map/ppermute | solution.py:417
  72.4 10.3 %collective-permute-start.25 = (bf16[2,128,1024]{2,1,0:T(8,128)(2,1)S(1)}, bf16[2,128,1024]{2,1,0:T(8,128)(2,1)S(1)}, u32[]{:S(2)}, u32[]{:S(2)}) collective-permute-start(bf16[2,128,1024]{2,1,0:T(8,128)(2,1)S(1)} %get-tuple-element.74.q), channel_id=1, source_target_pairs={{1,0},{2,1},{3,2},{4,3},{5,4},{6,5},{7,6},{9,8},{10,9},{11,10},{12... | collective-permute-start | bytes 1572872 | tf_op jit(solution)/shard_map/ppermute | solution.py:44
  76.8 10.4 %collective-permute-start.27 = (bf16[2,64,1024]{2,1,0:T(8,128)(2,1)S(1)}, bf16[2,64,1024]{2,1,0:T(8,128)(2,1)S(1)}, u32[]{:S(2)}, u32[]{:S(2)}) collective-permute-start(bf16[2,64,1024]{2,1,0:T(8,128)(2,1)S(1)} %get-tuple-element.75.turn), channel_id=1, source_target_pairs={{0,8},{8,0},{16,24},{24,16},{1,9},{9,1},{17,25},{25,17},{2,10},{10... | collective-permute-start | bytes 786440 | tf_op jit(solution)/shard_map/ppermute | solution.py:427
  77.8 6.2 %collective-permute-start.28 = (bf16[2,128,128]{2,1,0:T(8,128)(2,1)S(1)}, bf16[2,128,128]{2,1,0:T(8,128)(2,1)S(1)}, u32[]{:S(2)}, u32[]{:S(2)}) collective-permute-start(bf16[2,128,128]{2,1,0:T(8,128)(2,1)S(1)} %get-tuple-element.79), channel_id=1, source_target_pairs={{0,1},{1,2},{2,3},{3,4},{4,5},{5,6},{6,7},{7,0},{8,9},{9,10},{10,1... | collective-permute-start | bytes 196616 | tf_op jit(solution)/shard_map/ppermute | solution.py:39

commit v4 on v3

--- a/solution.py
+++ b/solution.py
@@ -16,7 +16,7 @@
 
 
 COSTS = dict.fromkeys(
-    ("first_south", "east", "south", "last_east0", "early_south", "last_east1", "middle0", "middle1"), 10**10
+    ("first_south", "pair", "east", "south", "last_east0", "early_south", "last_east1", "middle0", "middle1"), 10**10
 )
 
 
@@ -181,6 +181,11 @@
     @pl.when(jnp.logical_not(start))
     def _():
         first[...] = q[...]
+
+
+def pair_body(q, east_map, south_map, turn, east, south):
+    product_body(q, east_map, turn, east)
+    product_body(q, south_map, turn, south)
 
 
 def product_body(q, maps, turn, out):
@@ -362,10 +367,10 @@
         [*bench, dma((3,))],
     )(q0, info, *fixed[3:6], south_held, east)
     n0 = ring(south, "gy", 1)
-    east = kernel_call("east", product_body, part, [VMEM, VMEM, ANY], VMEM)(q1, east_held, south)
-    w1 = ring(east, "gx", 1)
-    south = kernel_call("south", product_body, part, [VMEM, VMEM, ANY], VMEM)(q1, south_held, east)
-    n1 = ring(south, "gy", 1)
+    east, south = kernel_call("pair", pair_body, (part, part), [VMEM] * 3 + [ANY], [VMEM] * 2)(
+        q1, east_held, south_held, south
+    )
+    w1, n1 = ring(east, "gx", 1), ring(south, "gy", 1)
     west, north = [w0, w1], [n0, n1]
     for tick in range(1, TICKS - 1):
         for p in range(PARTS):

time: 88.4 us -> 88.4 us (level)
  transfers between devices with their start and end apart: 29 -> 29, of which waited for: 21 -> 21; matrix products, arithmetic and copies ran while one was open for 0% -> 0% of each run, Pallas kernels for 24% -> 23%
where the time goes in v4:
time: 88.4 us; the launch traced here: 88.2 us
  waiting for transfers between devices  36.7 us (42%)
  starting transfers between devices  25.8 us (29%)
  Pallas kernels  24.5 us (28%)
  between operations  1.14 us (1%)
    ppermute x21, waiting for transfers between devices, ring(): lax.ppermute(x, axis, [(i, (i + distance) % size) for i in range(size)])  27.1 us
    ppermute x21, starting transfers between devices, ring(): lax.ppermute(x, axis, [(i, (i + distance) % size) for i in range(size)])  17.1 us
    pallas_call x8, Pallas kernels, on_device(): kernel_call('south', functools.partial(south_body, corner_width), part, [...  5.73 us
    pallas_call x6, Pallas kernels, on_device(): kernel_call('east', functools.partial(east_plain_body, tick, p), (part, p...  5.12 us
    ppermute x1, waiting for transfers between devices, on_device(): side0 = lax.ppermute(total, 'gx', pairs)  4.9 us
    ppermute x2, starting transfers between devices, line(): lax.ppermute(x, axis, [(i, i + distance) for i in range(size) if 0 <= i +...  3.75 us
    pallas_call x1, Pallas kernels, on_device(): kernel_call('first', first_body, (part, part, maps, info), [HBM] * 7, [VM...  2.99 us
    ppermute x1, waiting for transfers between devices, on_device(): side1 = lax.ppermute(total, 'gx', pairs)  2.91 us
  transfers between devices with their start and end apart: 29, of which 21 were waited for; matrix products, arithmetic and copies ran while one was open for 0% of the time, Pallas kernels for 23%

profile of v4, /device:TPU:0, one launch (start us, length us, event | category | flops | bytes accessed | tf_op | source)
XLA Modules:
  0.0 88.2 jit_solution(5131802380136088982)
XLA Ops:
  0.6 3.0 %first.1 = (bf16[2,64,1024]{2,1,0:T(8,128)(2,1)S(1)}, bf16[2,64,1024]{2,1,0:T(8,128)(2,1)S(1)}, bf16[2,1024,1024]{2,1,0:T(8,128)(2,1)S(1)}, f32[128,128]{1,0:T(8,128)S(1)}) custom-call(s32[16]{0:T(128)} %plan.1, f32[1,1,16,2,128]{4,3,2,1,0:T(2,128)} %amplitude.1, s32[1,1,16,128]{3,2,1,0:T(8,128)} %positions.1, bf16[1,1,2,128,1024]{4,3,2,1,0:T(8,128)(2,1)} %west.3, ...), custom_call_target="tpu_custom_call" | custom-call | flops 1000 | bytes 1000 | tf_op jit(solution)/shard_map/first/pallas_call | solution.py:341
  3.6 3.0 %collective-permute-start.2 = (bf16[2,64,1024]{2,1,0:T(8,128)(2,1)S(1)}, bf16[2,64,1024]{2,1,0:T(8,128)(2,1)S(1)}, u32[]{:S(2)}, u32[]{:S(2)}) collective-permute-start(bf16[2,64,1024]{2,1,0:T(8,128)(2,1)S(1)} %get-tuple-element.48.turn), channel_id=1, source_target_pairs={{0,8},{8,16},{16,24},{24,0},{1,9},{9,17},{17,25},{25,1},{2,10},{10... | collective-permute-start | bytes 786440 | tf_op jit(solution)/shard_map/ppermute | solution.py:39
  6.6 1.2 %first_south.1 = (bf16[2,64,1024]{2,1,0:T(8,128)(2,1)S(1)}, bf16[2,64,1024]{2,1,0:T(8,128)(2,1)S(1)}) custom-call(bf16[2,64,1024]{2,1,0:T(8,128)(2,1)S(1)} %get-tuple-element.46.q, f32[128,128]{1,0:T(8,128)S(1)} %get-tuple-element.47.info, bf16[1,1,2,128,1024]{4,3,2,1,0:T(8,128)(2,1)} %west.3, bf16[1,1,2,128,1024]{4,3,2,1,0:T(8,128)(2,1)} %north.3, ...), custom_call_target="tpu_custom_call" | custom-call | flops 10000000000 | bytes 1000 | tf_op jit(solution)/shard_map/first_south/pallas_call | solution.py:361
  8.0 1.3 %pair.1 = (bf16[2,64,1024]{2,1,0:T(8,128)(2,1)S(1)}, bf16[2,64,1024]{2,1,0:T(8,128)(2,1)S(1)}) custom-call(bf16[2,64,1024]{2,1,0:T(8,128)(2,1)S(1)} %get-tuple-element.49.q, bf16[2,1024,1024]{2,1,0:T(8,128)(2,1)S(1)} %get-tuple-element.50.east_map.maps, bf16[2,1024,1024]{2,1,0:T(8,128)(2,1)S(1)} %bitcast.2, bf16[2,64,1024]{2,1,0:T(8,128)(2,1)S(1)} %get-tuple-element.51.turn), custom_call_target="tpu_custom_call" | custom-call | flops 10000000000 | bytes 1000 | tf_op jit(solution)/shard_map/pair/pallas_call | solution.py:370
  9.2 1.5 %collective-permute-start = (bf16[2,64,1024]{2,1,0:T(8,128)(2,1)S(1)}, bf16[2,64,1024]{2,1,0:T(8,128)(2,1)S(1)}, u32[]{:S(2)}, u32[]{:S(2)}) collective-permute-start(bf16[2,64,1024]{2,1,0:T(8,128)(2,1)S(1)} %get-tuple-element.52), channel_id=1, source_target_pairs={{0,8},{8,16},{16,24},{24,0},{1,9},{9,17},{17,25},{25,1},{2,10},{10... | collective-permute-start | bytes 786440 | tf_op jit(solution)/shard_map/ppermute | solution.py:39
  10.8 1.4 %collective-permute-start.1 = (bf16[2,64,1024]{2,1,0:T(8,128)(2,1)S(1)}, bf16[2,64,1024]{2,1,0:T(8,128)(2,1)S(1)}, u32[]{:S(2)}, u32[]{:S(2)}) collective-permute-start(bf16[2,64,1024]{2,1,0:T(8,128)(2,1)S(1)} %get-tuple-element.53.turn), channel_id=1, source_target_pairs={{0,1},{1,2},{2,3},{3,4},{4,5},{5,6},{6,7},{7,0},{8,9},{9,10},{10,1... | collective-permute-start | bytes 786440 | tf_op jit(solution)/shard_map/ppermute | solution.py:39
  12.2 3.4 %collective-permute-done.3.n = bf16[2,64,1024]{2,1,0:T(8,128)(2,1)S(1)} collective-permute-done((bf16[2,64,1024]{2,1,0:T(8,128)(2,1)S(1)}, bf16[2,64,1024]{2,1,0:T(8,128)(2,1)S(1)}, u32[]{:S(2)}, u32[]{:S(2)}) %collective-permute-start.3) | collective-permute-done | bytes 262176 | tf_op jit(solution)/shard_map/ppermute | solution.py:39
  16.4 1.5 %collective-permute-start.6 = (bf16[2,64,1024]{2,1,0:T(8,128)(2,1)S(1)}, bf16[2,64,1024]{2,1,0:T(8,128)(2,1)S(1)}, u32[]{:S(2)}, u32[]{:S(2)}) collective-permute-start(bf16[2,64,1024]{2,1,0:T(8,128)(2,1)S(1)} %get-tuple-element.55.turn), channel_id=1, source_target_pairs={{0,8},{8,16},{16,24},{24,0},{1,9},{9,17},{17,25},{25,1},{2,10},{10... | collective-permute-start | bytes 786440 | tf_op jit(solution)/shard_map/ppermute | solution.py:39
  19.8 1.4 %collective-permute-start.4 = (bf16[2,64,1024]{2,1,0:T(8,128)(2,1)S(1)}, bf16[2,64,1024]{2,1,0:T(8,128)(2,1)S(1)}, u32[]{:S(2)}, u32[]{:S(2)}) collective-permute-start(bf16[2,64,1024]{2,1,0:T(8,128)(2,1)S(1)} %get-tuple-element.56.turn), channel_id=1, source_target_pairs={{0,8},{8,16},{16,24},{24,0},{1,9},{9,17},{17,25},{25,1},{2,10},{10... | collective-permute-start | bytes 786440 | tf_op jit(solution)/shard_map/ppermute | solution.py:39
  22.0 4.4 %collective-permute-done.7.n = bf16[2,64,1024]{2,1,0:T(8,128)(2,1)S(1)} collective-permute-done((bf16[2,64,1024]{2,1,0:T(8,128)(2,1)S(1)}, bf16[2,64,1024]{2,1,0:T(8,128)(2,1)S(1)}, u32[]{:S(2)}, u32[]{:S(2)}) %collective-permute-start.7) | collective-permute-done | bytes 262176 | tf_op jit(solution)/shard_map/ppermute | solution.py:39
  27.3 1.4 %collective-permute-start.10 = (bf16[2,64,1024]{2,1,0:T(8,128)(2,1)S(1)}, bf16[2,64,1024]{2,1,0:T(8,128)(2,1)S(1)}, u32[]{:S(2)}, u32[]{:S(2)}) collective-permute-start(bf16[2,64,1024]{2,1,0:T(8,128)(2,1)S(1)} %get-tuple-element.59.turn), channel_id=1, source_target_pairs={{0,8},{8,16},{16,24},{24,0},{1,9},{9,17},{17,25},{25,1},{2,10},{10... | collective-permute-start | bytes 786440 | tf_op jit(solution)/shard_map/ppermute | solution.py:39
  29.6 2.5 %collective-permute-done.4.w = bf16[2,64,1024]{2,1,0:T(8,128)(2,1)S(1)} collective-permute-done((bf16[2,64,1024]{2,1,0:T(8,128)(2,1)S(1)}, bf16[2,64,1024]{2,1,0:T(8,128)(2,1)S(1)}, u32[]{:S(2)}, u32[]{:S(2)}) %collective-permute-start.4) | collective-permute-done | bytes 262176 | tf_op jit(solution)/shard_map/ppermute | solution.py:39
  34.5 2.6 %collective-permute-done.11.n = bf16[2,64,1024]{2,1,0:T(8,128)(2,1)S(1)} collective-permute-done((bf16[2,64,1024]{2,1,0:T(8,128)(2,1)S(1)}, bf16[2,64,1024]{2,1,0:T(8,128)(2,1)S(1)}, u32[]{:S(2)}, u32[]{:S(2)}) %collective-permute-start.11) | collective-permute-done | bytes 262176 | tf_op jit(solution)/shard_map/ppermute | solution.py:39
  38.5 1.3 %collective-permute-start.14 = (bf16[2,64,1024]{2,1,0:T(8,128)(2,1)S(1)}, bf16[2,64,1024]{2,1,0:T(8,128)(2,1)S(1)}, u32[]{:S(2)}, u32[]{:S(2)}) collective-permute-start(bf16[2,64,1024]{2,1,0:T(8,128)(2,1)S(1)} %get-tuple-element.63.turn), channel_id=1, source_target_pairs={{0,8},{8,16},{16,24},{24,0},{1,9},{9,17},{17,25},{25,1},{2,10},{10... | collective-permute-start | bytes 786440 | tf_op jit(solution)/shard_map/ppermute | solution.py:39
  40.6 1.5 %collective-permute-done.9.n = bf16[2,64,1024]{2,1,0:T(8,128)(2,1)S(1)} collective-permute-done((bf16[2,64,1024]{2,1,0:T(8,128)(2,1)S(1)}, bf16[2,64,1024]{2,1,0:T(8,128)(2,1)S(1)}, u32[]{:S(2)}, u32[]{:S(2)}) %collective-permute-start.9) | collective-permute-done | bytes 262176 | tf_op jit(solution)/shard_map/ppermute | solution.py:39
  42.1 1.2 %collective-permute-done.8.w = bf16[2,64,1024]{2,1,0:T(8,128)(2,1)S(1)} collective-permute-done((bf16[2,64,1024]{2,1,0:T(8,128)(2,1)S(1)}, bf16[2,64,1024]{2,1,0:T(8,128)(2,1)S(1)}, u32[]{:S(2)}, u32[]{:S(2)}) %collective-permute-start.8) | collective-permute-done | bytes 262176 | tf_op jit(solution)/shard_map/ppermute | solution.py:39
  44.1 1.4 %collective-permute-start.12 = (bf16[2,64,1024]{2,1,0:T(8,128)(2,1)S(1)}, bf16[2,64,1024]{2,1,0:T(8,128)(2,1)S(1)}, u32[]{:S(2)}, u32[]{:S(2)}) collective-permute-start(bf16[2,64,1024]{2,1,0:T(8,128)(2,1)S(1)} %get-tuple-element.64.turn), channel_id=1, source_target_pairs={{0,8},{8,16},{16,24},{24,0},{1,9},{9,17},{17,25},{25,1},{2,10},{10... | collective-permute-start | bytes 786440 | tf_op jit(solution)/shard_map/ppermute | solution.py:39
  46.4 1.8 %collective-permute-done.15.n = bf16[2,64,1024]{2,1,0:T(8,128)(2,1)S(1)} collective-permute-done((bf16[2,64,1024]{2,1,0:T(8,128)(2,1)S(1)}, bf16[2,64,1024]{2,1,0:T(8,128)(2,1)S(1)}, u32[]{:S(2)}, u32[]{:S(2)}) %collective-permute-start.15) | collective-permute-done | bytes 262176 | tf_op jit(solution)/shard_map/ppermute | solution.py:39
  49.8 1.3 %collective-permute-start.18 = (bf16[2,64,1024]{2,1,0:T(8,128)(2,1)S(1)}, bf16[2,64,1024]{2,1,0:T(8,128)(2,1)S(1)}, u32[]{:S(2)}, u32[]{:S(2)}) collective-permute-start(bf16[2,64,1024]{2,1,0:T(8,128)(2,1)S(1)} %get-tuple-element.67.turn), channel_id=1, source_target_pairs={{0,8},{8,16},{16,24},{24,0},{1,9},{9,17},{17,25},{25,1},{2,10},{10... | collective-permute-start | bytes 786440 | tf_op jit(solution)/shard_map/ppermute | solution.py:39
  51.8 2.1 %collective-permute-done.13.n = bf16[2,64,1024]{2,1,0:T(8,128)(2,1)S(1)} collective-permute-done((bf16[2,64,1024]{2,1,0:T(8,128)(2,1)S(1)}, bf16[2,64,1024]{2,1,0:T(8,128)(2,1)S(1)}, u32[]{:S(2)}, u32[]{:S(2)}) %collective-permute-start.13) | collective-permute-done | bytes 262176 | tf_op jit(solution)/shard_map/ppermute | solution.py:39
  55.4 1.4 %collective-permute-start.16 = (bf16[2,64,1024]{2,1,0:T(8,128)(2,1)S(1)}, bf16[2,64,1024]{2,1,0:T(8,128)(2,1)S(1)}, u32[]{:S(2)}, u32[]{:S(2)}) collective-permute-start(bf16[2,64,1024]{2,1,0:T(8,128)(2,1)S(1)} %get-tuple-element.68.turn), channel_id=1, source_target_pairs={{0,8},{8,16},{16,24},{24,0},{1,9},{9,17},{17,25},{25,1},{2,10},{10... | collective-permute-start | bytes 786440 | tf_op jit(solution)/shard_map/ppermute | solution.py:39
  57.6 1.8 %collective-permute-done.19.n = bf16[2,64,1024]{2,1,0:T(8,128)(2,1)S(1)} collective-permute-done((bf16[2,64,1024]{2,1,0:T(8,128)(2,1)S(1)}, bf16[2,64,1024]{2,1,0:T(8,128)(2,1)S(1)}, u32[]{:S(2)}, u32[]{:S(2)}) %collective-permute-start.19) | collective-permute-done | bytes 262176 | tf_op jit(solution)/shard_map/ppermute | solution.py:39
  61.0 1.3 %collective-permute-start.20 = (bf16[2,64,1024]{2,1,0:T(8,128)(2,1)S(1)}, bf16[2,64,1024]{2,1,0:T(8,128)(2,1)S(1)}, u32[]{:S(2)}, u32[]{:S(2)}) collective-permute-start(bf16[2,64,1024]{2,1,0:T(8,128)(2,1)S(1)} %get-tuple-element.71.first), channel_id=1, source_target_pairs={{0,8},{24,16},{8,24},{16,0},{1,9},{25,17},{9,25},{17,1},{2,10},{26... | collective-permute-start | bytes 786440 | tf_op jit(solution)/shard_map/ppermute | solution.py:406
  63.0 2.2 %collective-permute-done.17.n = bf16[2,64,1024]{2,1,0:T(8,128)(2,1)S(1)} collective-permute-done((bf16[2,64,1024]{2,1,0:T(8,128)(2,1)S(1)}, bf16[2,64,1024]{2,1,0:T(8,128)(2,1)S(1)}, u32[]{:S(2)}, u32[]{:S(2)}) %collective-permute-start.17) | collective-permute-done | bytes 262176 | tf_op jit(solution)/shard_map/ppermute | solution.py:39
  66.7 1.2 %collective-permute-start.21 = (bf16[2,64,1024]{2,1,0:T(8,128)(2,1)S(1)}, bf16[2,64,1024]{2,1,0:T(8,128)(2,1)S(1)}, u32[]{:S(2)}, u32[]{:S(2)}) collective-permute-start(bf16[2,64,1024]{2,1,0:T(8,128)(2,1)S(1)} %get-tuple-element.74), channel_id=1, source_target_pairs={{0,8},{24,16},{8,24},{16,0},{1,9},{25,17},{9,25},{17,1},{2,10},{26... | collective-permute-start | bytes 786440 | tf_op jit(solution)/shard_map/ppermute | solution.py:406
  68.7 2.5 %collective-permute-start.24 = (bf16[2,128,2176]{2,1,0:T(8,128)(2,1)S(1)}, bf16[2,128,2176]{2,1,0:T(8,128)(2,1)S(1)}, u32[]{:S(2)}, u32[]{:S(2)}) collective-permute-start(bf16[2,128,2176]{2,1,0:T(8,128)(2,1)S(1)} %last_south.1.turn), channel_id=1, source_target_pairs={{0,1},{1,2},{2,3},{3,4},{4,5},{5,6},{6,7},{8,9},{9,10},{10,11},{11... | collective-permute-start | bytes 3342344 | tf_op jit(solution)/shard_map/ppermute | solution.py:44
  71.4 1.3 %collective-permute-start.26 = (bf16[2,64,1024]{2,1,0:T(8,128)(2,1)S(1)}, bf16[2,64,1024]{2,1,0:T(8,128)(2,1)S(1)}, u32[]{:S(2)}, u32[]{:S(2)}) collective-permute-start(bf16[2,64,1024]{2,1,0:T(8,128)(2,1)S(1)} %get-tuple-element.76.turn), channel_id=1, source_target_pairs={{0,8},{8,0},{16,24},{24,16},{1,9},{9,1},{17,25},{25,17},{2,10},{10... | collective-permute-start | bytes 786440 | tf_op jit(solution)/shard_map/ppermute | solution.py:422
  72.6 1.3 %collective-permute-start.25 = (bf16[2,128,1024]{2,1,0:T(8,128)(2,1)S(1)}, bf16[2,128,1024]{2,1,0:T(8,128)(2,1)S(1)}, u32[]{:S(2)}, u32[]{:S(2)}) collective-permute-start(bf16[2,128,1024]{2,1,0:T(8,128)(2,1)S(1)} %get-tuple-element.78.q), channel_id=1, source_target_pairs={{1,0},{2,1},{3,2},{4,3},{5,4},{6,5},{7,6},{9,8},{10,9},{11,10},{12... | collective-permute-start | bytes 1572872 | tf_op jit(solution)/shard_map/ppermute | solution.py:44
  73.9 1.8 %collective-permute-done.21.first1 = bf16[2,64,1024]{2,1,0:T(8,128)(2,1)S(1)} collective-permute-done((bf16[2,64,1024]{2,1,0:T(8,128)(2,1)S(1)}, bf16[2,64,1024]{2,1,0:T(8,128)(2,1)S(1)}, u32[]{:S(2)}, u32[]{:S(2)}) %collective-permute-start.21) | collective-permute-done | bytes 262176 | tf_op jit(solution)/shard_map/ppermute | solution.py:406
  76.8 1.2 %collective-permute-start.27 = (bf16[2,64,1024]{2,1,0:T(8,128)(2,1)S(1)}, bf16[2,64,1024]{2,1,0:T(8,128)(2,1)S(1)}, u32[]{:S(2)}, u32[]{:S(2)}) collective-permute-start(bf16[2,64,1024]{2,1,0:T(8,128)(2,1)S(1)} %get-tuple-element.79.turn), channel_id=1, source_target_pairs={{0,8},{8,0},{16,24},{24,16},{1,9},{9,1},{17,25},{25,17},{2,10},{10... | collective-permute-start | bytes 786440 | tf_op jit(solution)/shard_map/ppermute | solution.py:432
  78.0 4.9 %collective-permute-done.26.side = bf16[2,64,1024]{2,1,0:T(8,128)(2,1)S(1)} collective-permute-done((bf16[2,64,1024]{2,1,0:T(8,128)(2,1)S(1)}, bf16[2,64,1024]{2,1,0:T(8,128)(2,1)S(1)}, u32[]{:S(2)}, u32[]{:S(2)}) %collective-permute-start.26) | collective-permute-done | bytes 262176 | tf_op jit(solution)/shard_map/ppermute | solution.py:422
  84.3 2.9 %collective-permute-done.27.side = bf16[2,64,1024]{2,1,0:T(8,128)(2,1)S(1)} collective-permute-done((bf16[2,64,1024]{2,1,0:T(8,128)(2,1)S(1)}, bf16[2,64,1024]{2,1,0:T(8,128)(2,1)S(1)}, u32[]{:S(2)}, u32[]{:S(2)}) %collective-permute-start.27) | collective-permute-done | bytes 262176 | tf_op jit(solution)/shard_map/ppermute | solution.py:432
  (57 shorter events, 24.1 us)
Async XLA Ops:
  0.6 6.0 %copy-start = (bf16[1,1,2,1024,1024]{4,3,2,1,0:T(8,128)(2,1)S(1)}, bf16[1,1,2,1024,1024]{4,3,2,1,0:T(8,128)(2,1)}, u32[]{:S(2)}) copy-start(bf16[1,1,2,1024,1024]{4,3,2,1,0:T(8,128)(2,1)} %param.17) | copy-start | bytes 12582916
  3.6 11.9 %collective-permute-start.2 = (bf16[2,64,1024]{2,1,0:T(8,128)(2,1)S(1)}, bf16[2,64,1024]{2,1,0:T(8,128)(2,1)S(1)}, u32[]{:S(2)}, u32[]{:S(2)}) collective-permute-start(bf16[2,64,1024]{2,1,0:T(8,128)(2,1)S(1)} %get-tuple-element.48.turn), channel_id=1, source_target_pairs={{0,8},{8,16},{16,24},{24,0},{1,9},{9,17},{17,25},{25,1},{2,10},{10... | collective-permute-start | bytes 786440 | tf_op jit(solution)/shard_map/ppermute | solution.py:39
  7.9 7.6 %collective-permute-start.3 = (bf16[2,64,1024]{2,1,0:T(8,128)(2,1)S(1)}, bf16[2,64,1024]{2,1,0:T(8,128)(2,1)S(1)}, u32[]{:S(2)}, u32[]{:S(2)}) collective-permute-start(bf16[2,64,1024]{2,1,0:T(8,128)(2,1)S(1)} %get-tuple-element.51.turn), channel_id=1, source_target_pairs={{0,1},{1,2},{2,3},{3,4},{4,5},{5,6},{6,7},{7,0},{8,9},{9,10},{10,1... | collective-permute-start | bytes 786440 | tf_op jit(solution)/shard_map/ppermute | solution.py:39
  7.9 7.6 %copy-start.1 = (bf16[1,1,2,128,128]{4,3,2,1,0:T(8,128)(2,1)S(1)}, bf16[1,1,2,128,128]{4,3,2,1,0:T(8,128)(2,1)}, u32[]{:S(2)}) copy-start(bf16[1,1,2,128,128]{4,3,2,1,0:T(8,128)(2,1)} %corner.7) | copy-start | bytes 196612
  9.2 9.7 %collective-permute-start = (bf16[2,64,1024]{2,1,0:T(8,128)(2,1)S(1)}, bf16[2,64,1024]{2,1,0:T(8,128)(2,1)S(1)}, u32[]{:S(2)}, u32[]{:S(2)}) collective-permute-start(bf16[2,64,1024]{2,1,0:T(8,128)(2,1)S(1)} %get-tuple-element.52), channel_id=1, source_target_pairs={{0,8},{8,16},{16,24},{24,0},{1,9},{9,17},{17,25},{25,1},{2,10},{10... | collective-permute-start | bytes 786440 | tf_op jit(solution)/shard_map/ppermute | solution.py:39
  10.8 8.1 %collective-permute-start.1 = (bf16[2,64,1024]{2,1,0:T(8,128)(2,1)S(1)}, bf16[2,64,1024]{2,1,0:T(8,128)(2,1)S(1)}, u32[]{:S(2)}, u32[]{:S(2)}) collective-permute-start(bf16[2,64,1024]{2,1,0:T(8,128)(2,1)S(1)} %get-tuple-element.53.turn), channel_id=1, source_target_pairs={{0,1},{1,2},{2,3},{3,4},{4,5},{5,6},{6,7},{7,0},{8,9},{9,10},{10,1... | collective-permute-start | bytes 786440 | tf_op jit(solution)/shard_map/ppermute | solution.py:39
  16.4 10.0 %collective-permute-start.6 = (bf16[2,64,1024]{2,1,0:T(8,128)(2,1)S(1)}, bf16[2,64,1024]{2,1,0:T(8,128)(2,1)S(1)}, u32[]{:S(2)}, u32[]{:S(2)}) collective-permute-start(bf16[2,64,1024]{2,1,0:T(8,128)(2,1)S(1)} %get-tuple-element.55.turn), channel_id=1, source_target_pairs={{0,8},{8,16},{16,24},{24,0},{1,9},{9,17},{17,25},{25,1},{2,10},{10... | collective-permute-start | bytes 786440 | tf_op jit(solution)/shard_map/ppermute | solution.py:39
  18.7 7.6 %collective-permute-start.7 = (bf16[2,64,1024]{2,1,0:T(8,128)(2,1)S(1)}, bf16[2,64,1024]{2,1,0:T(8,128)(2,1)S(1)}, u32[]{:S(2)}, u32[]{:S(2)}) collective-permute-start(bf16[2,64,1024]{2,1,0:T(8,128)(2,1)S(1)} %south.8.turn), channel_id=1, source_target_pairs={{0,1},{1,2},{2,3},{3,4},{4,5},{5,6},{6,7},{7,0},{8,9},{9,10},{10,1... | collective-permute-start | bytes 786440 | tf_op jit(solution)/shard_map/ppermute | solution.py:39
  19.8 12.3 %collective-permute-start.4 = (bf16[2,64,1024]{2,1,0:T(8,128)(2,1)S(1)}, bf16[2,64,1024]{2,1,0:T(8,128)(2,1)S(1)}, u32[]{:S(2)}, u32[]{:S(2)}) collective-permute-start(bf16[2,64,1024]{2,1,0:T(8,128)(2,1)S(1)} %get-tuple-element.56.turn), channel_id=1, source_target_pairs={{0,8},{8,16},{16,24},{24,0},{1,9},{9,17},{17,25},{25,1},{2,10},{10... | collective-permute-start | bytes 786440 | tf_op jit(solution)/shard_map/ppermute | solution.py:39
  21.9 7.6 %collective-permute-start.5 = (bf16[2,64,1024]{2,1,0:T(8,128)(2,1)S(1)}, bf16[2,64,1024]{2,1,0:T(8,128)(2,1)S(1)}, u32[]{:S(2)}, u32[]{:S(2)}) collective-permute-start(bf16[2,64,1024]{2,1,0:T(8,128)(2,1)S(1)} %south.9.turn), channel_id=1, source_target_pairs={{0,1},{1,2},{2,3},{3,4},{4,5},{5,6},{6,7},{7,0},{8,9},{9,10},{10,1... | collective-permute-start | bytes 786440 | tf_op jit(solution)/shard_map/ppermute | solution.py:39
  27.3 10.4 %collective-permute-start.10 = (bf16[2,64,1024]{2,1,0:T(8,128)(2,1)S(1)}, bf16[2,64,1024]{2,1,0:T(8,128)(2,1)S(1)}, u32[]{:S(2)}, u32[]{:S(2)}) collective-permute-start(bf16[2,64,1024]{2,1,0:T(8,128)(2,1)S(1)} %get-tuple-element.59.turn), channel_id=1, source_target_pairs={{0,8},{8,16},{16,24},{24,0},{1,9},{9,17},{17,25},{25,1},{2,10},{10... | collective-permute-start | bytes 786440 | tf_op jit(solution)/shard_map/ppermute | solution.py:39
  29.5 7.6 %collective-permute-start.11 = (bf16[2,64,1024]{2,1,0:T(8,128)(2,1)S(1)}, bf16[2,64,1024]{2,1,0:T(8,128)(2,1)S(1)}, u32[]{:S(2)}, u32[]{:S(2)}) collective-permute-start(bf16[2,64,1024]{2,1,0:T(8,128)(2,1)S(1)} %south.10.turn), channel_id=1, source_target_pairs={{0,1},{1,2},{2,3},{3,4},{4,5},{5,6},{6,7},{7,0},{8,9},{9,10},{10,1... | collective-permute-start | bytes 786440 | tf_op jit(solution)/shard_map/ppermute | solution.py:39
  32.9 10.4 %collective-permute-start.8 = (bf16[2,64,1024]{2,1,0:T(8,128)(2,1)S(1)}, bf16[2,64,1024]{2,1,0:T(8,128)(2,1)S(1)}, u32[]{:S(2)}, u32[]{:S(2)}) collective-permute-start(bf16[2,64,1024]{2,1,0:T(8,128)(2,1)S(1)} %get-tuple-element.60.turn), channel_id=1, source_target_pairs={{0,8},{8,16},{16,24},{24,0},{1,9},{9,17},{17,25},{25,1},{2,10},{10... | collective-permute-start | bytes 786440 | tf_op jit(solution)/shard_map/ppermute | solution.py:39
  34.5 7.6 %collective-permute-start.9 = (bf16[2,64,1024]{2,1,0:T(8,128)(2,1)S(1)}, bf16[2,64,1024]{2,1,0:T(8,128)(2,1)S(1)}, u32[]{:S(2)}, u32[]{:S(2)}) collective-permute-start(bf16[2,64,1024]{2,1,0:T(8,128)(2,1)S(1)} %south.11.turn), channel_id=1, source_target_pairs={{0,1},{1,2},{2,3},{3,4},{4,5},{5,6},{6,7},{7,0},{8,9},{9,10},{10,1... | collective-permute-start | bytes 786440 | tf_op jit(solution)/shard_map/ppermute | solution.py:39
  38.5 10.4 %collective-permute-start.14 = (bf16[2,64,1024]{2,1,0:T(8,128)(2,1)S(1)}, bf16[2,64,1024]{2,1,0:T(8,128)(2,1)S(1)}, u32[]{:S(2)}, u32[]{:S(2)}) collective-permute-start(bf16[2,64,1024]{2,1,0:T(8,128)(2,1)S(1)} %get-tuple-element.63.turn), channel_id=1, source_target_pairs={{0,8},{8,16},{16,24},{24,0},{1,9},{9,17},{17,25},{25,1},{2,10},{10... | collective-permute-start | bytes 786440 | tf_op jit(solution)/shard_map/ppermute | solution.py:39
  40.5 7.6 %collective-permute-start.15 = (bf16[2,64,1024]{2,1,0:T(8,128)(2,1)S(1)}, bf16[2,64,1024]{2,1,0:T(8,128)(2,1)S(1)}, u32[]{:S(2)}, u32[]{:S(2)}) collective-permute-start(bf16[2,64,1024]{2,1,0:T(8,128)(2,1)S(1)} %south.12.turn), channel_id=1, source_target_pairs={{0,1},{1,2},{2,3},{3,4},{4,5},{5,6},{6,7},{7,0},{8,9},{9,10},{10,1... | collective-permute-start | bytes 786440 | tf_op jit(solution)/shard_map/ppermute | solution.py:39
  44.1 10.4 %collective-permute-start.12 = (bf16[2,64,1024]{2,1,0:T(8,128)(2,1)S(1)}, bf16[2,64,1024]{2,1,0:T(8,128)(2,1)S(1)}, u32[]{:S(2)}, u32[]{:S(2)}) collective-permute-start(bf16[2,64,1024]{2,1,0:T(8,128)(2,1)S(1)} %get-tuple-element.64.turn), channel_id=1, source_target_pairs={{0,8},{8,16},{16,24},{24,0},{1,9},{9,17},{17,25},{25,1},{2,10},{10... | collective-permute-start | bytes 786440 | tf_op jit(solution)/shard_map/ppermute | solution.py:39
  46.3 7.6 %collective-permute-start.13 = (bf16[2,64,1024]{2,1,0:T(8,128)(2,1)S(1)}, bf16[2,64,1024]{2,1,0:T(8,128)(2,1)S(1)}, u32[]{:S(2)}, u32[]{:S(2)}) collective-permute-start(bf16[2,64,1024]{2,1,0:T(8,128)(2,1)S(1)} %south.13.turn), channel_id=1, source_target_pairs={{0,1},{1,2},{2,3},{3,4},{4,5},{5,6},{6,7},{7,0},{8,9},{9,10},{10,1... | collective-permute-start | bytes 786440 | tf_op jit(solution)/shard_map/ppermute | solution.py:39
  49.8 10.4 %collective-permute-start.18 = (bf16[2,64,1024]{2,1,0:T(8,128)(2,1)S(1)}, bf16[2,64,1024]{2,1,0:T(8,128)(2,1)S(1)}, u32[]{:S(2)}, u32[]{:S(2)}) collective-permute-start(bf16[2,64,1024]{2,1,0:T(8,128)(2,1)S(1)} %get-tuple-element.67.turn), channel_id=1, source_target_pairs={{0,8},{8,16},{16,24},{24,0},{1,9},{9,17},{17,25},{25,1},{2,10},{10... | collective-permute-start | bytes 786440 | tf_op jit(solution)/shard_map/ppermute | solution.py:39
  51.8 7.6 %collective-permute-start.19 = (bf16[2,64,1024]{2,1,0:T(8,128)(2,1)S(1)}, bf16[2,64,1024]{2,1,0:T(8,128)(2,1)S(1)}, u32[]{:S(2)}, u32[]{:S(2)}) collective-permute-start(bf16[2,64,1024]{2,1,0:T(8,128)(2,1)S(1)} %south.14.turn), channel_id=1, source_target_pairs={{0,1},{1,2},{2,3},{3,4},{4,5},{5,6},{6,7},{7,0},{8,9},{9,10},{10,1... | collective-permute-start | bytes 786440 | tf_op jit(solution)/shard_map/ppermute | solution.py:39
  55.4 10.4 %collective-permute-start.16 = (bf16[2,64,1024]{2,1,0:T(8,128)(2,1)S(1)}, bf16[2,64,1024]{2,1,0:T(8,128)(2,1)S(1)}, u32[]{:S(2)}, u32[]{:S(2)}) collective-permute-start(bf16[2,64,1024]{2,1,0:T(8,128)(2,1)S(1)} %get-tuple-element.68.turn), channel_id=1, source_target_pairs={{0,8},{8,16},{16,24},{24,0},{1,9},{9,17},{17,25},{25,1},{2,10},{10... | collective-permute-start | bytes 786440 | tf_op jit(solution)/shard_map/ppermute | solution.py:39
  57.6 7.6 %collective-permute-start.17 = (bf16[2,64,1024]{2,1,0:T(8,128)(2,1)S(1)}, bf16[2,64,1024]{2,1,0:T(8,128)(2,1)S(1)}, u32[]{:S(2)}, u32[]{:S(2)}) collective-permute-start(bf16[2,64,1024]{2,1,0:T(8,128)(2,1)S(1)} %south.15.turn), channel_id=1, source_target_pairs={{0,1},{1,2},{2,3},{3,4},{4,5},{5,6},{6,7},{7,0},{8,9},{9,10},{10,1... | collective-permute-start | bytes 786440 | tf_op jit(solution)/shard_map/ppermute | solution.py:39
  61.0 10.2 %collective-permute-start.20 = (bf16[2,64,1024]{2,1,0:T(8,128)(2,1)S(1)}, bf16[2,64,1024]{2,1,0:T(8,128)(2,1)S(1)}, u32[]{:S(2)}, u32[]{:S(2)}) collective-permute-start(bf16[2,64,1024]{2,1,0:T(8,128)(2,1)S(1)} %get-tuple-element.71.first), channel_id=1, source_target_pairs={{0,8},{24,16},{8,24},{16,0},{1,9},{25,17},{9,25},{17,1},{2,10},{26... | collective-permute-start | bytes 786440 | tf_op jit(solution)/shard_map/ppermute | solution.py:406
  62.3 9.0 %collective-permute-start.22 = (bf16[2,64,1024]{2,1,0:T(8,128)(2,1)S(1)}, bf16[2,64,1024]{2,1,0:T(8,128)(2,1)S(1)}, u32[]{:S(2)}, u32[]{:S(2)}) collective-permute-start(bf16[2,64,1024]{2,1,0:T(8,128)(2,1)S(1)} %get-tuple-element.72.turn), channel_id=1, source_target_pairs={{0,1},{1,0},{2,3},{3,2},{4,5},{5,4},{6,7},{7,6},{24,8},{25,9},{26,... | collective-permute-start | bytes 786440 | tf_op jit(solution)/shard_map/ppermute | solution.py:407
  66.7 9.0 %collective-permute-start.21 = (bf16[2,64,1024]{2,1,0:T(8,128)(2,1)S(1)}, bf16[2,64,1024]{2,1,0:T(8,128)(2,1)S(1)}, u32[]{:S(2)}, u32[]{:S(2)}) collective-permute-start(bf16[2,64,1024]{2,1,0:T(8,128)(2,1)S(1)} %get-tuple-element.74), channel_id=1, source_target_pairs={{0,8},{24,16},{8,24},{16,0},{1,9},{25,17},{9,25},{17,1},{2,10},{26... | collective-permute-start | bytes 786440 | tf_op jit(solution)/shard_map/ppermute | solution.py:406
  67.9 7.8 %collective-permute-start.23 = (bf16[2,64,1024]{2,1,0:T(8,128)(2,1)S(1)}, bf16[2,64,1024]{2,1,0:T(8,128)(2,1)S(1)}, u32[]{:S(2)}, u32[]{:S(2)}) collective-permute-start(bf16[2,64,1024]{2,1,0:T(8,128)(2,1)S(1)} %get-tuple-element.75.turn), channel_id=1, source_target_pairs={{0,1},{1,0},{2,3},{3,2},{4,5},{5,4},{6,7},{7,6},{24,8},{25,9},{26,... | collective-permute-start | bytes 786440 | tf_op jit(solution)/shard_map/ppermute | solution.py:407
  68.7 14.2 %collective-permute-start.24 = (bf16[2,128,2176]{2,1,0:T(8,128)(2,1)S(1)}, bf16[2,128,2176]{2,1,0:T(8,128)(2,1)S(1)}, u32[]{:S(2)}, u32[]{:S(2)}) collective-permute-start(bf16[2,128,2176]{2,1,0:T(8,128)(2,1)S(1)} %last_south.1.turn), channel_id=1, source_target_pairs={{0,1},{1,2},{2,3},{3,4},{4,5},{5,6},{6,7},{8,9},{9,10},{10,11},{11... | collective-permute-start | bytes 3342344 | tf_op jit(solution)/shard_map/ppermute | solution.py:44
  71.4 11.6 %collective-permute-start.26 = (bf16[2,64,1024]{2,1,0:T(8,128)(2,1)S(1)}, bf16[2,64,1024]{2,1,0:T(8,128)(2,1)S(1)}, u32[]{:S(2)}, u32[]{:S(2)}) collective-permute-start(bf16[2,64,1024]{2,1,0:T(8,128)(2,1)S(1)} %get-tuple-element.76.turn), channel_id=1, source_target_pairs={{0,8},{8,0},{16,24},{24,16},{1,9},{9,1},{17,25},{25,17},{2,10},{10... | collective-permute-start | bytes 786440 | tf_op jit(solution)/shard_map/ppermute | solution.py:422
  72.6 10.3 %collective-permute-start.25 = (bf16[2,128,1024]{2,1,0:T(8,128)(2,1)S(1)}, bf16[2,128,1024]{2,1,0:T(8,128)(2,1)S(1)}, u32[]{:S(2)}, u32[]{:S(2)}) collective-permute-start(bf16[2,128,1024]{2,1,0:T(8,128)(2,1)S(1)} %get-tuple-element.78.q), channel_id=1, source_target_pairs={{1,0},{2,1},{3,2},{4,3},{5,4},{6,5},{7,6},{9,8},{10,9},{11,10},{12... | collective-permute-start | bytes 1572872 | tf_op jit(solution)/shard_map/ppermute | solution.py:44
  76.8 10.4 %collective-permute-start.27 = (bf16[2,64,1024]{2,1,0:T(8,128)(2,1)S(1)}, bf16[2,64,1024]{2,1,0:T(8,128)(2,1)S(1)}, u32[]{:S(2)}, u32[]{:S(2)}) collective-permute-start(bf16[2,64,1024]{2,1,0:T(8,128)(2,1)S(1)} %get-tuple-element.79.turn), channel_id=1, source_target_pairs={{0,8},{8,0},{16,24},{24,16},{1,9},{9,1},{17,25},{25,17},{2,10},{10... | collective-permute-start | bytes 786440 | tf_op jit(solution)/shard_map/ppermute | solution.py:432
  78.0 6.2 %collective-permute-start.28 = (bf16[2,128,128]{2,1,0:T(8,128)(2,1)S(1)}, bf16[2,128,128]{2,1,0:T(8,128)(2,1)S(1)}, u32[]{:S(2)}, u32[]{:S(2)}) collective-permute-start(bf16[2,128,128]{2,1,0:T(8,128)(2,1)S(1)} %get-tuple-element.83), channel_id=1, source_target_pairs={{0,1},{1,2},{2,3},{3,4},{4,5},{5,6},{6,7},{7,0},{8,9},{9,10},{10,1... | collective-permute-start | bytes 196616 | tf_op jit(solution)/shard_map/ppermute | solution.py:39
